TPU v7x, 32 devices: a whole 2x2x4 slice. The times are simulated.
32 devices in a mesh: dp: 8 (over y, x, core), fsdp: 4 (over z).
Axes of the slice: x: 2, y: 2, z: 4, core: 2. Of those that a mesh axis runs over, the one named last changes fastest.
Arguments:
- tokens: bfloat16 [8192, 2048], P(('dp', 'fsdp')), may hold values from -6 to 6
- cotangent: bfloat16 [8192, 2048], P(('dp', 'fsdp')), may hold values from -6 to 6
- group_ids: int32 [32], P(('dp', 'fsdp')), may hold values from 0 to 7
- norm_first: bfloat16 [2048], P(('dp', 'fsdp')), may hold values from 0.5 to 1.5
- input_weight: bfloat16 [2048, 12288], P(('dp', 'fsdp')), may hold values from -0.125 to 0.125
- decay_weight: bfloat16 [2048, 32], P(('dp', 'fsdp')), may hold values from -0.125 to 0.125
- conv_weight: bfloat16 [4, 8192], P(None, ('dp', 'fsdp')), may hold values from -2.5 to 2.5
- decay_scale: float32 [16], replicated, may hold values from -5 to -1
- decay_bias: float32 [16], replicated, may hold values from -1 to 1
- output_gain: float32 [256], replicated, may hold values from 0.5 to 1.5
- output_weight: bfloat16 [4096, 2048], P(('dp', 'fsdp')), may hold values from -0.09375 to 0.09375
- norm_second: bfloat16 [2048], P(('dp', 'fsdp')), may hold values from 0.5 to 1.5
- upgate_weight: bfloat16 [2048, 11264], P(('dp', 'fsdp')), may hold values from -0.125 to 0.125
- down_weight: bfloat16 [5632, 2048], P(('dp', 'fsdp')), may hold values from -0.078125 to 0.078125
Outputs:
- block_out: float32 [8192, 2048], P(('dp', 'fsdp'))
- tokens_grad: float32 [8192, 2048], P(('dp', 'fsdp'))
- norm_first_grad: float32 [2048], P(('dp', 'fsdp'))
- input_weight_grad: float32 [2048, 12288], P(('dp', 'fsdp'))
- decay_weight_grad: float32 [2048, 32], P(('dp', 'fsdp'))
- conv_weight_grad: float32 [4, 8192], P(None, ('dp', 'fsdp'))
- decay_scale_grad: float32 [16], replicated
- decay_bias_grad: float32 [16], replicated
- output_gain_grad: float32 [256], replicated
- output_weight_grad: float32 [4096, 2048], P(('dp', 'fsdp'))
- norm_second_grad: float32 [2048], P(('dp', 'fsdp'))
- upgate_weight_grad: float32 [2048, 11264], P(('dp', 'fsdp'))
- down_weight_grad: float32 [5632, 2048], P(('dp', 'fsdp'))
All inputs are finite; a program needn't handle non-finite values.
Results may differ from a plain program's by a relative error of at most 0.015.
Values may be sent and summed in bfloat16 or wider, within the bound.
A program may use at most 576 MiB of HBM per device.

v0:
```python
import jax
import jax.numpy as jnp
from jax import lax
from jax.sharding import PartitionSpec as P

H = 16
DK = 128
DV = 256
FF = 5632
SPAN = 64
GROUPS = 8


EPSILON = 1e-06
EXACT_MATMUL = lax.Precision.HIGHEST


def rms_norm(values_in, gain):
    return (
        values_in
        * lax.rsqrt(jnp.mean(values_in * values_in, axis=-1, keepdims=True) + EPSILON)
        * gain
    )


def prepare(projected, decay_raw, conv_taps, decay_scale, decay_bias):
    length = projected.shape[0]
    tap_count = conv_taps.shape[0]
    mix_width = conv_taps.shape[1]
    conv_input = projected[:, :mix_width]
    padded = jnp.pad(conv_input, ((tap_count - 1, 0), (0, 0)))
    convolved = padded[0:length] * conv_taps[0]
    for offset in range(1, tap_count):
        convolved = convolved + padded[offset : offset + length] * conv_taps[offset]
    active = jax.nn.silu(convolved)
    key_width = H * DK
    queries = active[:, :key_width].reshape(length, H, DK)
    keys_all = active[:, key_width : 2 * key_width].reshape(length, H, DK)
    values_all = active[:, 2 * key_width :].reshape(length, H, DV)
    queries = (
        queries
        * lax.rsqrt(jnp.sum(queries * queries, axis=-1, keepdims=True) + EPSILON)
        * DK ** (-0.5)
    )
    keys_all = keys_all * lax.rsqrt(jnp.sum(keys_all * keys_all, axis=-1, keepdims=True) + EPSILON)
    decay_rate = -jnp.exp(decay_scale) * jax.nn.softplus(decay_raw[:, :H] + decay_bias)
    strength = jax.nn.sigmoid(decay_raw[:, H:])
    gate_values = projected[:, mix_width:].reshape(length, H, DV)
    return (
        jnp.transpose(queries, (1, 0, 2)),
        jnp.transpose(keys_all, (1, 0, 2)),
        jnp.transpose(values_all, (1, 0, 2)),
        decay_rate.T,
        strength.T,
        gate_values,
    )


def delta_rule(queries, keys_all, values_all, decay_rate, strength):
    head_count, length, key_dim = queries.shape
    value_dim = values_all.shape[2]
    block_count = length // SPAN

    def to_blocks(tensor):
        return jnp.moveaxis(
            tensor.reshape((head_count, block_count, SPAN) + tensor.shape[2:]), 1, 0
        )

    query_blocks = to_blocks(queries)
    key_blocks = to_blocks(keys_all)
    value_blocks = to_blocks(values_all)
    rate_blocks = to_blocks(decay_rate)
    beta_blocks = to_blocks(strength)
    cumulated = jnp.cumsum(rate_blocks, axis=-1)
    row_ids = jnp.arange(SPAN, dtype=jnp.int32)
    strict = row_ids[:, None] > row_ids[None, :]
    within = row_ids[:, None] >= row_ids[None, :]
    gaps_log = cumulated[..., :, None] - cumulated[..., None, :]
    key_gram = jnp.einsum("bhid,bhjd->bhij", key_blocks, key_blocks, precision=EXACT_MATMUL)
    lower_part = jnp.where(
        strict,
        jnp.exp(jnp.where(strict, gaps_log, 0.0)) * key_gram * beta_blocks[..., :, None],
        0.0,
    )
    growth = jnp.exp(cumulated)
    solved_values = jax.scipy.linalg.solve_triangular(
        lower_part, beta_blocks[..., None] * value_blocks, lower=True, unit_diagonal=True
    )
    solved_keys = jax.scipy.linalg.solve_triangular(
        lower_part, (beta_blocks * growth)[..., None] * key_blocks, lower=True, unit_diagonal=True
    )
    query_key = jnp.einsum("bhid,bhjd->bhij", query_blocks, key_blocks, precision=EXACT_MATMUL)
    weights_in = jnp.where(within, jnp.exp(jnp.where(within, gaps_log, 0.0)) * query_key, 0.0)
    query_grow = growth[..., None] * query_blocks
    key_tail = jnp.exp(cumulated[..., -1:] - cumulated)[..., None] * key_blocks
    final_decay = jnp.exp(cumulated[..., -1])[..., None, None]

    def advance(running_state, span_items):
        current_values, current_keys, weights_now, current_query, current_tail, current_decay = (
            span_items
        )
        written_state = current_values - jnp.einsum(
            "ynr,yrg->yng", current_keys, running_state, precision=EXACT_MATMUL
        )
        current_output = jnp.einsum(
            "ynr,yrg->yng", current_query, running_state, precision=EXACT_MATMUL
        )
        current_output = current_output + jnp.einsum(
            "hij,hjv->hiv", weights_now, written_state, precision=EXACT_MATMUL
        )
        running_state = current_decay * running_state + jnp.einsum(
            "izu,izx->iux", current_tail, written_state, precision=EXACT_MATMUL
        )
        return (running_state, current_output)

    initial = jnp.zeros((head_count, key_dim, value_dim), queries.dtype)
    _, outputs = lax.scan(
        jax.checkpoint(advance),
        initial,
        (solved_values, solved_keys, weights_in, query_grow, key_tail, final_decay),
    )
    return jnp.moveaxis(outputs, 0, 1).reshape(head_count, length, value_dim)


def finish(core_out, gate_values, output_gain):
    length = gate_values.shape[0]
    ordered = jnp.transpose(core_out, (1, 0, 2))
    normed = rms_norm(ordered, output_gain) * jax.nn.silu(gate_values)
    return normed.reshape(length, -1)


def local(
    tokens,
    cotangent,
    group_ids,
    norm_first,
    input_weight,
    decay_weight,
    conv_weight,
    decay_scale,
    decay_bias,
    output_gain,
    output_weight,
    norm_second,
    upgate_weight,
    down_weight,
):
    labels = jnp.arange(GROUPS, dtype=jnp.int32)
    onehot = (group_ids[:, None] == labels[None, :]).astype(jnp.float32)
    counts = lax.psum(jnp.sum(onehot, axis=0), ("dp", "fsdp"))
    scales = 1.0 / jnp.sum(onehot * counts[None, :], axis=1)
    input_full, decay_full, output_full, conv_full, first_full = (
        lax.all_gather(input_weight, ("dp", "fsdp"), axis=0, tiled=True),
        lax.all_gather(decay_weight, ("dp", "fsdp"), axis=0, tiled=True),
        lax.all_gather(output_weight, ("dp", "fsdp"), axis=0, tiled=True),
        lax.all_gather(conv_weight, ("dp", "fsdp"), axis=1, tiled=True),
        lax.all_gather(norm_first, ("dp", "fsdp"), axis=0, tiled=True),
    )
    inputs = tokens.astype(jnp.float32)
    normed_one, first_back = jax.vjp(rms_norm, inputs, first_full.astype(jnp.float32))
    normed_low = normed_one.astype(jnp.bfloat16)
    projected = jnp.dot(normed_low, input_full, preferred_element_type=jnp.float32)
    decay_raw = jnp.dot(normed_low, decay_full, preferred_element_type=jnp.float32)
    prepared, prepare_back = jax.vjp(
        prepare, projected, decay_raw, conv_full.astype(jnp.float32), decay_scale, decay_bias
    )
    queries, keys_all, values_all, decay_rate, strength, gate_values = prepared
    query_low = queries.astype(jnp.bfloat16)
    key_low = keys_all.astype(jnp.bfloat16)
    value_low = values_all.astype(jnp.bfloat16)
    core_out, core_back = jax.vjp(
        delta_rule,
        query_low.astype(jnp.float32),
        key_low.astype(jnp.float32),
        value_low.astype(jnp.float32),
        decay_rate,
        strength,
    )
    finished, finish_back = jax.vjp(finish, core_out, gate_values, output_gain)
    mixed_low = finished.astype(jnp.bfloat16)
    middle = inputs + jnp.dot(mixed_low, output_full, preferred_element_type=jnp.float32)
    upgate_full, down_full, second_full = (
        lax.all_gather(upgate_weight, ("dp", "fsdp"), axis=0, tiled=True),
        lax.all_gather(down_weight, ("dp", "fsdp"), axis=0, tiled=True),
        lax.all_gather(norm_second, ("dp", "fsdp"), axis=0, tiled=True),
    )
    normed_two, second_back = jax.vjp(rms_norm, middle, second_full.astype(jnp.float32))
    second_low = normed_two.astype(jnp.bfloat16)
    upgate = jnp.dot(second_low, upgate_full, preferred_element_type=jnp.float32)
    gate_part = upgate[:, :FF]
    up_part = upgate[:, FF:]
    sigmoid_gate = jax.nn.sigmoid(gate_part)
    hidden_low = (gate_part * sigmoid_gate * up_part).astype(jnp.bfloat16)
    result = middle + jnp.dot(hidden_low, down_full, preferred_element_type=jnp.float32)
    seed_grad = cotangent.astype(jnp.float32) * scales[:, None]
    seed_low = seed_grad.astype(jnp.bfloat16)
    down_grad = jnp.einsum("sf,sd->fd", hidden_low, seed_low, preferred_element_type=jnp.float32)
    down_total = lax.psum_scatter(down_grad, ("dp", "fsdp"), scatter_dimension=0, tiled=True)
    upgate_again, down_again = (
        lax.all_gather(upgate_weight, ("dp", "fsdp"), axis=0, tiled=True),
        lax.all_gather(down_weight, ("dp", "fsdp"), axis=0, tiled=True),
    )
    hidden_grad = jnp.einsum("sd,fd->sf", seed_low, down_again, preferred_element_type=jnp.float32)
    gate_grad = hidden_grad * up_part * sigmoid_gate * (1.0 + gate_part * (1.0 - sigmoid_gate))
    up_grad = hidden_grad * gate_part * sigmoid_gate
    upgate_low = jnp.concatenate([gate_grad, up_grad], axis=1).astype(jnp.bfloat16)
    upgate_grad = jnp.einsum(
        "sd,sf->df", second_low, upgate_low, preferred_element_type=jnp.float32
    )
    normed_two_grad = jnp.einsum(
        "sf,df->sd", upgate_low, upgate_again, preferred_element_type=jnp.float32
    )
    middle_part, second_grad = second_back(normed_two_grad)
    middle_grad = seed_grad + middle_part
    upgate_total, second_total = (
        lax.psum_scatter(upgate_grad, ("dp", "fsdp"), scatter_dimension=0, tiled=True),
        lax.psum_scatter(second_grad, ("dp", "fsdp"), scatter_dimension=0, tiled=True),
    )
    input_again, decay_again, output_again = (
        lax.all_gather(input_weight, ("dp", "fsdp"), axis=0, tiled=True),
        lax.all_gather(decay_weight, ("dp", "fsdp"), axis=0, tiled=True),
        lax.all_gather(output_weight, ("dp", "fsdp"), axis=0, tiled=True),
    )
    middle_low = middle_grad.astype(jnp.bfloat16)
    output_grad = jnp.einsum("sh,sd->hd", mixed_low, middle_low, preferred_element_type=jnp.float32)
    mixed_grad = jnp.einsum(
        "sd,hd->sh", middle_low, output_again, preferred_element_type=jnp.float32
    )
    core_grad, gate_values_grad, gain_grad = finish_back(mixed_grad)
    query_grad, key_grad, value_grad, rate_grad, strength_grad = core_back(core_grad)
    projected_grad, decay_raw_grad, conv_grad, scale_grad, bias_grad = prepare_back(
        (query_grad, key_grad, value_grad, rate_grad, strength_grad, gate_values_grad)
    )
    projected_low = projected_grad.astype(jnp.bfloat16)
    decay_low = decay_raw_grad.astype(jnp.bfloat16)
    input_grad = jnp.einsum(
        "sd,sn->dn", normed_low, projected_low, preferred_element_type=jnp.float32
    )
    decay_grad = jnp.einsum("sd,sn->dn", normed_low, decay_low, preferred_element_type=jnp.float32)
    normed_one_grad = jnp.einsum(
        "sn,dn->sd", projected_low, input_again, preferred_element_type=jnp.float32
    )
    normed_one_grad = normed_one_grad + jnp.einsum(
        "sn,dn->sd", decay_low, decay_again, preferred_element_type=jnp.float32
    )
    input_part, first_grad = first_back(normed_one_grad)
    tokens_grad = middle_grad + input_part
    input_total, decay_total, output_total, conv_total, first_total = (
        lax.psum_scatter(input_grad, ("dp", "fsdp"), scatter_dimension=0, tiled=True),
        lax.psum_scatter(decay_grad, ("dp", "fsdp"), scatter_dimension=0, tiled=True),
        lax.psum_scatter(output_grad, ("dp", "fsdp"), scatter_dimension=0, tiled=True),
        lax.psum_scatter(conv_grad, ("dp", "fsdp"), scatter_dimension=1, tiled=True),
        lax.psum_scatter(first_grad, ("dp", "fsdp"), scatter_dimension=0, tiled=True),
    )
    scale_total, bias_total, gain_total = lax.psum(
        (scale_grad, bias_grad, gain_grad), ("dp", "fsdp")
    )
    return (
        result,
        tokens_grad,
        first_total,
        input_total,
        decay_total,
        conv_total,
        scale_total,
        bias_total,
        gain_total,
        output_total,
        second_total,
        upgate_total,
        down_total,
    )


def solution(mesh):
    return jax.shard_map(
        local,
        mesh=mesh,
        in_specs=(
            P(("dp", "fsdp"), None),
            P(("dp", "fsdp"), None),
            P(("dp", "fsdp")),
            P(("dp", "fsdp")),
            P(("dp", "fsdp"), None),
            P(("dp", "fsdp"), None),
            P(None, ("dp", "fsdp")),
            P(),
            P(),
            P(),
            P(("dp", "fsdp"), None),
            P(("dp", "fsdp")),
            P(("dp", "fsdp"), None),
            P(("dp", "fsdp"), None),
        ),
        out_specs=(
            P(("dp", "fsdp"), None),
            P(("dp", "fsdp"), None),
            P(("dp", "fsdp")),
            P(("dp", "fsdp"), None),
            P(("dp", "fsdp"), None),
            P(None, ("dp", "fsdp")),
            P(),
            P(),
            P(),
            P(("dp", "fsdp"), None),
            P(("dp", "fsdp")),
            P(("dp", "fsdp"), None),
            P(("dp", "fsdp"), None),
        ),
        check_vma=False,
    )
```

profile of v0, /device:TPU:0, one launch (start us, length us, event | category | flops | bytes accessed | tf_op | source)
XLA Modules:
  0.0 5872.3 jit_solution(18307930020194539952)
XLA Ops:
  10.7 44.7 psum.28
  55.5 71.9 %all-gather = bf16[32,64,32]{1,2,0:T(8,128)(2,1)S(1)} all-gather(bf16[1,64,32]{1,2,0:T(8,128)(2,1)S(1)} %bitcast.488), channel_id=1, replica_groups=mesh['dp'=8,'fsdp'=4] {'dp','fsdp'}, dimensions={0}, use_global_device_ids=true | all-gather | bytes 135168 | tf_op jit(solution)/shard_map/all_gather | solution.py:154
  128.3 43.9 all-reduce.23
  177.1 72.3 %all_gather.32 = bf16[4,8192]{1,0:T(4,128)(2,1)S(1)} all-gather(bf16[4,256]{1,0:T(4,128)(2,1)S(1)} %copy-done.103), channel_id=1, replica_groups=mesh['dp'=8,'fsdp'=4] {'dp','fsdp'}, dimensions={1}, use_global_device_ids=true | all-gather | bytes 67584 | tf_op jit(solution)/shard_map/all_gather | solution.py:156
  251.7 42.3 all-gather.6.cloned.1.call-done
  294.0 25.6 fusion.189
  319.7 7.5 slice.100
  327.2 4.7 slice.109
  331.9 18.5 fusion.45
  350.4 5.2 slice_bitcast_fusion.1
  362.5 3.7 copy.394
  374.3 316.0 %custom-call.16 = f32[4,16,1,64,64]{3,4,2,1,0:T(8,128)} custom-call(f32[4,16,1,64,64]{4,3,2,1,0:T(8,128)} %get-tuple-element.760), custom_call_target="InvertDiagBlocksLowerTriangular" | custom-call | tf_op jit(solution)/shard_map/jvp(jit(_solve_triangular))/vmap(vmap())/triangular_solve | solution.py:86
  690.3 7.0 fusion.81
  701.7 7.4 fusion.54
  709.1 53.4 while.42
  715.6 3.4 fusion.296
  719.1 3.5 multiply_add_fusion.7
  728.9 3.5 fusion.296
  732.4 3.5 multiply_add_fusion.7
  742.2 3.4 fusion.296
  745.6 3.6 multiply_add_fusion.7
  755.6 3.5 fusion.296
  759.1 3.5 multiply_add_fusion.7
  766.0 4.1 multiply_convert_fusion.3
  773.1 10.7 multiply_reduce_fusion.9
  783.8 26.2 fusion.186
  810.0 4.5 all-gather.12.cloned.1.call-done
  814.5 25.7 multiply_convert_fusion.1
  840.2 22.1 multiply_reduce_fusion.6
  862.3 3.5 fusion.77
  865.9 12.9 fusion.151
  878.8 8.3 multiply_reduce_fusion.5
  899.4 137.6 %while.43 = (s32[]{:T(128)}, f32[16,128,256]{2,1,0:T(8,128)}, f32[4,16,64,256]{3,2,1,0:T(8,128)}, f32[4,16,64,128]{3,2,1,0:T(8,128)}, f32[4,16,64,64]{3,2,1,0:T(...) while((s32[]{:T(128)}, f32[16,128,256]{2,1,0:T(8,128)}, ...), condition=%wide.region_14.15_spmd.clone, body=%wide.region_12.14_spmd.clone.sunk | while | flops 3225419776 | bytes 66324052 | solution.py:117
  916.0 3.6 add_add_fusion.8
  919.6 3.1 fusion.318
  950.6 3.6 add_add_fusion.8
  963.8 3.1 fusion.321
  985.3 3.6 add_add_fusion.8
  988.9 3.2 fusion.318
  1019.9 3.6 add_add_fusion.8
  1037.0 7.8 fusion.203
  1044.9 3.9 bitcast_multiply_fusion.4
  1048.9 3.8 fusion.107
  1058.2 4.8 fusion.92
  1063.0 4.9 fusion.202
  1067.9 7.5 multiply_reduce_fusion.7
  1102.3 18.5 multiply_reduce_fusion.3
  1126.9 15.0 fusion.149
  1143.1 19.9 fusion.141
  1163.1 4.8 copy.389
  1167.9 11.5 broadcast_multiply_fusion
  1179.4 13.7 pad_add_fusion
  1193.1 37.5 fusion.145
  1232.2 35.0 fusion.58
  1267.9 24.7 fusion.146
  1292.6 3.7 fusion.63
  1296.3 39.3 all-reduce.22
  1336.8 4.2 fusion.80
  1341.0 12.4 convolution_add_fusion.2
  1355.0 51.3 reduce-scatter.19.cloned.1.call-done
  1407.7 710.2 %reduce-scatter.13.cloned.1.call-done = f32[128,2048]{1,0:T(8,128)} async-done(((f32[4096,2048]{1,0:T(8,128)}), f32[128,2048]{1,0:T(8,128)}) %reduce-scatter.13.cloned.1.call-update) | async-done | bytes 1048592 | tf_op jit(solution)/shard_map/reduce_scatter | solution.py:251
  2117.9 974.7 %reduce-scatter.17.cloned.1.call-done = f32[176,2048]{1,0:T(8,128)} async-done(((f32[5632,2048]{1,0:T(8,128)}), f32[176,2048]{1,0:T(8,128)}) %reduce-scatter.17.cloned.1.call-update) | async-done | bytes 1441808 | tf_op jit(solution)/shard_map/reduce_scatter | solution.py:198
  3092.7 835.1 %reduce-scatter.11.cloned.1.call-done = f32[64,12288]{1,0:T(8,128)} async-done(((f32[2048,12288]{1,0:T(8,128)}), f32[64,12288]{1,0:T(8,128)}) %reduce-scatter.11.cloned.1.call-update) | async-done | bytes 3145744 | tf_op jit(solution)/shard_map/reduce_scatter | solution.py:249
  3927.7 1937.5 %reduce-scatter.15.cloned.1.call-done = f32[64,11264]{1,0:T(8,128)} async-done(((f32[2048,11264]{1,0:T(8,128)}), f32[64,11264]{1,0:T(8,128)}) %reduce-scatter.15.cloned.1.call-update) | async-done | bytes 2883600 | tf_op jit(solution)/shard_map/reduce_scatter | solution.py:216
  (443 shorter events, 231.8 us)
Async XLA Ops:
  7.2 48.3 copy-start.95
  7.2 286.9 %all-gather.6.cloned.1.call-start = ((), (), s32[]{:S(2)}) async-start(), calls=%async_computation.6 | async-start | bytes 51904512 | tf_op jit(solution)/shard_map/all_gather | solution.py:153
  7.9 119.8 %copy-start.106 = (bf16[64]{0:T(256)(128)(2,1)S(1)}, bf16[64]{0:T(256)(128)(2,1)}, u32[]{:S(2)}) copy-start(bf16[64]{0:T(256)(128)(2,1)} %param.23) | copy-start | bytes 388
  7.9 120.1 %copy-start.107 = (bf16[64]{0:T(256)(128)(2,1)S(1)}, bf16[64]{0:T(256)(128)(2,1)}, u32[]{:S(2)}) copy-start(bf16[64]{0:T(256)(128)(2,1)} %param.31) | copy-start | bytes 388
  7.9 164.2 %copy-start.10 = (bf16[256,2048]{1,0:T(8,128)(2,1)S(1)}, bf16[256,2048]{1,0:T(8,128)(2,1)}, u32[]{:S(2)}) copy-start(bf16[256,2048]{1,0:T(8,128)(2,1)} %param.20) | copy-start | bytes 3145732
  8.0 765.1 %all-gather.8.cloned.1.call-start = ((), (), s32[]{:S(2)}) async-start(), calls=%async_computation.7 | async-start | bytes 17301504 | tf_op jit(solution)/shard_map/all_gather | solution.py:155
  8.7 775.1 %all-gather.10.cloned.1.call-start = ((), (), s32[]{:S(2)}) async-start(), calls=%async_computation.8 | async-start | bytes 47579136 | tf_op jit(solution)/shard_map/all_gather | solution.py:183
  9.4 805.0 %all-gather.12.cloned.1.call-start = ((), (), s32[]{:S(2)}) async-start(), calls=%async_computation.9 | async-start | bytes 23789568 | tf_op jit(solution)/shard_map/all_gather | solution.py:184
  10.0 1343.4 %reduce-scatter.21.cloned.1.call-start = ((), (), s32[]{:S(2)}) async-start(), calls=%async_computation.15 | async-start | bytes 4325376
  55.5 118.2 %copy-start.98 = (f32[16]{0:T(128)S(1)}, f32[16]{0:T(128)}, u32[]{:S(2)}) copy-start(f32[16]{0:T(128)} %param.28) | copy-start | bytes 196
  127.4 49.8 copy-start.103
  127.7 191.9 %copy-start.53 = (bf16[2048,32]{0,1:T(8,128)(2,1)}, bf16[2048,32]{0,1:T(8,128)(2,1)S(1)}, u32[]{:S(2)}) copy-start(bf16[2048,32]{0,1:T(8,128)(2,1)S(1)} %reshape.331) | copy-start | bytes 393220
  172.2 147.4 %copy-start.47 = (f32[2048]{0:T(1024)}, f32[2048]{0:T(1024)S(1)}, u32[]{:S(2)}) copy-start(f32[2048]{0:T(1024)S(1)} %convert_element_type.76) | copy-start | bytes 24580
  173.2 146.5 %copy-start.57 = (f32[256]{0:T(256)}, f32[256]{0:T(256)S(1)}, u32[]{:S(2)}) copy-start(f32[256]{0:T(256)S(1)} %fusion.173) | copy-start | bytes 3076
  174.0 145.7 %copy-start.55 = (f32[16,4,64]{2,1,0:T(4,128)}, f32[16,4,64]{2,1,0:T(4,128)S(1)}, u32[]{:S(2)}) copy-start(f32[16,4,64]{2,1,0:T(4,128)S(1)} %reshape.300) | copy-start | bytes 49156
  174.0 526.1 %copy-start.45 = (f32[16,4,64]{2,0,1:T(8,128)}, f32[16,4,64]{2,0,1:T(8,128)S(1)}, u32[]{:S(2)}) copy-start(f32[16,4,64]{2,0,1:T(8,128)S(1)} %copy.464) | copy-start | bytes 49156
  174.3 688.1 %copy-start.49 = (f32[2048]{0:T(1024)}, f32[2048]{0:T(1024)S(1)}, u32[]{:S(2)}) copy-start(f32[2048]{0:T(1024)S(1)} %convert_element_type.87) | copy-start | bytes 24580
  175.1 196.4 %copy-start.37 = (f32[4,16,64]{2,1,0:T(8,128)}, f32[4,16,64]{2,1,0:T(8,128)S(1)}, u32[]{:S(2)}) copy-start(f32[4,16,64]{2,1,0:T(8,128)S(1)} %reduce_window_sum.22) | copy-start | bytes 49156
  249.5 122.1 %copy-start.73 = (pred[64,64]{1,0:T(8,128)(4,1)}, pred[64,64]{1,0:T(8,128)(4,1)S(1)}, u32[]{:S(2)}) copy-start(pred[64,64]{1,0:T(8,128)(4,1)S(1)} %get-tuple-element.779) | copy-start | bytes 12292
  249.5 122.1 %copy-start.75 = (pred[64,64]{1,0:T(8,128)(4,1)}, pred[64,64]{1,0:T(8,128)(4,1)S(1)}, u32[]{:S(2)}) copy-start(pred[64,64]{1,0:T(8,128)(4,1)S(1)} %get-tuple-element.778) | copy-start | bytes 12292
  250.9 120.7 %copy-start.90 = (pred[64,64]{1,0:T(8,128)(4,1)}, pred[64,64]{1,0:T(8,128)(4,1)S(1)}, u32[]{:S(2)}) copy-start(pred[64,64]{1,0:T(8,128)(4,1)S(1)} %get-tuple-element.780) | copy-start | bytes 12292
  250.9 439.3 %copy-start.61 = (f32[4,16,64]{2,1,0:T(8,128)}, f32[4,16,64]{2,1,0:T(8,128)S(1)}, u32[]{:S(2)}) copy-start(f32[4,16,64]{2,1,0:T(8,128)S(1)} %get-tuple-element.763) | copy-start | bytes 49156
  251.0 446.3 %copy-start.51 = (f32[4,16,64]{2,1,0:T(8,128)}, f32[4,16,64]{2,1,0:T(8,128)S(1)}, u32[]{:S(2)}) copy-start(f32[4,16,64]{2,1,0:T(8,128)S(1)} %get-tuple-element.762) | copy-start | bytes 49156
  251.0 446.3 %copy-start.63 = (f32[4,16,64]{2,1,0:T(8,128)}, f32[4,16,64]{2,1,0:T(8,128)S(1)}, u32[]{:S(2)}) copy-start(f32[4,16,64]{2,1,0:T(8,128)S(1)} %get-tuple-element.761) | copy-start | bytes 49156
  251.7 80.2 %copy-start.65 = (f32[1,8192]{1,0:T(1,128)}, f32[1,8192]{1,0:T(1,128)S(1)}, u32[]{:S(2)}) copy-start(f32[1,8192]{1,0:T(1,128)S(1)} %get-tuple-element.751) | copy-start | bytes 98308
  327.2 4.7 copy-start.67
  327.2 4.7 copy-start.69
  327.2 4.7 copy-start.71
  356.7 9.5 copy-start.85
  360.0 6.2 copy-start.83
  367.1 330.2 %copy-start.1 = (bf16[256,16,128]{2,0,1:T(8,128)(2,1)}, bf16[256,16,128]{2,0,1:T(8,128)(2,1)S(1)}, u32[]{:S(2)}) copy-start(bf16[256,16,128]{2,0,1:T(8,128)(2,1)S(1)} %fusion.90) | copy-start | bytes 3145732
  690.3 7.0 copy-start.22
  697.3 4.3 copy-start.14
  701.7 7.4 copy-start.104
  773.0 10.7 copy-start.24
  783.8 78.6 %copy-start.59 = (f32[256]{0:T(256)}, f32[256]{0:T(256)S(1)}, u32[]{:S(2)}) copy-start(f32[256]{0:T(256)S(1)} %fusion.174) | copy-start | bytes 3076
  783.8 30.7 copy-start.43
  810.0 30.2 copy-start.26
  878.8 8.3 copy-start.6
  1037.0 7.9 copy-start.4
  1037.0 7.9 copy-start.13
  1037.0 7.9 copy-start.46
  1058.2 4.8 copy-start.9
  1058.2 4.8 copy-start.34
  1063.0 4.9 copy-start.29
  1063.0 4.9 copy-start.31
  1063.0 4.9 copy-start.74
  1063.0 4.9 copy-start.91
  1123.7 282.6 %reduce-scatter.19.cloned.1.call-start = ((), (), s32[]{:S(2)}) async-start(), calls=%async_computation.14 | async-start | bytes 1081344
  1125.1 16.8 copy-start.77
  1125.1 16.8 copy-start.79
  1126.9 991.1 %reduce-scatter.13.cloned.1.call-start = ((), (), s32[]{:S(2)}) async-start(), calls=%async_computation.11 | async-start | bytes 34603008 | tf_op jit(solution)/shard_map/reduce_scatter | solution.py:251
  1141.9 1950.7 %reduce-scatter.17.cloned.1.call-start = ((), (), s32[]{:S(2)}) async-start(), calls=%async_computation.13 | async-start | bytes 47579136 | tf_op jit(solution)/shard_map/reduce_scatter | solution.py:198
  1163.0 2764.7 %reduce-scatter.11.cloned.1.call-start = ((), (), s32[]{:S(2)}) async-start(), calls=%async_computation.10 | async-start | bytes 103809024 | tf_op jit(solution)/shard_map/reduce_scatter | solution.py:249
  1163.1 4.8 copy-start.66
  1163.1 4.8 copy-start.68
  1163.1 4.8 copy-start.70
  1163.1 4.8 copy-start.72
  1230.6 4634.6 %reduce-scatter.15.cloned.1.call-start = ((), (), s32[]{:S(2)}) async-start(), calls=%async_computation.12 | async-start | bytes 95158272 | tf_op jit(solution)/shard_map/reduce_scatter | solution.py:216
  1267.9 24.7 copy-start.54
  1267.9 24.7 copy-start.78
  1267.9 24.7 copy-start.80
  1292.6 44.2 copy-start.93
  1336.8 4.2 copy-start.42
  (64 other events, 143.0 us)
Sparse Core Ops, SparseCore 0:
  10.9 283.0 all-gather.5
  297.0 113.7 all-gather.7
  413.6 254.8 all-gather.9
  671.2 143.2 all-gather.11
  1123.8 145.9 reduce-scatter.20
  1271.9 134.3 reduce-scatter.18
  1409.3 708.6 reduce-scatter.12
  2120.9 971.7 reduce-scatter.16
  3100.8 826.8 reduce-scatter.10
  3930.6 1934.5 reduce-scatter.14
where the time goes:
time: 5880 us; the launch traced here: 5870 us
  waiting for transfers between devices  4560 us (78%)
  matrix products  465 us (8%)
  other arithmetic  446 us (8%)
  blocking collectives  272 us (5%)
  local copies, waits for them, and re-layouts  112 us (2%)
    reduce_scatter x1, waiting for transfers between devices, local(): lax.psum_scatter(upgate_grad, ('dp', 'fsdp'), scatter_dimension=0, tiled=...  1940 us
    reduce_scatter x1, waiting for transfers between devices, local(): lax.psum_scatter(down_grad, ('dp', 'fsdp'), scatter_dimension=0, tiled=True)  975 us
    reduce_scatter x1, waiting for transfers between devices, local(): lax.psum_scatter(input_grad, ('dp', 'fsdp'), scatter_dimension=0, tiled=T...  835 us
    reduce_scatter x1, waiting for transfers between devices, local(): lax.psum_scatter(output_grad, ('dp', 'fsdp'), scatter_dimension=0, tiled=...  710 us
    another operation x3, other arithmetic, delta_rule(): jax.scipy.linalg.solve_triangular(lower_part, beta_blocks[..., None] * va...  317 us
  transfers between devices with their start and end apart: 10, of which 7 were waited for; matrix products, arithmetic and copies ran while one was open for 12% of the time, Pallas kernels for 0%

commit v1 on v0

v1 whole, which is shorter than its diff:
```python
import functools

import jax
import jax.numpy as jnp
from jax import lax
from jax.experimental import pallas as pl
from jax.experimental.pallas import tpu as pltpu
from jax.sharding import PartitionSpec as P

MESH = pl.DeviceIdType.MESH
F32 = jnp.float32
BF16 = jnp.bfloat16
EPSILON = 1e-06
DK = 128
DV = 256
NN = (((1,), (0,)), ((), ()))
NT = (((1,), (1,)), ((), ()))
TN = (((0,), (0,)), ((), ()))


def dot1(a, b, dims=NN):
    return lax.dot_general(a.astype(BF16), b.astype(BF16), dims, preferred_element_type=F32)


def halves(a):
    if a.dtype == BF16:
        return (a,)
    high = a.astype(BF16)
    return (high, (a - high.astype(F32)).astype(BF16))


def dot3(a, b, dims=NN):
    a, b = halves(a), halves(b)
    total = lax.dot_general(a[0], b[0], dims, preferred_element_type=F32)
    if len(a) > 1:
        total = total + lax.dot_general(a[1], b[0], dims, preferred_element_type=F32)
    if len(b) > 1:
        total = total + lax.dot_general(a[0], b[1], dims, preferred_element_type=F32)
    return total


def dot6(a, b, dims=NN):
    return lax.dot_general(a, b, dims, precision=lax.Precision.HIGHEST, preferred_element_type=F32)


def shift_down(v, n, rows):
    if n == 0:
        return v
    return jnp.where(rows >= n, pltpu.roll(v, n, 0), 0.0)


def shift_up(v, n, rows):
    if n == 0:
        return v
    length = v.shape[0]
    return jnp.where(rows < length - n, pltpu.roll(v, length - n, 0), 0.0)


def conv(c, taps, rows):
    count = taps.shape[0]
    total = c * taps[count - 1 : count]
    for j in range(count - 1):
        total = total + shift_down(c, count - 1 - j, rows) * taps[j : j + 1]
    return total


def sigmoid(v):
    return 1.0 / (1.0 + jnp.exp(-v))


def softplus(v):
    return jnp.maximum(v, 0.0) + jnp.log1p(jnp.exp(-jnp.abs(v)))


def unit_inverse(lower, row_ids, col_ids):
    length = lower.shape[0]
    eye = jnp.where(row_ids == col_ids, 1.0, 0.0)
    size = 8
    base = jnp.where(row_ids // size == col_ids // size, lower, 0.0)
    square = dot6(base, base)
    inverse = dot6(eye - base, eye + square)
    inverse = inverse + dot6(inverse, dot6(square, square))
    while size < length:
        wide = 2 * size
        off = jnp.where(
            (row_ids // wide == col_ids // wide) & (row_ids // size != col_ids // size), lower, 0.0
        )
        inverse = inverse - dot3(inverse, dot3(off, inverse))
        size = wide
    return inverse


def common(proj, taps, decay, heads, length):
    rows = lax.broadcasted_iota(jnp.int32, (length, 1), 0)
    row_ids = lax.broadcasted_iota(jnp.int32, (length, length), 0)
    col_ids = lax.broadcasted_iota(jnp.int32, (length, length), 1)
    raw = proj[:, heads * 768 :]
    lanes = lax.broadcasted_iota(jnp.int32, raw.shape, 1)
    shifted = raw + decay[1:2]
    rate = jnp.where(lanes < heads, -jnp.exp(decay[0:1]) * softplus(shifted), 0.0)
    beta = sigmoid(raw)
    cumulated = dot6(jnp.where(row_ids >= col_ids, 1.0, 0.0), rate)
    return rows, row_ids, col_ids, raw, lanes, shifted, rate, beta, cumulated, cumulated.T


def head_parts(h, proj, taps, heads, rows):
    key = slice(h * DK, (h + 1) * DK)
    keyk = slice((heads + h) * DK, (heads + h + 1) * DK)
    val = slice(heads * DV + h * DV, heads * DV + (h + 1) * DV)
    gat = slice(2 * heads * DV + h * DV, 2 * heads * DV + (h + 1) * DV)
    return key, keyk, val, gat


def mixer_forward_kernel(heads, proj_ref, taps_ref, decay_ref, gain_ref, mixed_ref, inv_ref, solved_ref, core_ref):
    length = proj_ref.shape[0]
    taps_all = taps_ref[...]
    decay = decay_ref[...]
    gain = gain_ref[...]
    rows, row_ids, col_ids, raw, lanes, shifted, rate, beta, cumulated, cum_t = common(
        proj_ref[...], taps_all, decay, heads, length
    )
    for h in range(heads):
        qs, ks, vs, gs = head_parts(h, None, None, heads, rows)

        def active(cols):
            y = conv(proj_ref[:, cols], taps_ref[:, cols], rows)
            return y * sigmoid(y)

        q = active(qs)
        q = (q * lax.rsqrt(jnp.sum(q * q, axis=-1, keepdims=True) + EPSILON) * DK ** (-0.5)).astype(BF16)
        k = active(ks)
        k = (k * lax.rsqrt(jnp.sum(k * k, axis=-1, keepdims=True) + EPSILON)).astype(BF16)
        v = active(vs).astype(BF16)
        beta_h = beta[:, heads + h : heads + h + 1]
        gap = cumulated[:, h : h + 1] - cum_t[h : h + 1, :]
        growth = jnp.where(row_ids >= col_ids, jnp.exp(jnp.where(row_ids >= col_ids, gap, 0.0)), 0.0)
        gram = dot1(k, k, NT)
        lower = jnp.where(row_ids > col_ids, growth * gram * beta_h, 0.0)
        inverse = unit_inverse(lower, row_ids, col_ids)
        solved = dot3(inverse, beta_h * v.astype(F32))
        weights = growth * dot1(q, k, NT)
        core = dot3(weights, solved)
        inv_ref[h] = inverse
        solved_ref[:, h * DV : (h + 1) * DV] = solved
        core_ref[:, h * DV : (h + 1) * DV] = core
        gate = proj_ref[:, gs]
        normed = core * lax.rsqrt(jnp.mean(core * core, axis=-1, keepdims=True) + EPSILON) * gain
        mixed_ref[:, h * DV : (h + 1) * DV] = (normed * (gate * sigmoid(gate))).astype(BF16)


def mixer_forward(proj, taps, decay, gain, heads, length):
    tokens, width = proj.shape
    seqs = tokens // length
    hv = heads * DV
    row = lambda cols: pl.BlockSpec((length, cols), lambda s: (s, 0))
    whole = lambda a: pl.BlockSpec(a.shape, lambda s: (0,) * a.ndim)
    return pl.pallas_call(
        functools.partial(mixer_forward_kernel, heads),
        grid=(seqs,),
        in_specs=[row(width), whole(taps), whole(decay), whole(gain)],
        out_specs=[row(hv), pl.BlockSpec((None, heads, length, length), lambda s: (s, 0, 0, 0)), row(hv), row(hv)],
        out_shape=[
            jax.ShapeDtypeStruct((tokens, hv), BF16),
            jax.ShapeDtypeStruct((seqs, heads, length, length), F32),
            jax.ShapeDtypeStruct((tokens, hv), F32),
            jax.ShapeDtypeStruct((tokens, hv), F32),
        ],
        compiler_params=pltpu.CompilerParams(vmem_limit_bytes=48 << 20),
    )(proj, taps, decay, gain)


def mixer_backward_kernel(
    heads, proj_ref, taps_ref, decay_ref, gain_ref, inv_ref, solved_ref, core_ref, grad_ref,
    low_ref, conv_ref, gain_grad_ref, decay_grad_ref,
):
    length = proj_ref.shape[0]
    count = taps_ref.shape[0]
    decay = decay_ref[...]
    gain = gain_ref[...]
    rows, row_ids, col_ids, raw, lanes, shifted, rate, beta, cumulated, cum_t = common(
        proj_ref[...], None, decay, heads, length
    )
    within = row_ids >= col_ids
    strict = row_ids > col_ids

    @pl.when(pl.program_id(0) == 0)
    def _():
        conv_ref[...] = jnp.zeros_like(conv_ref)
        gain_grad_ref[...] = jnp.zeros_like(gain_grad_ref)
        decay_grad_ref[...] = jnp.zeros_like(decay_grad_ref)

    cum_grad = jnp.zeros(raw.shape, F32)
    beta_grad = jnp.zeros(raw.shape, F32)
    for h in range(heads):
        qs, ks, vs, gs = head_parts(h, None, None, heads, rows)
        hs = slice(h * DV, (h + 1) * DV)

        def active(cols):
            y = conv(proj_ref[:, cols], taps_ref[:, cols], rows)
            s = sigmoid(y)
            return y * s, s * (1.0 + y * (1.0 - s))

        def conv_back(cols, grad):
            c = proj_ref[:, cols]
            total = grad * taps_ref[count - 1 : count, cols]
            conv_ref[count - 1 : count, cols] += jnp.sum(grad * c, axis=0, keepdims=True)
            for j in range(count - 1):
                n = count - 1 - j
                total = total + shift_up(grad, n, rows) * taps_ref[j : j + 1, cols]
                conv_ref[j : j + 1, cols] += jnp.sum(grad * shift_down(c, n, rows), axis=0, keepdims=True)
            low_ref[:, cols] = total.astype(BF16)

        core = core_ref[:, hs]
        gate = proj_ref[:, gs]
        gate_sig = sigmoid(gate)
        grad = grad_ref[:, hs]
        root = lax.rsqrt(jnp.mean(core * core, axis=-1, keepdims=True) + EPSILON)
        normed = core * root
        silu_gate = gate * gate_sig
        gain_grad_ref[...] += jnp.sum(grad * normed * silu_gate, axis=0, keepdims=True)
        low_ref[:, gs] = (grad * normed * gain * gate_sig * (1.0 + gate * (1.0 - gate_sig))).astype(BF16)
        normed_grad = grad * gain * silu_gate
        core_grad = root * (normed_grad - normed * jnp.mean(normed_grad * normed, axis=-1, keepdims=True))

        q_act, q_slope = active(qs)
        q_root = lax.rsqrt(jnp.sum(q_act * q_act, axis=-1, keepdims=True) + EPSILON)
        q_unit = q_act * q_root
        q = (q_unit * DK ** (-0.5)).astype(BF16)
        k_act, k_slope = active(ks)
        k_root = lax.rsqrt(jnp.sum(k_act * k_act, axis=-1, keepdims=True) + EPSILON)
        k_unit = k_act * k_root
        k = k_unit.astype(BF16)
        v_act, v_slope = active(vs)
        v = v_act.astype(BF16).astype(F32)
        beta_h = beta[:, heads + h : heads + h + 1]
        gap = cumulated[:, h : h + 1] - cum_t[h : h + 1, :]
        growth = jnp.where(within, jnp.exp(jnp.where(within, gap, 0.0)), 0.0)
        decayed_gram = jnp.where(strict, growth * dot1(k, k, NT), 0.0)
        weights = growth * dot1(q, k, NT)
        inverse = inv_ref[h]
        solved = solved_ref[:, hs]
        solved_grad = dot3(weights, core_grad, TN)
        weights_grad = dot3(core_grad, solved, NT)
        value_grad = dot3(inverse, solved_grad, TN)
        lower_grad = jnp.where(strict, -dot3(value_grad, solved, NT), 0.0)
        gap_part = lower_grad * decayed_gram
        beta_col = jnp.sum(gap_part, axis=-1, keepdims=True) + jnp.sum(value_grad * v, axis=-1, keepdims=True)
        gap_grad = gap_part * beta_h + weights_grad * weights
        cum_col = jnp.sum(gap_grad, axis=-1, keepdims=True)
        cum_row = jnp.sum(gap_grad, axis=0, keepdims=True)
        cum_col = cum_col - jnp.broadcast_to(cum_row, (8, length)).T[:, 0:1]
        gram_grad = lower_grad * growth * beta_h
        score_grad = weights_grad * growth
        k_grad = dot3(gram_grad, k) + dot3(gram_grad, k, TN) + dot3(score_grad, q, TN)
        q_grad = dot3(score_grad, k)
        cum_grad = jnp.where(lanes == h, cum_col, cum_grad)
        beta_grad = jnp.where(lanes == heads + h, beta_col, beta_grad)

        q_grad = q_grad * DK ** (-0.5)
        q_grad = q_root * (q_grad - q_unit * jnp.sum(q_grad * q_unit, axis=-1, keepdims=True))
        conv_back(qs, q_grad * q_slope)
        k_grad = k_root * (k_grad - k_unit * jnp.sum(k_grad * k_unit, axis=-1, keepdims=True))
        conv_back(ks, k_grad * k_slope)
        conv_back(vs, value_grad * beta_h * v_slope)

    rate_grad = dot6(jnp.where(col_ids >= row_ids, 1.0, 0.0), cum_grad)
    bias_part = rate_grad * -jnp.exp(decay[0:1]) * sigmoid(shifted)
    raw_grad = jnp.where(lanes < heads, bias_part, beta_grad * beta * (1.0 - beta))
    low_ref[:, heads * 768 :] = raw_grad.astype(BF16)
    decay_grad_ref[0:1] += jnp.sum(jnp.where(lanes < heads, rate_grad * rate, 0.0), axis=0, keepdims=True)
    decay_grad_ref[1:2] += jnp.sum(jnp.where(lanes < heads, bias_part, 0.0), axis=0, keepdims=True)


def mixer_backward(proj, taps, decay, gain, inverse, solved, core, grad, heads, length):
    tokens, width = proj.shape
    seqs = tokens // length
    hv = heads * DV
    row = lambda cols: pl.BlockSpec((length, cols), lambda s: (s, 0))
    whole = lambda a: pl.BlockSpec(a.shape, lambda s: (0,) * a.ndim)
    return pl.pallas_call(
        functools.partial(mixer_backward_kernel, heads),
        grid=(seqs,),
        in_specs=[row(width), whole(taps), whole(decay), whole(gain),
                  pl.BlockSpec((None, heads, length, length), lambda s: (s, 0, 0, 0)), row(hv), row(hv), row(hv)],
        out_specs=[row(width), whole(taps), whole(gain), whole(decay)],
        out_shape=[
            jax.ShapeDtypeStruct((tokens, width), BF16),
            jax.ShapeDtypeStruct(taps.shape, F32),
            jax.ShapeDtypeStruct(gain.shape, F32),
            jax.ShapeDtypeStruct(decay.shape, F32),
        ],
        compiler_params=pltpu.CompilerParams(vmem_limit_bytes=56 << 20),
    )(proj, taps, decay, gain, inverse, solved, core, grad)


def _place(n_dp):
    me = lax.axis_index("dp")
    z = lax.axis_index("fsdp")
    core = lax.rem(me, 2)
    chip = me // 2
    return me, z, core, lax.rem(chip, 2), chip // 2

def ag_square(x, cid, chunks=4):
    rows, cols = x.shape
    r = rows // chunks
    def kernel(x_ref, o_ref, lsem, ssem, rsem, dssem, drsem, fs, fr):
        me, z, core, cx, cy = _place(8)
        dev = lambda dx, dy, c: 2*(2*lax.rem(cy+dy,2)+lax.rem(cx+dx,2))+c
        nx, ny, nd = dev(1,0,core), dev(0,1,core), dev(1,1,core)
        src = dev(1-core, core, core)
        tgt = dev(core, 1-core, core)
        sib = dev(0,0,1-core)
        bar = pltpu.get_barrier_semaphore()
        for d in (sib,nx,ny):
            pl.semaphore_signal(bar, inc=1, device_id=(d,z), device_id_type=MESH)
        pl.semaphore_wait(bar, 3)
        lc = pltpu.make_async_copy(x_ref, o_ref.at[me], lsem); lc.start()
        def rc(a, b, s, q, d):
            return pltpu.make_async_remote_copy(a, b, s, q, device_id=(d,z), device_id_type=MESH)
        own = []
        for c in range(chunks):
            sl = pl.ds(c*r, r)
            for i, d in ((0,nx),(1,ny)):
                cp = rc(x_ref.at[sl], o_ref.at[me,sl], ssem.at[i,c], rsem.at[i,c], d); cp.start(); own.append(cp)
        sibs=[]
        for c in range(chunks):
            sl = pl.ds(c*r, r)
            cp = rc(x_ref.at[sl], o_ref.at[me,sl], fs.at[0,c], fr.at[0,c], sib); cp.start(); sibs.append(cp)
        other = dev(core, 1-core, core)
        for c in range(chunks):
            sl = pl.ds(c*r, r)
            rc(x_ref.at[sl], o_ref.at[src,sl], ssem.at[core,c], rsem.at[core,c], sib).wait_recv()
            cp = rc(o_ref.at[src,sl], o_ref.at[src,sl], dssem.at[c], drsem.at[c], tgt); cp.start(); sibs.append((cp,))
            cp = rc(o_ref.at[src,sl], o_ref.at[src,sl], fs.at[1,c], fr.at[1,c], sib); cp.start(); sibs.append(cp)
            rc(x_ref.at[sl], o_ref.at[other,sl], ssem.at[1-core,c], rsem.at[1-core,c], sib).wait_recv()
            cp = rc(o_ref.at[other,sl], o_ref.at[other,sl], fs.at[2,c], fr.at[2,c], sib); cp.start(); sibs.append(cp)
        for c in range(chunks):
            sl = pl.ds(c*r, r)
            rc(x_ref.at[sl], o_ref.at[nd,sl], dssem.at[c], drsem.at[c], sib).wait_recv()
            cp = rc(o_ref.at[nd,sl], o_ref.at[nd,sl], fs.at[3,c], fr.at[3,c], sib); cp.start(); sibs.append(cp)
        for cp in own: cp.wait_send()
        for cp in sibs:
            if isinstance(cp, tuple): cp[0].wait_send()
            else: cp.wait()
        lc.wait()
    D=pltpu.SemaphoreType.DMA
    return pl.pallas_call(kernel, out_shape=jax.ShapeDtypeStruct((8,rows,cols),x.dtype),
        in_specs=[pl.BlockSpec(memory_space=pl.ANY)], out_specs=pl.BlockSpec(memory_space=pl.ANY),
        scratch_shapes=[D, D((2,chunks)), D((2,chunks)), D((chunks,)), D((chunks,)), D((4,chunks)), D((4,chunks))],
        compiler_params=pltpu.CompilerParams(collective_id=cid, has_side_effects=True))(x)

def rs_square(x, cid, chunks=4):
    _, rows, cols = x.shape
    r = rows // chunks
    def kernel(x_ref, o_ref, X, A, B, R, lsem, sa, ra, sb, rb):
        me, z, core, cx, cy = _place(8)
        dev = lambda dx, dy, c: 2*(2*lax.rem(cy+dy,2)+lax.rem(cx+dx,2))+c
        fdx, fdy = 1-core, core
        nf, ng = dev(fdx,fdy,core), dev(fdy,fdx,core)
        sib = dev(0,0,1-core)
        bar = pltpu.get_barrier_semaphore()
        for d in (sib,nf,ng):
            pl.semaphore_signal(bar, inc=1, device_id=(d,z), device_id_type=MESH)
        mine = [dev(1,1,core), ng, nf, me]
        s_f, s_g = dev(core,1-core,1-core), dev(1-core,core,1-core)
        theirs = [dev(1,1,1-core), s_g, s_f, sib]
        loads=[]
        for k in range(4):
            for c in range(chunks):
                sl=pl.ds(c*r,r)
                cp=pltpu.make_async_copy(x_ref.at[mine[k],sl], X.at[k,sl], lsem.at[k,c]); cp.start(); loads.append(cp)
        pl.semaphore_wait(bar, 3)
        def rc(a, b, s, q, d):
            return pltpu.make_async_remote_copy(a, b, s, q, device_id=(d,z), device_id_type=MESH)
        sends=[]; ga={}
        for k in range(4):
            for c in range(chunks):
                sl=pl.ds(c*r,r)
                cp=rc(x_ref.at[theirs[k],sl], A.at[k,sl], sa.at[k,c], ra.at[k,c], sib); cp.start(); sends.append(cp); ga[k,c]=cp
        def pair(k,c):
            sl=pl.ds(c*r,r)
            loads[k*chunks+c].wait(); ga[k,c].wait_recv()
            return X[k,sl].astype(F32)+A[k,sl].astype(F32)
        gb={}
        def ship(slot, c, d):
            sl=pl.ds(c*r,r)
            cp=rc(B.at[slot,sl], R.at[slot,sl], sb.at[slot,c], rb.at[slot,c], d); cp.start(); sends.append(cp); gb[slot,c]=cp
        for c in range(chunks):
            sl=pl.ds(c*r,r)
            B[0,sl]=pair(0,c).astype(BF16); ship(0,c,nf)
        for c in range(chunks):
            sl=pl.ds(c*r,r)
            B[2,sl]=pair(2,c).astype(BF16); ship(2,c,nf)
        for c in range(chunks):
            sl=pl.ds(c*r,r)
            v=pair(1,c)
            gb[0,c].wait_recv()
            B[1,sl]=(v+R[0,sl].astype(F32)).astype(BF16); ship(1,c,ng)
        for c in range(chunks):
            sl=pl.ds(c*r,r)
            v=pair(3,c)
            gb[2,c].wait_recv()
            o_ref[sl]=v+R[2,sl].astype(F32)
        for c in range(chunks):
            sl=pl.ds(c*r,r)
            gb[1,c].wait_recv()
            o_ref[sl]=o_ref[sl]+R[1,sl].astype(F32)
        for cp in sends: cp.wait_send()
    D=pltpu.SemaphoreType.DMA
    V=lambda n: pltpu.VMEM((n,rows,cols),x.dtype)
    return pl.pallas_call(kernel, out_shape=jax.ShapeDtypeStruct((rows,cols),F32),
        in_specs=[pl.BlockSpec(memory_space=pl.ANY)], out_specs=pl.BlockSpec(memory_space=pltpu.VMEM),
        scratch_shapes=[V(4),V(4),V(3),V(3), D((4,chunks)), D((4,chunks)), D((4,chunks)), D((3,chunks)), D((3,chunks))],
        compiler_params=pltpu.CompilerParams(collective_id=cid, has_side_effects=True, vmem_limit_bytes=40<<20))(x)

def gather_small(x, n_dp, n_z, cid):
    rows, cols = x.shape
    count = n_dp * n_z

    def kernel(x_ref, o_ref, lsem, ssem, rsem):
        flat = lax.axis_index("dp") * n_z + lax.axis_index("fsdp")
        bar = pltpu.get_barrier_semaphore()

        def device(o):
            other = lax.rem(flat + o, count)
            return (other // n_z, lax.rem(other, n_z))

        def copy(o):
            return pltpu.make_async_remote_copy(
                x_ref, o_ref.at[flat], ssem.at[o - 1], rsem.at[o - 1], device_id=device(o), device_id_type=MESH
            )

        def greet(o, _):
            pl.semaphore_signal(bar, inc=1, device_id=device(o), device_id_type=MESH)
            return 0

        def send(o, _):
            copy(o).start()
            return 0

        def wait(o, _):
            copy(o).wait()
            return 0

        lax.fori_loop(1, count, greet, 0)
        local = pltpu.make_async_copy(x_ref, o_ref.at[flat], lsem)
        local.start()
        pl.semaphore_wait(bar, count - 1)
        lax.fori_loop(1, count, send, 0)
        lax.fori_loop(1, count, wait, 0)
        local.wait()

    dma = pltpu.SemaphoreType.DMA
    return pl.pallas_call(
        kernel,
        out_shape=jax.ShapeDtypeStruct((count, rows, cols), x.dtype),
        in_specs=[pl.BlockSpec(memory_space=pl.ANY)],
        out_specs=pl.BlockSpec(memory_space=pl.ANY),
        scratch_shapes=[dma, dma((count - 1,)), dma((count - 1,))],
        compiler_params=pltpu.CompilerParams(collective_id=cid, has_side_effects=True),
    )(x)


def pack(parts, unit):
    flat = jnp.concatenate([part.reshape(-1) for part in parts])
    size = flat.shape[0]
    full = -(-size // (128 * unit)) * 128 * unit
    return jnp.pad(flat, (0, full - size)).reshape(-1, 128)


def dot(a, b, dims=NN, out=F32):
    return lax.dot_general(a, b, dims, preferred_element_type=F32).astype(out)


def local(
    n_dp,
    n_z,
    tokens,
    cotangent,
    group_ids,
    norm_first,
    input_weight,
    decay_weight,
    conv_weight,
    decay_scale,
    decay_bias,
    output_gain,
    output_weight,
    norm_second,
    upgate_weight,
    down_weight,
):
    count = n_dp * n_z
    rows, width = tokens.shape
    all_heads = decay_scale.shape[0]
    heads = all_heads // n_dp
    taps = conv_weight.shape[0]
    own_conv = conv_weight.shape[1]
    own_d = norm_first.shape[0]
    units = upgate_weight.shape[1] // (2 * n_dp)
    key, value = heads * DK, heads * DV
    cols = 2 * key + 2 * value + 128
    square = n_dp == 8
    here = lax.axis_index("dp")
    flat = here * n_z + lax.axis_index("fsdp")

    def spread(x, cid):
        if square:
            return ag_square(x, cid).reshape(n_dp * rows, width)
        return lax.all_gather(x, "dp", axis=0, tiled=True)

    def total(x, cid):
        if square:
            return rs_square(x.reshape(n_dp, rows, width), cid)
        return lax.psum_scatter(x, "dp", scatter_dimension=0, tiled=True).astype(F32)

    def by_dp(a, parts):
        return a.reshape(a.shape[0], n_dp, parts)

    pieces = (
        by_dp(input_weight[:, : n_dp * key], key),
        by_dp(input_weight[:, n_dp * key : 2 * n_dp * key], key),
        by_dp(input_weight[:, 2 * n_dp * key : 2 * n_dp * key + n_dp * value], value),
        by_dp(input_weight[:, 2 * n_dp * key + n_dp * value :], value),
        by_dp(decay_weight[:, :all_heads], heads),
        by_dp(decay_weight[:, all_heads:], heads),
        jnp.zeros((own_d, n_dp, 128 - 2 * heads), BF16),
    )
    in_mine = jnp.concatenate(pieces, axis=2).transpose(1, 0, 2)
    gate_mine = by_dp(upgate_weight[:, : n_dp * units], units).transpose(1, 0, 2)
    up_mine = by_dp(upgate_weight[:, n_dp * units :], units).transpose(1, 0, 2)

    def whole_rows(a):
        a = lax.all_to_all(a, "dp", 0, 0, tiled=True)
        a = lax.all_gather(a[:, None], "fsdp", axis=1, tiled=True)
        return a.reshape(width, a.shape[-1])

    in_full = whole_rows(in_mine)
    out_full = lax.all_gather(output_weight, "fsdp", axis=0, tiled=True)
    gate_full = whole_rows(gate_mine)
    up_full = whole_rows(up_mine)
    down_full = lax.all_gather(down_weight, "fsdp", axis=0, tiled=True)

    small = gather_small(
        pack((conv_weight, norm_first, norm_second, group_ids.astype(BF16)), 16), n_dp, n_z, 1
    ).reshape(count, -1)
    conv_size = taps * own_conv
    conv_full = small[:, :conv_size].reshape(count, taps, own_conv).transpose(1, 0, 2).reshape(taps, -1)
    first_full = small[:, conv_size : conv_size + own_d].reshape(1, width).astype(F32)
    second_full = small[:, conv_size + own_d : conv_size + 2 * own_d].reshape(1, width).astype(F32)
    every_id = small[:, conv_size + 2 * own_d].astype(jnp.int32)
    scale = 1.0 / jnp.sum((every_id == group_ids[0]).astype(F32))

    def conv_columns(start, size):
        return lax.dynamic_slice_in_dim(conv_full, start + here * size, size, axis=1)

    conv_mine = jnp.concatenate(
        [conv_columns(0, key), conv_columns(n_dp * key, key), conv_columns(2 * n_dp * key, value)], axis=1
    ).astype(F32)
    decay_mine = jnp.pad(
        jnp.stack(
            [
                lax.dynamic_slice_in_dim(decay_scale, here * heads, heads),
                lax.dynamic_slice_in_dim(decay_bias, here * heads, heads),
            ]
        ),
        ((0, 0), (0, 128 - heads)),
    )
    gain = output_gain[None, :]

    inputs = tokens.astype(F32)
    first_root = lax.rsqrt(jnp.mean(inputs * inputs, axis=-1, keepdims=True) + EPSILON)
    normed_all = spread((inputs * first_root * first_full).astype(BF16), 2)
    seed = cotangent.astype(F32) * scale
    seed_all = spread(seed.astype(BF16), 3)
    projected = dot(normed_all, in_full)
    mixed, inverse, solved, core = mixer_forward(projected, conv_mine, decay_mine, gain, heads, rows)
    middle = inputs + total(dot(mixed, out_full, out=BF16), 4)
    second_root = lax.rsqrt(jnp.mean(middle * middle, axis=-1, keepdims=True) + EPSILON)
    second_all = spread((middle * second_root * second_full).astype(BF16), 5)
    gate_part = dot(second_all, gate_full)
    up_part = dot(second_all, up_full)
    gate_sig = jax.nn.sigmoid(gate_part)
    hidden = (gate_part * gate_sig * up_part).astype(BF16)
    hidden_grad = dot(seed_all, down_full, NT)
    gate_low = (hidden_grad * up_part * gate_sig * (1.0 + gate_part * (1.0 - gate_sig))).astype(BF16)
    up_low = (hidden_grad * gate_part * gate_sig).astype(BF16)

    back_two = (dot(gate_low, gate_full, NT) + dot(up_low, up_full, NT)).astype(BF16)
    normed_two_grad = total(back_two, 6)
    result = middle + total(dot(hidden, down_full, out=BF16), 7)

    def norm_back(v, root, gain_row, grad):
        hat = v * root
        scaled = grad * gain_row
        gain_grad = jnp.sum(grad * hat, axis=0)
        return root * (scaled - hat * jnp.mean(scaled * hat, axis=-1, keepdims=True)), gain_grad

    middle_part, second_grad = norm_back(middle, second_root, second_full, normed_two_grad)
    middle_grad = seed + middle_part
    middle_all = spread(middle_grad.astype(BF16), 8)
    mixed_grad = dot(middle_all, out_full, NT)
    projected_low, conv_grad, gain_grad, decay_grad = mixer_backward(
        projected, conv_mine, decay_mine, gain, inverse, solved, core, mixed_grad, heads, rows
    )
    normed_one_grad = total(dot(projected_low, in_full, NT, out=BF16), 9)
    input_part, first_grad = norm_back(inputs, first_root, first_full, normed_one_grad)
    tokens_grad = middle_grad + input_part

    def owned_rows(a):
        return lax.psum_scatter(a, "fsdp", scatter_dimension=0, tiled=True)

    def owned_parts(a):
        a = a.reshape(n_dp, n_z, own_d, a.shape[-1]).transpose(1, 0, 2, 3)
        a = lax.psum_scatter(a.reshape(width, -1), "fsdp", scatter_dimension=0, tiled=True)
        a = lax.all_to_all(a.reshape(n_dp, own_d, -1), "dp", 0, 0, tiled=True)
        return a.transpose(1, 0, 2).astype(F32)

    down_total = owned_rows(dot(hidden, seed_all, TN, out=BF16)).astype(F32)
    gate_total = owned_parts(dot(second_all, gate_low, TN, out=BF16))
    up_total = owned_parts(dot(second_all, up_low, TN, out=BF16))
    upgate_total = jnp.concatenate([gate_total.reshape(own_d, -1), up_total.reshape(own_d, -1)], axis=1)
    output_total = owned_rows(dot(mixed, middle_all, TN, out=BF16)).astype(F32)
    in_total = owned_parts(dot(normed_all, projected_low, TN, out=BF16))
    bounds = (0, key, 2 * key, 2 * key + value, 2 * key + 2 * value)
    input_total = jnp.concatenate(
        [in_total[:, :, a:b].reshape(own_d, -1) for a, b in zip(bounds[:-1], bounds[1:])], axis=1
    )
    start = bounds[-1]
    decay_total = jnp.concatenate(
        [
            in_total[:, :, start : start + heads].reshape(own_d, -1),
            in_total[:, :, start + heads : start + 2 * heads].reshape(own_d, -1),
        ],
        axis=1,
    )

    sizes = (first_grad.size, second_grad.size, gain_grad.size, conv_grad.size, 2 * heads)
    shared = gather_small(
        pack((first_grad, second_grad, gain_grad, conv_grad, decay_grad[:, :heads]), 8), n_dp, n_z, 10
    ).reshape(count, -1)
    edges = [0]
    for size in sizes:
        edges.append(edges[-1] + size)
    summed = jnp.sum(shared[:, : edges[3]], axis=0)
    first_total = lax.dynamic_slice_in_dim(summed, flat * own_d, own_d)
    second_total = lax.dynamic_slice_in_dim(summed, edges[1] + flat * own_d, own_d)
    gain_total = summed[edges[2] : edges[3]]
    by_plane = jnp.sum(shared[:, edges[3] : edges[5]].reshape(n_dp, n_z, -1), axis=1)
    conv_all = by_plane[:, : sizes[3]].reshape(n_dp, taps, 2 * key + value)
    conv_row = jnp.concatenate(
        [
            conv_all[:, :, a:b].transpose(1, 0, 2).reshape(taps, -1)
            for a, b in ((0, key), (key, 2 * key), (2 * key, 2 * key + value))
        ],
        axis=1,
    )
    conv_total = lax.dynamic_slice_in_dim(conv_row, flat * own_conv, own_conv, axis=1)
    scale_bias = by_plane[:, sizes[3] :].reshape(n_dp, 2, heads)
    scale_total = scale_bias[:, 0].reshape(-1)
    bias_total = scale_bias[:, 1].reshape(-1)
    return (
        result,
        tokens_grad,
        first_total,
        input_total,
        decay_total,
        conv_total,
        scale_total,
        bias_total,
        gain_total,
        output_total,
        second_total,
        upgate_total,
        down_total,
    )


def solution(mesh):
    both = ("dp", "fsdp")
    rows, vector = P(both, None), P(both)
    return jax.shard_map(
        functools.partial(local, mesh.shape["dp"], mesh.shape["fsdp"]),
        mesh=mesh,
        in_specs=(
            rows, rows, vector, vector, rows, rows, P(None, both), P(), P(), P(), rows, vector, rows, rows,
        ),
        out_specs=(
            rows, rows, vector, rows, rows, P(None, both), P(), P(), P(), rows, vector, rows, rows,
        ),
        check_vma=False,
    )
```

time: 5880 us -> 1040 us (0.18)
  waiting for transfers between devices: 4560 us -> 118 us
  Pallas kernels: 0 us -> 525 us
  other arithmetic: 446 us -> 27.7 us
  matrix products: 465 us -> 190 us
  blocking collectives: 272 us -> 57.4 us
    reduce_scatter x4 -> x5, waiting for transfers between devices: 4460 us -> 2.56 us  [the longest x2 2.53 us: owned_rows(): return lax.psum_scatter(a, 'fsdp', scatter_dimension=0, tiled=True)]
    pallas_call x0 -> x12, Pallas kernels: none -> 525 us  [the longest x4 159 us: rs_square(): pl.pallas_call(kernel, out_shape=jax.ShapeDtypeStruct((rows, cols), F32),...]
    another operation x10 -> x1, other arithmetic: 325 us -> 0.01 us  [local(): jnp.stack([lax.dynamic_slice_in_dim(decay_scale, here * heads, heads), la...]
    dot_general x74 -> x15, matrix products: 430 us -> 190 us  [dot(): return lax.dot_general(a, b, dims, preferred_element_type=F32).astype(out)]
    all_gather x2 -> x0, blocking collectives: 144 us -> none  [the longest x1 72.3 us: local(): lax.all_gather(conv_weight, ('dp', 'fsdp'), axis=1, tiled=True)]
    unnamed x2 -> x0, blocking collectives: 83.2 us -> none
  transfers between devices with their start and end apart: 10 -> 13, of which waited for: 7 -> 5; matrix products, arithmetic and copies ran while one was open for 12% -> 24% of each run, Pallas kernels for 0% -> 51%
where the time goes in v1:
time: 1040 us; the launch traced here: 1030 us
  Pallas kernels  525 us (50%)
  matrix products  190 us (18%)
  waiting for transfers between devices  118 us (11%)
  local copies, waits for them, and re-layouts  82 us (8%)
  blocking collectives  57.4 us (6%)
  other arithmetic  27.7 us (3%)
  between operations  16.7 us (2%)
  starting transfers between devices  13 us (1%)
    dot_general x15, matrix products, dot(): return lax.dot_general(a, b, dims, preferred_element_type=F32).astype(out)  190 us
    pallas_call x4, Pallas kernels, rs_square(): pl.pallas_call(kernel, out_shape=jax.ShapeDtypeStruct((rows, cols), F32),...  159 us
    pallas_call x4, Pallas kernels, ag_square(): pl.pallas_call(kernel, out_shape=jax.ShapeDtypeStruct((8, rows, cols), x....  154 us
    pallas_call x1, Pallas kernels, mixer_forward(): pl.pallas_call(functools.partial(mixer_forward_kernel, heads), grid=(seqs...  95.7 us
    all_gather x3, waiting for transfers between devices, whole_rows(): a = lax.all_gather(a[:, None], 'fsdp', axis=1, tiled=True)  89.4 us
    pallas_call x2, Pallas kernels, gather_small(): pl.pallas_call(kernel, out_shape=jax.ShapeDtypeStruct((count, rows, cols)...  65.1 us
    all_to_all x3, blocking collectives, whole_rows(): a = lax.all_to_all(a, 'dp', 0, 0, tiled=True)  57.4 us
    pallas_call x1, Pallas kernels, mixer_backward(): pl.pallas_call(functools.partial(mixer_backward_kernel, heads), grid=(seq...  50.6 us
  transfers between devices with their start and end apart: 13, of which 5 were waited for; matrix products, arithmetic and copies ran while one was open for 24% of the time, Pallas kernels for 51%

profile of v1, /device:TPU:0, one launch (start us, length us, event | category | flops | bytes accessed | tf_op | source)
XLA Modules:
  0.0 1029.1 jit_solution(11210110673858168572)
XLA Ops:
  9.5 17.5 %all_to_all.30 = bf16[8,64,704]{2,1,0:T(8,128)(2,1)S(1)} all-to-all(bf16[8,64,704]{2,1,0:T(8,128)(2,1)S(1)} %copy.103), channel_id=1, replica_groups=mesh['dp'=8,'fsdp'=4] {'dp'}, dimensions={0} | all-to-all | bytes 1441792 | tf_op jit(solution)/shard_map/all_to_all | solution.py:534
  29.2 15.1 %all_to_all.31 = bf16[8,64,704]{2,1,0:T(8,128)(2,1)S(1)} all-to-all(bf16[8,64,704]{2,1,0:T(8,128)(2,1)S(1)} %copy.106), channel_id=1, replica_groups=mesh['dp'=8,'fsdp'=4] {'dp'}, dimensions={0} | all-to-all | bytes 1441792 | tf_op jit(solution)/shard_map/all_to_all | solution.py:534
  47.4 1.9 concatenate.28
  49.5 24.8 %all_to_all.32 = bf16[8,64,1664]{2,1,0:T(8,128)(2,1)S(1)} all-to-all(bf16[8,64,1664]{2,1,0:T(8,128)(2,1)S(1)} %copy.100), channel_id=1, replica_groups=mesh['dp'=8,'fsdp'=4] {'dp'}, dimensions={0} | all-to-all | bytes 3407872 | tf_op jit(solution)/shard_map/all_to_all | solution.py:534
  74.3 2.1 copy.101
  79.3 12.6 %shard_map.237 = bf16[32,16,128]{2,1,0:T(8,128)(2,1)} custom-call(bf16[16,128]{1,0:T(8,128)(2,1)} %pad_bitcast_fusion.1.x_ref), custom_call_target="tpu_custom_call" | custom-call | tf_op jit(solution)/shard_map/pallas_call | solution.py:454
  95.9 37.6 %shard_map.243 = bf16[8,256,2048]{2,1,0:T(8,128)(2,1)} custom-call(bf16[256,2048]{1,0:T(8,128)(2,1)} %fusion.11.x_ref), custom_call_target="tpu_custom_call" | custom-call | tf_op jit(solution)/shard_map/pallas_call | solution.py:347
  134.8 39.3 %shard_map.238 = bf16[8,256,2048]{2,1,0:T(8,128)(2,1)} custom-call(bf16[256,2048]{1,0:T(8,128)(2,1)} %fusion.4.x_ref), custom_call_target="tpu_custom_call" | custom-call | tf_op jit(solution)/shard_map/pallas_call | solution.py:347
  174.4 5.3 copy.105
  179.7 4.4 copy.135
  184.1 5.3 copy.108
  189.4 4.4 copy.136
  193.8 89.4 %all-gather.13.cloned.1.call-done = bf16[8,256,1664]{2,0,1:T(8,128)(2,1)} async-done(((bf16[8,64,1664]{2,0,1:T(8,128)(2,1)}), bf16[8,256,1664]{2,0,1:T(8,128)(2,1)}) %all-gather.13.cloned.1.call-update) | async-done | bytes 6815760 | tf_op jit(solution)/shard_map/all_gather | solution.py:535
  283.1 3.8 copy.102
  286.9 21.1 %fusion.22.proj_ref = f32[2048,1664]{1,0:T(8,128)} fusion(bf16[2048,2048]{1,0:T(8,128)(2,1)} %bitcast.155, bf16[2048,1664]{1,0:T(8,128)(2,1)S(1)} %bitcast.164), kind=kOutput, calls=%fused_computation.83 | convolution fusion | flops 13958643712 | bytes 28835840 | tf_op jit(solution)/shard_map/dot_general | solution.py:472
  308.1 95.7 %shard_map.239 = (bf16[2048,512]{1,0:T(8,128)(2,1)S(1)}, f32[8,2,256,256]{3,2,1,0:T(8,128)}, f32[2048,512]{1,0:T(8,128)}, f32[2048,512]{1,0:T(8,128)}) custom-call(f32[2048,1664]{1,0:T(8,128)} %fusion.22.proj_ref, f32[4,1024]{1,0:T(4,128)S(1)} %maximum_convert_fusion.1.taps_ref, f32[2,128]{1,0:T(2,128)S(1)} %select_maximum_fusion.decay_ref, ...), custom_call_target="tpu_custom_call" | custom-call | tf_op jit(solution)/shard_map/pallas_call | solution.py:157
  403.8 7.1 convolution_convert_fusion.1
  410.9 40.0 %shard_map.240 = f32[256,2048]{1,0:T(8,128)S(1)} custom-call(bf16[8,256,2048]{2,1,0:T(8,128)(2,1)S(1)} %bitcast.143), custom_call_target="tpu_custom_call" | custom-call | tf_op jit(solution)/shard_map/pallas_call | solution.py:411
  453.9 38.8 %shard_map.241 = bf16[8,256,2048]{2,1,0:T(8,128)(2,1)} custom-call(bf16[256,2048]{1,0:T(8,128)(2,1)} %multiply_convert_fusion.3.x_ref), custom_call_target="tpu_custom_call" | custom-call | tf_op jit(solution)/shard_map/pallas_call | solution.py:347
  492.7 11.1 %fusion.24 = f32[2048,704]{0,1:T(8,128)} fusion(bf16[2048,2048]{1,0:T(8,128)(2,1)} %bitcast.159, bf16[2048,704]{0,1:T(8,128)(2,1)S(1)} %bitcast.174), kind=kOutput, calls=%fused_computation.85 | convolution fusion | flops 5905580032 | bytes 17039360 | tf_op jit(solution)/shard_map/dot_general | solution.py:472
  503.8 8.0 fusion.23
  511.9 16.1 %multiply_convert_fusion = (bf16[2048,704]{0,1:T(8,128)(2,1)}, bf16[2048,704]{0,1:T(8,128)(2,1)S(1)}, bf16[2048,704]{0,1:T(8,128)(2,1)}) fusion(f32[2048,704]{0,1:T(8,128)} %fusion.23, f32[2048,704]{0,1:T(8,128)} %fusion.24, bf16[2048,2048]{1,0:T(8,128)(2,1)} %bitcast.153, bf16[704,2048]{1,0:T(8,128)(2,1)} %all-gather.11.cloned.1.call-done), kind=kOutput, calls=%fused_computation.5 | convolution fusion | flops 5928648704 | bytes 31457280 | tf_op jit(solution)/shard_map/dot_general | solution.py:472
  528.0 1.6 copy-done.35
  529.6 10.8 %convolution_convert_fusion.5 = bf16[2048,704]{0,1:T(8,128)(2,1)} fusion(bf16[2048,704]{0,1:T(8,128)(2,1)S(1)} %get-tuple-element.36, bf16[2048,2048]{1,0:T(8,128)(2,1)} %bitcast.160), kind=kOutput, calls=%fused_computation.11 | convolution fusion | flops 5907021824 | bytes 14155776 | tf_op jit(solution)/shard_map/dot_general | solution.py:472
  540.4 3.1 copy.119
  543.6 1.9 copy.120
  545.6 1.7 copy-done.37
  547.3 11.5 %convolution_convert_fusion.4 = bf16[2048,704]{0,1:T(8,128)(2,1)} fusion(bf16[2048,704]{0,1:T(8,128)(2,1)S(1)} %copy-done.37, bf16[2048,2048]{1,0:T(8,128)(2,1)} %bitcast.161), kind=kOutput, calls=%fused_computation.10 | convolution fusion | flops 5907021824 | bytes 14155776 | tf_op jit(solution)/shard_map/dot_general | solution.py:472
  558.8 3.1 copy.122
  562.0 1.9 copy.123
  565.9 10.4 %fusion.25 = f32[2048,2048]{1,0:T(8,128)} fusion(bf16[2048,704]{0,1:T(8,128)(2,1)S(1)} %copy-done.36, bf16[2048,704]{0,1:T(8,128)(2,1)S(1)} %bitcast.177), kind=kOutput, calls=%fused_computation.86 | convolution fusion | flops 5905580032 | bytes 22544384 | tf_op jit(solution)/shard_map/dot_general | solution.py:472
  576.3 1.7 copy-done.17
  578.1 11.3 %add_convert_fusion = bf16[2048,2048]{1,0:T(8,128)(2,1)S(1)} fusion(f32[2048,2048]{1,0:T(8,128)} %fusion.25, bf16[2048,704]{0,1:T(8,128)(2,1)} %get-tuple-element.35, bf16[2048,704]{0,1:T(8,128)(2,1)S(1)} %bitcast.175), kind=kOutput, calls=%fused_computation | convolution fusion | flops 5913968640 | bytes 30932992 | tf_op jit(solution)/shard_map/dot_general | solution.py:472
  589.4 39.4 %shard_map.244 = f32[256,2048]{1,0:T(8,128)S(1)} custom-call(bf16[8,256,2048]{2,1,0:T(8,128)(2,1)S(1)} %bitcast.141), custom_call_target="tpu_custom_call" | custom-call | tf_op jit(solution)/shard_map/pallas_call | solution.py:411
  630.0 1.7 fusion.14.x_ref
  631.7 38.6 %shard_map.245 = bf16[8,256,2048]{2,1,0:T(8,128)(2,1)} custom-call(bf16[256,2048]{1,0:T(8,128)(2,1)} %fusion.14.x_ref), custom_call_target="tpu_custom_call" | custom-call | tf_op jit(solution)/shard_map/pallas_call | solution.py:347
  670.4 10.7 %fusion.26.grad_ref = f32[2048,512]{1,0:T(8,128)} fusion(bf16[2048,2048]{1,0:T(8,128)(2,1)} %bitcast.157, bf16[512,2048]{1,0:T(8,128)(2,1)} %all-gather.9.cloned.1.call-done), kind=kOutput, calls=%fused_computation.87 | convolution fusion | flops 4294967296 | bytes 14680064 | tf_op jit(solution)/shard_map/dot_general | solution.py:472
  681.1 50.6 %shard_map.246 = (bf16[2048,1664]{1,0:T(8,128)(2,1)}, f32[4,1024]{1,0:T(4,128)}, f32[1,256]{1,0:T(1,128)}, f32[2,128]{1,0:T(2,128)}) custom-call(f32[2048,1664]{1,0:T(8,128)} %fusion.22.proj_ref, f32[4,1024]{1,0:T(4,128)} %copy-done.3, f32[2,128]{1,0:T(2,128)} %copy-done.4, f32[1,256]{1,0:T(1,128)} %bitcast.144, ...), custom_call_target="tpu_custom_call" | custom-call | tf_op jit(solution)/shard_map/pallas_call | solution.py:280
  731.7 19.7 %convolution_convert_fusion.2 = bf16[2048,1664]{1,0:T(8,128)(2,1)S(1)} fusion(bf16[2048,2048]{1,0:T(8,128)(2,1)} %bitcast.156, bf16[2048,1664]{1,0:T(8,128)(2,1)} %get-tuple-element.25), kind=kOutput, calls=%fused_computation.3 | convolution fusion | flops 13962051584 | bytes 22020096 | tf_op jit(solution)/shard_map/dot_general | solution.py:472
  751.4 3.4 copy.109
  755.1 10.8 %convolution_convert_fusion.7 = bf16[512,2048]{1,0:T(8,128)(2,1)} fusion(bf16[2048,512]{1,0:T(8,128)(2,1)} %copy-done.6, bf16[2048,2048]{1,0:T(8,128)(2,1)} %bitcast.158), kind=kOutput, calls=%fused_computation.21 | convolution fusion | flops 4296015872 | bytes 12582912 | tf_op jit(solution)/shard_map/dot_general | solution.py:472
  765.9 10.5 %convolution_convert_fusion.6 = bf16[704,2048]{1,0:T(8,128)(2,1)} fusion(bf16[2048,704]{0,1:T(8,128)(2,1)} %get-tuple-element.37, bf16[2048,2048]{1,0:T(8,128)(2,1)} %bitcast.154), kind=kOutput, calls=%fused_computation.12 | convolution fusion | flops 5907021824 | bytes 14155776 | tf_op jit(solution)/shard_map/dot_general | solution.py:472
  776.5 21.0 %convolution_convert_fusion.3 = bf16[2048,2048]{1,0:T(8,128)(2,1)} fusion(bf16[2048,1664]{1,0:T(8,128)(2,1)} %get-tuple-element.25, bf16[2048,1664]{1,0:T(8,128)(2,1)} %bitcast.165), kind=kOutput, calls=%fused_computation.4 | convolution fusion | flops 13962838016 | bytes 22020096 | tf_op jit(solution)/shard_map/dot_general | solution.py:472
  797.6 3.4 copy-done.1
  801.0 39.5 %shard_map.247 = f32[256,2048]{1,0:T(8,128)S(1)} custom-call(bf16[8,256,2048]{2,1,0:T(8,128)(2,1)S(1)} %bitcast.140), custom_call_target="tpu_custom_call" | custom-call | tf_op jit(solution)/shard_map/pallas_call | solution.py:411
  843.2 52.4 %shard_map.248 = f32[32,72,128]{2,1,0:T(8,128)} custom-call(f32[72,128]{1,0:T(8,128)} %pad_bitcast_fusion.x_ref), custom_call_target="tpu_custom_call" | custom-call | tf_op jit(solution)/shard_map/pallas_call | solution.py:454
  898.9 2.0 reshape.270
  902.3 9.9 convolution_convert_fusion
  912.2 40.0 %shard_map.242 = f32[256,2048]{1,0:T(8,128)S(1)} custom-call(bf16[8,256,2048]{2,1,0:T(8,128)(2,1)S(1)} %bitcast.142), custom_call_target="tpu_custom_call" | custom-call | tf_op jit(solution)/shard_map/pallas_call | solution.py:411
  956.7 4.2 all-to-all-start.4
  961.1 12.4 %all-to-all-done.4 = bf16[8,64,704]{2,1,0:T(8,128)(2,1)} async-done(((bf16[8,64,704]{2,1,0:T(8,128)(2,1)}), bf16[8,64,704]{2,1,0:T(8,128)(2,1)}, u32[]{:S(2)}, u32[]{:S(2)}) %all-to-all-start.4) | async-done | bytes 720928 | tf_op jit(solution)/shard_map/all_to_all | solution.py:616
  973.6 4.2 all-to-all-start.5
  977.8 6.4 fusion.8
  984.2 6.2 all-to-all-done.5
  990.4 3.8 all-to-all-start.3
  995.4 2.1 convert_element_type.141
  997.6 2.5 reduce-scatter.14.cloned.1.call-done
  1000.1 2.4 convert_element_type.147
  1002.5 1.6 copy.121
  1004.8 1.6 copy.124
  1006.4 1.6 reshape.283
  1008.0 2.9 maximum_convert_fusion
  1010.9 5.7 all-to-all-done.3
  1020.2 1.9 pad_maximum_fusion
  (184 shorter events, 38.4 us)
Async XLA Ops:
  7.2 167.2 %all-gather.15.cloned.1.call-start = ((), (), s32[]{:S(2)}) async-start(), calls=%async_computation.19 | async-start | bytes 3932160 | tf_op jit(solution)/shard_map/all_gather | solution.py:535
  28.3 155.8 %all-gather.17.cloned.1.call-start = ((), (), s32[]{:S(2)}) async-start(), calls=%async_computation.20 | async-start | bytes 3932160 | tf_op jit(solution)/shard_map/all_gather | solution.py:535
  29.0 16.7 %copy-start.27 = (bf16[64,32]{0,1:T(8,128)(2,1)S(1)}, bf16[64,32]{0,1:T(8,128)(2,1)}, u32[]{:S(2)}) copy-start(bf16[64,32]{0,1:T(8,128)(2,1)} %param.19) | copy-start | bytes 12292
  29.1 17.0 %copy-start.20 = (bf16[64,12288]{1,0:T(8,128)(2,1)S(1)}, bf16[64,12288]{1,0:T(8,128)(2,1)}, u32[]{:S(2)}) copy-start(bf16[64,12288]{1,0:T(8,128)(2,1)} %param.18) | copy-start | bytes 4718596
  45.7 237.5 %all-gather.13.cloned.1.call-start = ((), (), s32[]{:S(2)}) async-start(), calls=%async_computation.18 | async-start | bytes 8519680 | tf_op jit(solution)/shard_map/all_gather | solution.py:535
  74.3 4.2 copy-start.28
  74.3 4.2 copy-start.32
  74.3 4.2 copy-start.33
  74.3 18.6 %copy-start.9 = (bf16[256,2048]{1,0:T(8,128)(2,1)S(1)}, bf16[256,2048]{1,0:T(8,128)(2,1)}, u32[]{:S(2)}) copy-start(bf16[256,2048]{1,0:T(8,128)(2,1)} %param.14) | copy-start | bytes 3145732
  76.5 18.3 %copy-start.11 = (bf16[256,2048]{1,0:T(8,128)(2,1)S(1)}, bf16[256,2048]{1,0:T(8,128)(2,1)}, u32[]{:S(2)}) copy-start(bf16[256,2048]{1,0:T(8,128)(2,1)} %param.15) | copy-start | bytes 3145732
  76.5 327.3 %all-gather.9.cloned.1.call-start = ((), (), s32[]{:S(2)}) async-start(), calls=%async_computation.11 | async-start | bytes 2621440 | tf_op jit(solution)/shard_map/all_gather | solution.py:539
  77.1 434.8 %all-gather.11.cloned.1.call-start = ((), (), s32[]{:S(2)}) async-start(), calls=%async_computation.12 | async-start | bytes 3604480 | tf_op jit(solution)/shard_map/all_gather | solution.py:542
  77.7 879.0 %reduce-scatter.10.cloned.1.call-start = ((), (), s32[]{:S(2)}) async-start(), calls=%async_computation.15 | async-start | bytes 3932160 | tf_op jit(solution)/shard_map/reduce_scatter | solution.py:615
  93.2 40.3 %copy-start.24 = (f32[256]{0:T(256)}, f32[256]{0:T(256)S(1)}, u32[]{:S(2)}) copy-start(f32[256]{0:T(256)S(1)} %add_rsqrt_fusion.1) | copy-start | bytes 3076
  94.0 39.5 %copy-start.22 = (f32[2048]{0:T(1024)}, f32[2048]{0:T(1024)S(1)}, u32[]{:S(2)}) copy-start(f32[2048]{0:T(1024)S(1)} %reshape.284) | copy-start | bytes 24580
  134.8 39.3 %copy-start.30 = (f32[16]{0:T(128)S(1)}, f32[16]{0:T(128)}, u32[]{:S(2)}) copy-start(f32[16]{0:T(128)} %param.22) | copy-start | bytes 196
  134.8 39.3 %copy-start.31 = (f32[16]{0:T(128)S(1)}, f32[16]{0:T(128)}, u32[]{:S(2)}) copy-start(f32[16]{0:T(128)} %param.21) | copy-start | bytes 196
  174.3 133.8 %copy-start.4 = (f32[2,128]{1,0:T(2,128)}, f32[2,128]{1,0:T(2,128)S(1)}, u32[]{:S(2)}) copy-start(f32[2,128]{1,0:T(2,128)S(1)} %select_maximum_fusion.decay_ref) | copy-start | bytes 3076
  174.3 133.7 %copy-start.3 = (f32[4,1024]{1,0:T(4,128)}, f32[4,1024]{1,0:T(4,128)S(1)}, u32[]{:S(2)}) copy-start(f32[4,1024]{1,0:T(4,128)S(1)} %maximum_convert_fusion.1.taps_ref) | copy-start | bytes 49156
  286.9 21.2 %copy-start.14 = (bf16[8,256,1664]{2,1,0:T(8,128)(2,1)}, bf16[8,256,1664]{2,1,0:T(8,128)(2,1)S(1)}, u32[]{:S(2)}) copy-start(bf16[8,256,1664]{2,1,0:T(8,128)(2,1)S(1)} %copy.102) | copy-start | bytes 20447236
  286.9 21.2 %copy-start.5 = (f32[256]{0:T(256)S(1)}, f32[256]{0:T(256)}, u32[]{:S(2)}) copy-start(f32[256]{0:T(256)} %param.23) | copy-start | bytes 3076
  403.8 7.1 copy-start.6
  451.3 1.3 copy-start.7
  453.9 38.8 %copy-start.16 = (bf16[88,8,8,256]{3,1,2,0:T(8,128)(2,1)S(1)}, bf16[88,8,8,256]{3,1,2,0:T(8,128)(2,1)}, u32[]{:S(2)}) copy-start(bf16[88,8,8,256]{3,1,2,0:T(8,128)(2,1)} %copy.136) | copy-start | bytes 8650756
  492.7 11.2 %copy-start.13 = (bf16[8,256,2048]{2,1,0:T(8,128)(2,1)S(1)}, bf16[8,256,2048]{2,1,0:T(8,128)(2,1)}, u32[]{:S(2)}) copy-start(bf16[8,256,2048]{2,1,0:T(8,128)(2,1)} %shard_map.241) | copy-start | bytes 25165828
  492.7 11.1 %copy-start.18 = (bf16[88,8,8,256]{3,1,2,0:T(8,128)(2,1)S(1)}, bf16[88,8,8,256]{3,1,2,0:T(8,128)(2,1)}, u32[]{:S(2)}) copy-start(bf16[88,8,8,256]{3,1,2,0:T(8,128)(2,1)} %copy.135) | copy-start | bytes 8650756
  528.0 1.6 copy-start.35
  545.5 1.8 copy-start.37
  545.5 415.6 %reduce-scatter.12.cloned.1.call-start = ((), (), s32[]{:S(2)}) async-start(), calls=%async_computation.16 | async-start | bytes 3932160 | tf_op jit(solution)/shard_map/reduce_scatter | solution.py:615
  562.0 3.0 copy-start.19
  562.0 3.9 copy-start.36
  576.3 1.8 copy-start.17
  576.3 414.1 %reduce-scatter.6.cloned.1.call-start = ((), (), s32[]{:S(2)}) async-start(), calls=%async_computation.13 | async-start | bytes 8519680 | tf_op jit(solution)/shard_map/reduce_scatter | solution.py:615
  589.3 39.4 %copy-start.8 = (f32[256,2048]{1,0:T(8,128)S(1)}, f32[256,2048]{1,0:T(8,128)}, u32[]{:S(2)}) copy-start(f32[256,2048]{1,0:T(8,128)} %copy-done.7) | copy-start | bytes 6291460
  628.8 1.2 copy-start.12
  754.8 240.6 %reduce-scatter.8.cloned.1.call-start = ((), (), s32[]{:S(2)}) async-start(), calls=%async_computation.14 | async-start | bytes 2621440 | tf_op jit(solution)/shard_map/reduce_scatter | solution.py:611
  765.9 234.2 %reduce-scatter.14.cloned.1.call-start = ((), (), s32[]{:S(2)}) async-start(), calls=%async_computation.17 | async-start | bytes 3604480 | tf_op jit(solution)/shard_map/reduce_scatter | solution.py:611
  776.5 21.0 %copy-start.34 = (f32[2,128]{1,0:T(2,128)S(1)}, f32[2,128]{1,0:T(2,128)}, u32[]{:S(2)}) copy-start(f32[2,128]{1,0:T(2,128)} %get-tuple-element.28) | copy-start | bytes 3076
  797.6 3.4 copy-start.1
  801.0 40.8 %copy-start.10 = (bf16[256,2048]{1,0:T(8,128)(2,1)S(1)}, bf16[256,2048]{1,0:T(8,128)(2,1)}, u32[]{:S(2)}) copy-start(bf16[256,2048]{1,0:T(8,128)(2,1)} %param.14) | copy-start | bytes 3145732
  801.0 40.8 %copy-start.23 = (f32[2048]{0:T(1024)S(1)}, f32[2048]{0:T(1024)}, u32[]{:S(2)}) copy-start(f32[2048]{0:T(1024)} %copy-done.22) | copy-start | bytes 24580
  801.0 40.8 %copy-start.25 = (f32[256]{0:T(256)S(1)}, f32[256]{0:T(256)}, u32[]{:S(2)}) copy-start(f32[256]{0:T(256)} %copy-done.24) | copy-start | bytes 3076
  840.4 1.3 copy-start
  841.8 0.7 copy-start.29
  841.8 0.7 copy-start.26
  897.1 1.0 copy-start.15
  902.3 9.9 copy-start.21
  912.2 43.0 %slice-start = ((f32[8,4100]{1,0:T(8,128)}), f32[8,4]{1,0:T(8,128)S(1)}, s32[]{:S(2)}) async-start(f32[8,4100]{1,0:T(8,128)} %copy-done.21), calls=%async_computation.21 | async-start | bytes 8192 | tf_op jit(solution)/shard_map/slice | solution.py:659
  952.3 1.3 copy-start.2
  956.7 16.8 %all-to-all-start.4 = ((bf16[8,64,704]{2,1,0:T(8,128)(2,1)}), bf16[8,64,704]{2,1,0:T(8,128)(2,1)}, u32[]{:S(2)}, u32[]{:S(2)}) async-start(bf16[8,64,704]{2,1,0:T(8,128)(2,1)} %bitcast.190), calls=%async_computation.7 | async-start | bytes 1572864 | tf_op jit(solution)/shard_map/all_to_all | solution.py:616
  973.6 16.8 %all-to-all-start.5 = ((bf16[8,64,704]{2,1,0:T(8,128)(2,1)}), bf16[8,64,704]{2,1,0:T(8,128)(2,1)}, u32[]{:S(2)}, u32[]{:S(2)}) async-start(bf16[8,64,704]{2,1,0:T(8,128)(2,1)} %bitcast.189), calls=%async_computation.9 | async-start | bytes 1572864 | tf_op jit(solution)/shard_map/all_to_all | solution.py:616
  990.4 26.2 %all-to-all-start.3 = ((bf16[8,64,1664]{2,1,0:T(8,128)(2,1)}), bf16[8,64,1664]{2,1,0:T(8,128)(2,1)S(1)}, u32[]{:S(2)}, u32[]{:S(2)}) async-start(bf16[8,64,1664]{2,1,0:T(8,128)(2,1)} %bitcast.184), calls=%async_computation.4 | async-start | bytes 3407872 | tf_op jit(solution)/shard_map/all_to_all | solution.py:616
Sparse Core Ops, SparseCore 0:
  28.4 65.6 all-gather.14
  96.3 62.0 all-gather.16
  160.5 122.5 all-gather.12
  284.6 44.1 all-gather.8
  330.2 57.8 all-gather.10
  545.6 57.5 reduce-scatter.9
  606.1 60.2 reduce-scatter.11
  755.0 133.7 reduce-scatter.5
  891.1 50.6 reduce-scatter.7
  944.6 55.4 reduce-scatter.13

commit v2 on v1

--- a/solution.py
+++ b/solution.py
@@ -13,6 +13,7 @@
 EPSILON = 1e-06
 DK = 128
 DV = 256
+BASE = 8
 NN = (((1,), (0,)), ((), ()))
 NT = (((1,), (1,)), ((), ()))
 TN = (((0,), (0,)), ((), ()))
@@ -72,25 +73,28 @@
     return jnp.maximum(v, 0.0) + jnp.log1p(jnp.exp(-jnp.abs(v)))
 
 
-def unit_inverse(lower, row_ids, col_ids):
-    length = lower.shape[0]
-    eye = jnp.where(row_ids == col_ids, 1.0, 0.0)
-    size = 8
-    base = jnp.where(row_ids // size == col_ids // size, lower, 0.0)
-    square = dot6(base, base)
-    inverse = dot6(eye - base, eye + square)
-    inverse = inverse + dot6(inverse, dot6(square, square))
+def unit_inverses(lowers, row_ids, col_ids):
+    length = lowers[0].shape[0]
+    size = BASE
+    same = row_ids // size == col_ids // size
+    pick = jnp.where(col_ids[:, :128] == lax.rem(row_ids[:, :128], size), 1.0, 0.0).astype(BF16)
+    lanes = lax.broadcasted_iota(jnp.int32, (length // size, size, 128), 2)
+    places = lax.broadcasted_iota(jnp.int32, (length // size, size, 128), 1)
+    compact = [dot3(jnp.where(same, lower, 0.0), pick).reshape(length // size, size, 128) for lower in lowers]
+    solved = [jnp.where(lanes == places, 1.0, 0.0) for _ in lowers]
+    for j in range(size - 1):
+        solved = [x - a[:, :, j : j + 1] * x[:, j : j + 1, :] for a, x in zip(compact, solved)]
+    inverses = [jnp.where(same, dot3(x.reshape(length, 128), pick, NT), 0.0) for x in solved]
     while size < length:
         wide = 2 * size
-        off = jnp.where(
-            (row_ids // wide == col_ids // wide) & (row_ids // size != col_ids // size), lower, 0.0
-        )
-        inverse = inverse - dot3(inverse, dot3(off, inverse))
+        off = (row_ids // wide == col_ids // wide) & (row_ids // size != col_ids // size)
+        inner = [dot3(jnp.where(off, lower, 0.0), inverse) for lower, inverse in zip(lowers, inverses)]
+        inverses = [inverse - dot3(inverse, x) for inverse, x in zip(inverses, inner)]
         size = wide
-    return inverse
-
-
-def common(proj, taps, decay, heads, length):
+    return inverses
+
+
+def common(proj, decay, heads, length):
     rows = lax.broadcasted_iota(jnp.int32, (length, 1), 0)
     row_ids = lax.broadcasted_iota(jnp.int32, (length, length), 0)
     col_ids = lax.broadcasted_iota(jnp.int32, (length, length), 1)
@@ -103,7 +107,7 @@
     return rows, row_ids, col_ids, raw, lanes, shifted, rate, beta, cumulated, cumulated.T
 
 
-def head_parts(h, proj, taps, heads, rows):
+def head_parts(h, heads):
     key = slice(h * DK, (h + 1) * DK)
     keyk = slice((heads + h) * DK, (heads + h + 1) * DK)
     val = slice(heads * DV + h * DV, heads * DV + (h + 1) * DV)
@@ -113,34 +117,35 @@
 
 def mixer_forward_kernel(heads, proj_ref, taps_ref, decay_ref, gain_ref, mixed_ref, inv_ref, solved_ref, core_ref):
     length = proj_ref.shape[0]
-    taps_all = taps_ref[...]
     decay = decay_ref[...]
     gain = gain_ref[...]
     rows, row_ids, col_ids, raw, lanes, shifted, rate, beta, cumulated, cum_t = common(
-        proj_ref[...], taps_all, decay, heads, length
+        proj_ref[...], decay, heads, length
     )
-    for h in range(heads):
-        qs, ks, vs, gs = head_parts(h, None, None, heads, rows)
-
-        def active(cols):
-            y = conv(proj_ref[:, cols], taps_ref[:, cols], rows)
-            return y * sigmoid(y)
-
-        q = active(qs)
-        q = (q * lax.rsqrt(jnp.sum(q * q, axis=-1, keepdims=True) + EPSILON) * DK ** (-0.5)).astype(BF16)
+    def active(cols):
+        y = conv(proj_ref[:, cols], taps_ref[:, cols], rows)
+        return y * sigmoid(y)
+
+    parts = [head_parts(h, heads) for h in range(heads)]
+    queries, keys, values, growths, betas, lowers = [], [], [], [], [], []
+    for h, (qs, ks, vs, gs) in enumerate(parts):
         k = active(ks)
         k = (k * lax.rsqrt(jnp.sum(k * k, axis=-1, keepdims=True) + EPSILON)).astype(BF16)
-        v = active(vs).astype(BF16)
         beta_h = beta[:, heads + h : heads + h + 1]
         gap = cumulated[:, h : h + 1] - cum_t[h : h + 1, :]
         growth = jnp.where(row_ids >= col_ids, jnp.exp(jnp.where(row_ids >= col_ids, gap, 0.0)), 0.0)
-        gram = dot1(k, k, NT)
-        lower = jnp.where(row_ids > col_ids, growth * gram * beta_h, 0.0)
-        inverse = unit_inverse(lower, row_ids, col_ids)
-        solved = dot3(inverse, beta_h * v.astype(F32))
-        weights = growth * dot1(q, k, NT)
-        core = dot3(weights, solved)
-        inv_ref[h] = inverse
+        keys.append(k)
+        growths.append(growth)
+        betas.append(beta_h)
+        lowers.append(jnp.where(row_ids > col_ids, growth * dot1(k, k, NT) * beta_h, 0.0))
+    inverses = unit_inverses(lowers, row_ids, col_ids)
+    for h, (qs, ks, vs, gs) in enumerate(parts):
+        q = active(qs)
+        q = (q * lax.rsqrt(jnp.sum(q * q, axis=-1, keepdims=True) + EPSILON) * DK ** (-0.5)).astype(BF16)
+        v = active(vs).astype(BF16)
+        inv_ref[h] = inverses[h]
+        solved = dot3(inverses[h], betas[h] * v.astype(F32))
+        core = dot3(growths[h] * dot1(q, keys[h], NT), solved)
         solved_ref[:, h * DV : (h + 1) * DV] = solved
         core_ref[:, h * DV : (h + 1) * DV] = core
         gate = proj_ref[:, gs]
@@ -165,7 +170,7 @@
             jax.ShapeDtypeStruct((tokens, hv), F32),
             jax.ShapeDtypeStruct((tokens, hv), F32),
         ],
-        compiler_params=pltpu.CompilerParams(vmem_limit_bytes=48 << 20),
+        cost_estimate=busy(55), compiler_params=pltpu.CompilerParams(vmem_limit_bytes=48 << 20),
     )(proj, taps, decay, gain)
 
 
@@ -178,7 +183,7 @@
     decay = decay_ref[...]
     gain = gain_ref[...]
     rows, row_ids, col_ids, raw, lanes, shifted, rate, beta, cumulated, cum_t = common(
-        proj_ref[...], None, decay, heads, length
+        proj_ref[...], decay, heads, length
     )
     within = row_ids >= col_ids
     strict = row_ids > col_ids
@@ -192,7 +197,7 @@
     cum_grad = jnp.zeros(raw.shape, F32)
     beta_grad = jnp.zeros(raw.shape, F32)
     for h in range(heads):
-        qs, ks, vs, gs = head_parts(h, None, None, heads, rows)
+        qs, ks, vs, gs = head_parts(h, heads)
         hs = slice(h * DV, (h + 1) * DV)
 
         def active(cols):
@@ -289,8 +294,12 @@
             jax.ShapeDtypeStruct(gain.shape, F32),
             jax.ShapeDtypeStruct(decay.shape, F32),
         ],
-        compiler_params=pltpu.CompilerParams(vmem_limit_bytes=56 << 20),
+        cost_estimate=busy(50), compiler_params=pltpu.CompilerParams(vmem_limit_bytes=56 << 20),
     )(proj, taps, decay, gain, inverse, solved, core, grad)
+
+
+def busy(us):
+    return pl.CostEstimate(flops=us * 1_000_000_000, bytes_accessed=0, transcendentals=0)
 
 
 def _place(n_dp):
@@ -347,7 +356,7 @@
     return pl.pallas_call(kernel, out_shape=jax.ShapeDtypeStruct((8,rows,cols),x.dtype),
         in_specs=[pl.BlockSpec(memory_space=pl.ANY)], out_specs=pl.BlockSpec(memory_space=pl.ANY),
         scratch_shapes=[D, D((2,chunks)), D((2,chunks)), D((chunks,)), D((chunks,)), D((4,chunks)), D((4,chunks))],
-        compiler_params=pltpu.CompilerParams(collective_id=cid, has_side_effects=True))(x)
+        cost_estimate=busy(40), compiler_params=pltpu.CompilerParams(collective_id=cid, has_side_effects=True))(x)
 
 def rs_square(x, cid, chunks=4):
     _, rows, cols = x.shape
@@ -411,7 +420,292 @@
     return pl.pallas_call(kernel, out_shape=jax.ShapeDtypeStruct((rows,cols),F32),
         in_specs=[pl.BlockSpec(memory_space=pl.ANY)], out_specs=pl.BlockSpec(memory_space=pltpu.VMEM),
         scratch_shapes=[V(4),V(4),V(3),V(3), D((4,chunks)), D((4,chunks)), D((4,chunks)), D((3,chunks)), D((3,chunks))],
-        compiler_params=pltpu.CompilerParams(collective_id=cid, has_side_effects=True, vmem_limit_bytes=40<<20))(x)
+        cost_estimate=busy(40), compiler_params=pltpu.CompilerParams(collective_id=cid, has_side_effects=True, vmem_limit_bytes=40<<20))(x)
+
+def begin(weight, decays, ups, tokens, cotangent, small, bounds, n_z, cid):
+    own = weight.shape[0]
+    cols = bounds[-1] + 128
+    units = ups.shape[2]
+    rows, width = tokens.shape
+    count = 8 * n_z
+    chunks = 2
+    part = rows // chunks
+
+    def kernel(
+        w_ref, dec_ref, u_ref, t_ref, c_ref, small_ref, w_out, u_out, n_out, c_out, small_out,
+        toks, lsem, a_send, a_recv, g_send, g_recv, up_send, up_recv, down_send, down_recv,
+        small_send, small_recv, x_send, x_recv, d_send, d_recv, f_send, f_recv,
+    ):
+        me, z, core, cx, cy = _place(8)
+        flat = me * n_z + z
+        bar = pltpu.get_barrier_semaphore()
+
+        def dev(dx, dy, c):
+            return 2 * (2 * lax.rem(cy + dy, 2) + lax.rem(cx + dx, 2)) + c
+
+        sib = dev(0, 0, 1 - core)
+
+        def partner(o):
+            return dev(o // 4, lax.rem(o // 2, 2), lax.rem(core + o, 2))
+
+        def anyone(o):
+            other = lax.rem(flat + o, count)
+            return (other // n_z, lax.rem(other, n_z))
+
+        def remote(src, dst, send, recv, device):
+            return pltpu.make_async_remote_copy(src, dst, send, recv, device_id=device, device_id_type=MESH)
+
+        def loop(first, last, body):
+            def step(o, _):
+                body(o)
+                return 0
+
+            lax.fori_loop(first, last, step, 0)
+
+        def sections(q):
+            for first, last in zip(bounds[:-1], bounds[1:]):
+                size = last - first
+                at = pl.multiple_of(8 * first + q * size, 128)
+                yield w_ref.at[:, pl.ds(at, size)], w_out.at[me, z, :, pl.ds(first, size)]
+            yield dec_ref.at[q], w_out.at[me, z, :, pl.ds(bounds[-1], 128)]
+
+        def send_piece(o):
+            q = partner(o)
+            for src, dst in sections(q):
+                remote(src, dst, a_send.at[o - 1], a_recv.at[o - 1], (q, z)).start()
+
+        def landed(o):
+            at = w_out.at[partner(o), z]
+            return remote(at, at, a_send.at[o - 1], a_recv.at[o - 1], (sib, z))
+
+        def up(t, o):
+            at = w_out.at[partner(o), z - t]
+            return remote(at, at, up_send.at[t, o], up_recv.at[t, o], (me, z + 1))
+
+        def down(t, o):
+            at = w_out.at[partner(o), z + t]
+            return remote(at, at, down_send.at[t, o], down_recv.at[t, o], (me, z - 1))
+
+        def pass_on(t, o):
+            if t > 0:
+
+                @pl.when(z >= t)
+                def _():
+                    at = w_out.at[partner(o), z - t]
+                    remote(at, at, up_send.at[t - 1, o], up_recv.at[t - 1, o], (sib, z)).wait_recv()
+
+                @pl.when(z + t < n_z)
+                def _():
+                    at = w_out.at[partner(o), z + t]
+                    remote(at, at, down_send.at[t - 1, o], down_recv.at[t - 1, o], (sib, z)).wait_recv()
+
+            if t < n_z - 1:
+
+                @pl.when((z >= t) & (z < n_z - 1))
+                def _():
+                    up(t, o).start()
+
+                @pl.when((z + t < n_z) & (z > 0))
+                def _():
+                    down(t, o).start()
+
+        def sent(t, o):
+            @pl.when((z >= t) & (z < n_z - 1))
+            def _():
+                up(t, o).wait_send()
+
+            @pl.when((z + t < n_z) & (z > 0))
+            def _():
+                down(t, o).wait_send()
+
+        def unit_piece(o):
+            q = partner(o)
+            return remote(u_ref.at[q], u_out.at[me], g_send.at[o - 1], g_recv.at[o - 1], (q, z))
+
+        def tiny(o):
+            return remote(small_ref, small_out.at[flat], small_send.at[o - 1], small_recv.at[o - 1], anyone(o))
+
+        near = (dev(1, 0, core), dev(0, 1, core))
+        source, other, across = dev(1 - core, core, core), dev(core, 1 - core, core), dev(1, 1, core)
+
+        def gather(i, ref, out):
+            def at(q, c):
+                return out.at[q, pl.ds(c * part, part)]
+
+            def mine(c):
+                return ref.at[pl.ds(c * part, part)]
+
+            def first(k, c):
+                return remote(mine(c), at(me, c), x_send.at[i, k, c], x_recv.at[i, k, c], (near[k], z))
+
+            def twin(k, q, c):
+                src = mine(c) if k == 0 else at(q, c)
+                return remote(src, at(q, c), f_send.at[i, k, c], f_recv.at[i, k, c], (sib, z))
+
+            def second(c):
+                return remote(at(source, c), at(source, c), d_send.at[i, c], d_recv.at[i, c], (other, z))
+
+            def keep():
+                return pltpu.make_async_copy(ref, out.at[me], lsem.at[i])
+
+            def begin_():
+                keep().start()
+                for c in range(chunks):
+                    for k in range(2):
+                        first(k, c).start()
+                for c in range(chunks):
+                    twin(0, me, c).start()
+
+            def forward():
+                for c in range(chunks):
+                    remote(mine(c), at(source, c), x_send.at[i, core, c], x_recv.at[i, core, c], (sib, z)).wait_recv()
+                    second(c).start()
+                    twin(1, source, c).start()
+                    remote(
+                        mine(c), at(other, c), x_send.at[i, 1 - core, c], x_recv.at[i, 1 - core, c], (sib, z)
+                    ).wait_recv()
+                    twin(2, other, c).start()
+
+            def last():
+                for c in range(chunks):
+                    remote(at(across, c), at(across, c), d_send.at[i, c], d_recv.at[i, c], (other, z)).wait_recv()
+                    twin(3, across, c).start()
+
+            def finish():
+                keep().wait()
+                theirs = (sib, dev(core, 1 - core, 1 - core), dev(1 - core, core, 1 - core), dev(1, 1, 1 - core))
+                for c in range(chunks):
+                    for k in range(4):
+                        remote(
+                            at(theirs[k], c), at(theirs[k], c), f_send.at[i, k, c], f_recv.at[i, k, c], (sib, z)
+                        ).wait_recv()
+
+            def close():
+                for c in range(chunks):
+                    for k in range(2):
+                        first(k, c).wait_send()
+                    second(c).wait_send()
+                    for k, q in enumerate((me, source, other, across)):
+                        twin(k, q, c).wait_send()
+
+            return begin_, forward, last, finish, close
+
+        tok_begin, tok_forward, tok_last, tok_finish, tok_close = gather(0, t_ref, toks)
+        cot_begin, cot_forward, cot_last, cot_finish, cot_close = gather(1, c_ref, c_out)
+
+        loop(1, count, lambda o: pl.semaphore_signal(bar, inc=1, device_id=anyone(o), device_id_type=MESH))
+        for src, dst in sections(me):
+            pltpu.make_async_copy(src, dst, lsem.at[2]).start()
+        keep_u = pltpu.make_async_copy(u_ref.at[me], u_out.at[me], lsem.at[3])
+        keep_s = pltpu.make_async_copy(small_ref, small_out.at[flat], lsem.at[4])
+        keep_u.start()
+        keep_s.start()
+        pl.semaphore_wait(bar, count - 1)
+
+        loop(1, 8, send_piece)
+        pltpu.make_async_copy(w_out.at[me, z], w_out.at[me, z], lsem.at[2]).wait()
+        pass_on(0, 0)
+        loop(1, count, lambda o: tiny(o).start())
+
+        def first_leg(o):
+            landed(o).wait_recv()
+            pass_on(0, o)
+
+        tok_begin()
+        loop(1, 8, first_leg)
+        loop(0, 8, lambda o: pass_on(1, o))
+        tok_forward()
+        cot_begin()
+        loop(1, 8, lambda o: unit_piece(o).start())
+        loop(0, 4, lambda o: pass_on(2, o))
+        tok_last()
+        tok_finish()
+        keep_s.wait()
+        loop(1, count, lambda o: tiny(o).wait_recv())
+
+        lanes = lax.broadcasted_iota(jnp.int32, (1, 128), 1)
+        per = 128 // own
+        blocks = []
+        for m in range(width // 128):
+            block = small_out[m * per, 0:1, :].astype(F32)
+            for i in range(1, per):
+                block = jnp.where(lanes >= i * own, small_out[m * per + i, 0:1, :].astype(F32), block)
+            blocks.append(block)
+        gain = jnp.concatenate(blocks, axis=1)
+        step = 32
+
+        def norm_rows(o):
+            def some(r, _):
+                sl = pl.ds(r * step, step)
+                v = toks[o, sl].astype(F32)
+                n_out[o, sl] = (
+                    v * lax.rsqrt(jnp.mean(v * v, axis=-1, keepdims=True) + EPSILON) * gain
+                ).astype(BF16)
+                return 0
+
+            lax.fori_loop(0, rows // step, some, 0)
+
+        def third_leg(o):
+            pass_on(2, o)
+            norm_rows(o - 4)
+            norm_rows(o)
+
+        loop(4, 8, third_leg)
+        cot_forward()
+        loop(0, 4, lambda o: pass_on(3, o))
+        cot_last()
+        loop(4, 8, lambda o: pass_on(3, o))
+        cot_finish()
+        for t in range(n_z - 1):
+            loop(0, 8, functools.partial(sent, t))
+        loop(1, 8, lambda o: landed(o).wait_send())
+        loop(1, 8, lambda o: unit_piece(o).wait())
+        loop(1, count, lambda o: tiny(o).wait_send())
+        keep_u.wait()
+        tok_close()
+        cot_close()
+
+    dma = pltpu.SemaphoreType.DMA
+    anywhere, vmem = pl.BlockSpec(memory_space=pl.ANY), pl.BlockSpec(memory_space=pltpu.VMEM)
+    plane = jax.ShapeDtypeStruct((8, rows, width), BF16)
+    legs = n_z - 1
+    return pl.pallas_call(
+        kernel,
+        out_shape=[
+            jax.ShapeDtypeStruct((8, n_z, own, cols), BF16),
+            jax.ShapeDtypeStruct((8, own, units), BF16),
+            plane,
+            plane,
+            jax.ShapeDtypeStruct((count,) + small.shape, BF16),
+        ],
+        in_specs=[anywhere] * 6,
+        out_specs=[anywhere, anywhere, vmem, anywhere, vmem],
+        scratch_shapes=[
+            pltpu.VMEM((8, rows, width), BF16),
+            dma((5,)),
+            dma((7,)),
+            dma((7,)),
+            dma((7,)),
+            dma((7,)),
+            dma((legs, 8)),
+            dma((legs, 8)),
+            dma((legs, 8)),
+            dma((legs, 8)),
+            dma((count - 1,)),
+            dma((count - 1,)),
+            dma((2, 2, chunks)),
+            dma((2, 2, chunks)),
+            dma((2, chunks)),
+            dma((2, chunks)),
+            dma((2, 4, chunks)),
+            dma((2, 4, chunks)),
+        ],
+        cost_estimate=busy(150),
+        compiler_params=pltpu.CompilerParams(
+            collective_id=cid, has_side_effects=True, vmem_limit_bytes=32 << 20
+        ),
+    )(weight, decays, ups, tokens, cotangent, small)
+
 
 def gather_small(x, n_dp, n_z, cid):
     rows, cols = x.shape
@@ -457,6 +751,7 @@
         in_specs=[pl.BlockSpec(memory_space=pl.ANY)],
         out_specs=pl.BlockSpec(memory_space=pl.ANY),
         scratch_shapes=[dma, dma((count - 1,)), dma((count - 1,))],
+        cost_estimate=busy(15),
         compiler_params=pltpu.CompilerParams(collective_id=cid, has_side_effects=True),
     )(x)
 
@@ -500,7 +795,7 @@
     units = upgate_weight.shape[1] // (2 * n_dp)
     key, value = heads * DK, heads * DV
     cols = 2 * key + 2 * value + 128
-    square = n_dp == 8
+    square = n_dp == 8 and n_z == 4
     here = lax.axis_index("dp")
     flat = here * n_z + lax.axis_index("fsdp")
 
@@ -517,39 +812,82 @@
     def by_dp(a, parts):
         return a.reshape(a.shape[0], n_dp, parts)
 
-    pieces = (
-        by_dp(input_weight[:, : n_dp * key], key),
-        by_dp(input_weight[:, n_dp * key : 2 * n_dp * key], key),
-        by_dp(input_weight[:, 2 * n_dp * key : 2 * n_dp * key + n_dp * value], value),
-        by_dp(input_weight[:, 2 * n_dp * key + n_dp * value :], value),
-        by_dp(decay_weight[:, :all_heads], heads),
-        by_dp(decay_weight[:, all_heads:], heads),
-        jnp.zeros((own_d, n_dp, 128 - 2 * heads), BF16),
-    )
-    in_mine = jnp.concatenate(pieces, axis=2).transpose(1, 0, 2)
-    gate_mine = by_dp(upgate_weight[:, : n_dp * units], units).transpose(1, 0, 2)
-    up_mine = by_dp(upgate_weight[:, n_dp * units :], units).transpose(1, 0, 2)
+    main = units // 128 * 128
+    bounds = (0, key, 2 * key, 2 * key + value, 2 * key + 2 * value)
+    gates = by_dp(upgate_weight[:, : n_dp * units], units)
+    ups = by_dp(upgate_weight[:, n_dp * units :], units)
+    up_mine = jnp.concatenate(
+        [gates[:, :, :main], ups[:, :, :main], gates[:, :, main:], ups[:, :, main:]], axis=2
+    ).transpose(1, 0, 2)
+    decay_cols = jnp.concatenate(
+        [
+            by_dp(decay_weight[:, :all_heads], heads),
+            by_dp(decay_weight[:, all_heads:], heads),
+            jnp.zeros((own_d, n_dp, 128 - 2 * heads), BF16),
+        ],
+        axis=2,
+    ).transpose(1, 0, 2)
 
     def whole_rows(a):
-        a = lax.all_to_all(a, "dp", 0, 0, tiled=True)
         a = lax.all_gather(a[:, None], "fsdp", axis=1, tiled=True)
         return a.reshape(width, a.shape[-1])
 
-    in_full = whole_rows(in_mine)
+    conv_size = taps * own_conv
+    inputs = tokens.astype(F32)
+    first_root = lax.rsqrt(jnp.mean(inputs * inputs, axis=-1, keepdims=True) + EPSILON)
+    if square:
+        small = jnp.concatenate(
+            [
+                jnp.tile(norm_first, 128 // own_d)[None],
+                jnp.tile(norm_second, 128 // own_d)[None],
+                jnp.broadcast_to(group_ids.astype(BF16)[:, None], (1, 128)),
+                jnp.zeros((5, 128), BF16),
+                conv_weight.reshape(8, 128),
+            ],
+            axis=0,
+        )
+        in_full, up_plane, normed_all, cot_all, small = begin(
+            input_weight, decay_cols, up_mine, tokens, cotangent, small, bounds, n_z, 1
+        )
+        in_full = in_full.reshape(width, cols)
+        normed_all = normed_all.reshape(n_dp * rows, width)
+        cot_all = cot_all.reshape(n_dp * rows, width)
+        conv_full = small[:, 8:].reshape(count, taps, own_conv)
+        first_full = small[:, 0, :own_d]
+        second_full = small[:, 1, :own_d]
+        every_id = small[:, 2, 0]
+        output_weight, down_weight, up_plane = lax.optimization_barrier(
+            (output_weight, down_weight, up_plane, small)
+        )[:3]
+    else:
+        in_mine = [
+            by_dp(input_weight[:, n_dp * a : n_dp * b], b - a).transpose(1, 0, 2)
+            for a, b in zip(bounds[:-1], bounds[1:])
+        ]
+        in_mine = jnp.concatenate(in_mine + [decay_cols], axis=2)
+        in_full = whole_rows(lax.all_to_all(in_mine, "dp", 0, 0, tiled=True))
+        up_plane = lax.all_to_all(up_mine, "dp", 0, 0, tiled=True)
+        small = gather_small(
+            pack((conv_weight, norm_first, norm_second, group_ids.astype(BF16)), 16), n_dp, n_z, 1
+        ).reshape(count, -1)
+        conv_full = small[:, :conv_size].reshape(count, taps, own_conv)
+        first_full = small[:, conv_size : conv_size + own_d]
+        second_full = small[:, conv_size + own_d : conv_size + 2 * own_d]
+        every_id = small[:, conv_size + 2 * own_d]
     out_full = lax.all_gather(output_weight, "fsdp", axis=0, tiled=True)
-    gate_full = whole_rows(gate_mine)
-    up_full = whole_rows(up_mine)
+    up_full = whole_rows(up_plane)
     down_full = lax.all_gather(down_weight, "fsdp", axis=0, tiled=True)
-
-    small = gather_small(
-        pack((conv_weight, norm_first, norm_second, group_ids.astype(BF16)), 16), n_dp, n_z, 1
-    ).reshape(count, -1)
-    conv_size = taps * own_conv
-    conv_full = small[:, :conv_size].reshape(count, taps, own_conv).transpose(1, 0, 2).reshape(taps, -1)
-    first_full = small[:, conv_size : conv_size + own_d].reshape(1, width).astype(F32)
-    second_full = small[:, conv_size + own_d : conv_size + 2 * own_d].reshape(1, width).astype(F32)
-    every_id = small[:, conv_size + 2 * own_d].astype(jnp.int32)
-    scale = 1.0 / jnp.sum((every_id == group_ids[0]).astype(F32))
+    conv_full = conv_full.transpose(1, 0, 2).reshape(taps, -1)
+    first_full = first_full.reshape(1, width).astype(F32)
+    second_full = second_full.reshape(1, width).astype(F32)
+    every_id = every_id.astype(jnp.int32)
+    scales = 1.0 / jnp.sum((every_id[:, None] == every_id[None, :]).astype(F32), axis=0).reshape(n_dp, n_z)
+    scales = lax.dynamic_index_in_dim(scales, lax.axis_index("fsdp"), axis=1, keepdims=False)
+    seed = cotangent.astype(F32) * lax.dynamic_index_in_dim(scales, here, axis=0, keepdims=False)
+    scales = jnp.broadcast_to(scales[:, None, None], (n_dp, rows, 1)).reshape(n_dp * rows, 1)
+    if not square:
+        normed_all = spread((inputs * first_root * first_full).astype(BF16), 2)
+        cot_all = spread(cotangent, 3)
 
     def conv_columns(start, size):
         return lax.dynamic_slice_in_dim(conv_full, start + here * size, size, axis=1)
@@ -568,27 +906,32 @@
     )
     gain = output_gain[None, :]
 
-    inputs = tokens.astype(F32)
-    first_root = lax.rsqrt(jnp.mean(inputs * inputs, axis=-1, keepdims=True) + EPSILON)
-    normed_all = spread((inputs * first_root * first_full).astype(BF16), 2)
-    seed = cotangent.astype(F32) * scale
-    seed_all = spread(seed.astype(BF16), 3)
     projected = dot(normed_all, in_full)
     mixed, inverse, solved, core = mixer_forward(projected, conv_mine, decay_mine, gain, heads, rows)
     middle = inputs + total(dot(mixed, out_full, out=BF16), 4)
     second_root = lax.rsqrt(jnp.mean(middle * middle, axis=-1, keepdims=True) + EPSILON)
     second_all = spread((middle * second_root * second_full).astype(BF16), 5)
-    gate_part = dot(second_all, gate_full)
-    up_part = dot(second_all, up_full)
-    gate_sig = jax.nn.sigmoid(gate_part)
-    hidden = (gate_part * gate_sig * up_part).astype(BF16)
-    hidden_grad = dot(seed_all, down_full, NT)
-    gate_low = (hidden_grad * up_part * gate_sig * (1.0 + gate_part * (1.0 - gate_sig))).astype(BF16)
-    up_low = (hidden_grad * gate_part * gate_sig).astype(BF16)
-
-    back_two = (dot(gate_low, gate_full, NT) + dot(up_low, up_full, NT)).astype(BF16)
+    upgate = dot(second_all, up_full)
+
+    def halves_of(a):
+        return (a[:, :main], a[:, main : 2 * main]), (a[:, 2 * main : main + units], a[:, main + units :])
+
+    acts = [(g, u, jax.nn.sigmoid(g)) for g, u in halves_of(upgate)]
+    hidden = jnp.concatenate([g * s * u for g, u, s in acts], axis=1)
+    hidden_seed = (hidden * scales).astype(BF16)
+    hidden = hidden.astype(BF16)
+
+    down_grad = dot(hidden_seed, cot_all, TN, out=BF16)
+    down_grad, cot_all = lax.optimization_barrier((down_grad, cot_all))
+    hidden_grad = dot(cot_all, down_full, NT) * scales
+    parts = list(zip(acts, (hidden_grad[:, :main], hidden_grad[:, main:])))
+    upgate_low = jnp.concatenate(
+        [x for (g, u, s), grad in parts for x in (grad * u * s * (1.0 + g * (1.0 - s)), grad * g * s)], axis=1
+    ).astype(BF16)
+    back_two = dot(upgate_low, up_full, NT, out=BF16)
+    upgate_grad = dot(second_all, upgate_low, TN, out=BF16)
+    back_two, down_grad, upgate_grad = lax.optimization_barrier((back_two, down_grad, upgate_grad))
     normed_two_grad = total(back_two, 6)
-    result = middle + total(dot(hidden, down_full, out=BF16), 7)
 
     def norm_back(v, root, gain_row, grad):
         hat = v * root
@@ -598,31 +941,55 @@
 
     middle_part, second_grad = norm_back(middle, second_root, second_full, normed_two_grad)
     middle_grad = seed + middle_part
-    middle_all = spread(middle_grad.astype(BF16), 8)
+
+    def owned_rows(a):
+        return lax.psum_scatter(a, "fsdp", scatter_dimension=0, tiled=True)
+
+    def owned_parts(a):
+        a = a.reshape(n_dp, n_z, own_d, a.shape[-1]).transpose(1, 0, 2, 3)
+        return lax.psum_scatter(a.reshape(width, -1), "fsdp", scatter_dimension=0, tiled=True)
+
+    def to_owners(a):
+        a = lax.all_to_all(a.reshape(n_dp, own_d, -1), "dp", 0, 0, tiled=True)
+        return a.transpose(1, 0, 2).astype(F32)
+
+    down_total = owned_rows(down_grad)
+    middle_low, down_total = lax.optimization_barrier((middle_grad.astype(BF16), down_total))
+    middle_all = spread(middle_low, 8)
+    upgate_sum = owned_parts(upgate_grad)
     mixed_grad = dot(middle_all, out_full, NT)
+    output_grad = dot(mixed, middle_all, TN, out=BF16)
+    mixed_grad, output_grad = lax.optimization_barrier((mixed_grad, output_grad))
     projected_low, conv_grad, gain_grad, decay_grad = mixer_backward(
         projected, conv_mine, decay_mine, gain, inverse, solved, core, mixed_grad, heads, rows
     )
-    normed_one_grad = total(dot(projected_low, in_full, NT, out=BF16), 9)
+    projected_low, upgate_sum = lax.optimization_barrier((projected_low, upgate_sum))
+    output_total = owned_rows(output_grad)
+    in_grad = dot(normed_all, projected_low, TN, out=BF16)
+    projected_low, in_grad = lax.optimization_barrier((projected_low, in_grad))
+    back_one = dot(projected_low, in_full, NT, out=BF16)
+    back_one, output_total = lax.optimization_barrier((back_one, output_total))
+    in_sum = owned_parts(in_grad)
+    normed_one_grad = total(back_one, 9)
+    hidden, normed_one_grad = lax.optimization_barrier((hidden, normed_one_grad))
+    result = middle + total(dot(hidden, down_full, out=BF16), 7)
     input_part, first_grad = norm_back(inputs, first_root, first_full, normed_one_grad)
     tokens_grad = middle_grad + input_part
 
-    def owned_rows(a):
-        return lax.psum_scatter(a, "fsdp", scatter_dimension=0, tiled=True)
-
-    def owned_parts(a):
-        a = a.reshape(n_dp, n_z, own_d, a.shape[-1]).transpose(1, 0, 2, 3)
-        a = lax.psum_scatter(a.reshape(width, -1), "fsdp", scatter_dimension=0, tiled=True)
-        a = lax.all_to_all(a.reshape(n_dp, own_d, -1), "dp", 0, 0, tiled=True)
-        return a.transpose(1, 0, 2).astype(F32)
-
-    down_total = owned_rows(dot(hidden, seed_all, TN, out=BF16)).astype(F32)
-    gate_total = owned_parts(dot(second_all, gate_low, TN, out=BF16))
-    up_total = owned_parts(dot(second_all, up_low, TN, out=BF16))
-    upgate_total = jnp.concatenate([gate_total.reshape(own_d, -1), up_total.reshape(own_d, -1)], axis=1)
-    output_total = owned_rows(dot(mixed, middle_all, TN, out=BF16)).astype(F32)
-    in_total = owned_parts(dot(normed_all, projected_low, TN, out=BF16))
-    bounds = (0, key, 2 * key, 2 * key + value, 2 * key + 2 * value)
+    down_total = down_total.astype(F32)
+    output_total = output_total.astype(F32)
+    up_total = to_owners(upgate_sum)
+    upgate_total = jnp.concatenate(
+        [
+            jnp.concatenate([a, b], axis=2).reshape(own_d, -1)
+            for a, b in (
+                (up_total[:, :, :main], up_total[:, :, 2 * main : main + units]),
+                (up_total[:, :, main : 2 * main], up_total[:, :, main + units :]),
+            )
+        ],
+        axis=1,
+    )
+    in_total = to_owners(in_sum)
     input_total = jnp.concatenate(
         [in_total[:, :, a:b].reshape(own_d, -1) for a, b in zip(bounds[:-1], bounds[1:])], axis=1
     )

time: 1040 us -> 856 us (0.82)
  waiting for transfers between devices: 118 us -> 14 us
  blocking collectives: 57.4 us -> 0 us
  other arithmetic: 27.7 us -> 50.1 us
  matrix products: 190 us -> 170 us
  local copies, waits for them, and re-layouts: 82 us -> 67.3 us
    pallas_call x0 -> x1, Pallas kernels: none -> 118 us  [begin(): pl.pallas_call(kernel, out_shape=[jax.ShapeDtypeStruct((8, n_z, own, cols...]
    all_gather x3 -> x1, waiting for transfers between devices: 89.4 us -> 0.02 us  [whole_rows(): a = lax.all_gather(a[:, None], 'fsdp', axis=1, tiled=True)]
    pallas_call x4 -> x2, Pallas kernels: 154 us -> 77.7 us  [ag_square(): pl.pallas_call(kernel, out_shape=jax.ShapeDtypeStruct((8, rows, cols), x....]
    all_to_all x3 -> x0, blocking collectives: 57.4 us -> none  [whole_rows(): a = lax.all_to_all(a, 'dp', 0, 0, tiled=True)]
    pallas_call x1, Pallas kernels: 95.7 us -> 52.8 us  [mixer_forward(): pl.pallas_call(functools.partial(mixer_forward_kernel, heads), grid=(seqs...]
    dot_general x15 -> x12, matrix products: 190 us -> 170 us  [dot(): return lax.dot_general(a, b, dims, preferred_element_type=F32).astype(out)]
    all_gather x3 -> x0, local copies, waits for them, and re-layouts: 14.4 us -> none  [whole_rows(): a = lax.all_gather(a[:, None], 'fsdp', axis=1, tiled=True)]
    all_to_all x3 -> x2, waiting for transfers between devices: 24.4 us -> 12 us  [to_owners(): a = lax.all_to_all(a.reshape(n_dp, own_d, -1), 'dp', 0, 0, tiled=True)]
  transfers between devices with their start and end apart: 13 -> 9, of which waited for: 5 -> 2; matrix products, arithmetic and copies ran while one was open for 24% -> 23% of each run, Pallas kernels for 51% -> 48%
where the time goes in v2:
time: 856 us; the launch traced here: 846 us
  Pallas kernels  520 us (61%)
  matrix products  170 us (20%)
  local copies, waits for them, and re-layouts  67.3 us (8%)
  other arithmetic  50.1 us (6%)
  between operations  16.2 us (2%)
  waiting for transfers between devices  14 us (2%)
  starting transfers between devices  8.96 us (1%)
    dot_general x12, matrix products, dot(): return lax.dot_general(a, b, dims, preferred_element_type=F32).astype(out)  170 us
    pallas_call x4, Pallas kernels, rs_square(): pl.pallas_call(kernel, out_shape=jax.ShapeDtypeStruct((rows, cols), F32),...  164 us
    pallas_call x1, Pallas kernels, begin(): pl.pallas_call(kernel, out_shape=[jax.ShapeDtypeStruct((8, n_z, own, cols...  118 us
    pallas_call x2, Pallas kernels, ag_square(): pl.pallas_call(kernel, out_shape=jax.ShapeDtypeStruct((8, rows, cols), x....  77.7 us
    pallas_call x1, Pallas kernels, gather_small(): pl.pallas_call(kernel, out_shape=jax.ShapeDtypeStruct((count, rows, cols)...  58.2 us
    pallas_call x1, Pallas kernels, mixer_forward(): pl.pallas_call(functools.partial(mixer_forward_kernel, heads), grid=(seqs...  52.8 us
    pallas_call x1, Pallas kernels, mixer_backward(): pl.pallas_call(functools.partial(mixer_backward_kernel, heads), grid=(seq...  50.1 us
    unnamed x131, local copies, waits for them, and re-layouts  27.3 us
  transfers between devices with their start and end apart: 9, of which 2 were waited for; matrix products, arithmetic and copies ran while one was open for 23% of the time, Pallas kernels for 48%

profile of v2, /device:TPU:0, one launch (start us, length us, event | category | flops | bytes accessed | tf_op | source)
XLA Modules:
  0.0 846.4 jit_solution(2570360555608879729)
XLA Ops:
  7.2 1.4 fusion.20
  17.5 1.6 copy.115
  19.9 2.6 concatenate.41
  24.7 1.4 copy-done.11
  26.1 117.7 %shard_map.237 = (bf16[8,4,64,1664]{3,2,1,0:T(8,128)(2,1)S(1)}, bf16[8,64,1408]{2,1,0:T(8,128)(2,1)}, bf16[8,256,2048]{2,1,0:T(8,128)(2,1)S(1)}, bf16[8,256,2048]{2,1,0:T(8,128)(2,1)}, bf16[32,16,128]{2,1,0:T(8,128)(2,1)S(1)}) custom-call(bf16[64,12288]{1,0:T(8,128)(2,1)S(1)} %copy-done.11, bf16[8,64,128]{2,1,0:T(8,128)(2,1)S(1)} %copy-done.7, ...), custom_call_target="tpu_custom_call" | custom-call | flops 149999992832 | tf_op jit(solution)/shard_map/pallas_call | solution.py:672
  144.5 3.3 copy-done.13
  147.8 2.8 copy-done.16
  152.7 1.5 convert_reduce_fusion.1
  154.2 1.6 convert_reduce_fusion
  158.7 21.6 %fusion.24.proj_ref = f32[2048,1664]{1,0:T(8,128)} fusion(bf16[2048,2048]{1,0:T(8,128)(2,1)} %bitcast.111, bf16[2048,1664]{1,0:T(8,128)(2,1)} %bitcast.117), kind=kOutput, calls=%fused_computation.97 | convolution fusion | flops 13958643712 | bytes 28835840 | tf_op jit(solution)/shard_map/dot_general | solution.py:767
  180.3 52.8 %shard_map.238 = (bf16[2048,512]{1,0:T(8,128)(2,1)S(1)}, f32[8,2,256,256]{3,2,1,0:T(8,128)}, f32[2048,512]{1,0:T(8,128)}, f32[2048,512]{1,0:T(8,128)}) custom-call(f32[2048,1664]{1,0:T(8,128)} %fusion.24.proj_ref, f32[4,1024]{1,0:T(4,128)S(1)} %maximum_convert_fusion.taps_ref, f32[2,128]{1,0:T(2,128)S(1)} %select_maximum_fusion.decay_ref, f32[1,256]{1,0:T(1,128)S(1)} %bitcast.110), custom_call_target="tpu_custom_call" | custom-call | flops 54999998464 | tf_op jit(solution)/shard_map/pallas_call | solution.py:162
  233.7 7.1 convolution_convert_fusion.2
  240.8 43.9 %shard_map.239 = f32[256,2048]{1,0:T(8,128)S(1)} custom-call(bf16[8,256,2048]{2,1,0:T(8,128)(2,1)S(1)} %bitcast.116), custom_call_target="tpu_custom_call" | custom-call | flops 40000000000 | tf_op jit(solution)/shard_map/pallas_call | solution.py:420
  284.7 1.1 multiply_reduce_fusion.2
  285.8 1.3 copy-done.19
  287.1 1.2 multiply_convert_fusion.4.x_ref
  288.4 38.4 %shard_map.240 = bf16[8,256,2048]{2,1,0:T(8,128)(2,1)} custom-call(bf16[256,2048]{1,0:T(8,128)(2,1)} %multiply_convert_fusion.4.x_ref), custom_call_target="tpu_custom_call" | custom-call | flops 40000000000 | tf_op jit(solution)/shard_map/pallas_call | solution.py:356
  326.8 19.0 %fusion.25 = f32[2048,1408]{0,1:T(8,128)} fusion(bf16[2048,2048]{1,0:T(8,128)(2,1)} %bitcast.155, bf16[2048,1408]{1,0:T(8,128)(2,1)} %bitcast.151), kind=kOutput, calls=%fused_computation.98 | convolution fusion | flops 11811160064 | bytes 25690112 | tf_op jit(solution)/shard_map/dot_general | solution.py:767
  345.8 1.3 multiply_multiply_fusion.1
  347.1 5.0 multiply_multiply_fusion
  352.1 2.3 copy-done.22
  354.4 11.0 %convolution_convert_fusion.6 = bf16[704,2048]{1,0:T(8,128)(2,1)} fusion(bf16[2048,2048]{1,0:T(8,128)(2,1)} %bitcast.153, f32[2048,64]{0,1:T(8,128)S(1)} %multiply_multiply_fusion.1, f32[2048,640]{0,1:T(8,128)S(1)} %multiply_multiply_fusion, f32[2048]{0:T(1024)S(1)} %bitcast.148), kind=kOutput, calls=%fused_computation.16 | convolution fusion | flops 5911347200 | bytes 17047552 | tf_op jit(solution)/shard_map/dot_general | solution.py:767
  366.0 9.5 %convolution_multiply_fusion = f32[2048,704]{0,1:T(8,128)S(1)} fusion(bf16[2048,2048]{1,0:T(8,128)(2,1)} %bitcast.154, bf16[704,2048]{1,0:T(8,128)(2,1)} %all-gather.7.cloned.1.call-done, f32[2048]{0:T(1024)S(1)} %bitcast.149), kind=kOutput, calls=%fused_computation.14 | convolution fusion | flops 5907021824 | bytes 17047552 | tf_op jit(solution)/shard_map/dot_general | solution.py:767
  375.5 1.4 multiply_convert_fusion.6
  376.9 6.8 multiply_convert_fusion.2
  383.7 18.0 %convolution_convert_fusion.5 = bf16[2048,1408]{1,0:T(8,128)(2,1)} fusion(bf16[2048,2048]{1,0:T(8,128)(2,1)} %bitcast.156, bf16[2048,64]{0,1:T(8,128)(2,1)S(1)} %get-tuple-element.90, bf16[2048,64]{0,1:T(8,128)(2,1)S(1)} %get-tuple-element.89, bf16[2048,640]{0,1:T(8,128)(2,1)} %get-tuple-element.88, bf16[2048,640]{0,1:T(8,128)(2,1)S(1)} %get-tuple-element.87), kind=kOutput, calls=%fused_computation.5 | convolution fusion | flops 11837112320 | bytes 19922944 | tf_op jit(solution)/shard_map/dot_general | solution.py:767
  401.7 19.0 %convolution_convert_fusion.1 = bf16[2048,2048]{1,0:T(8,128)(2,1)} fusion(bf16[2048,1408]{1,0:T(8,128)(2,1)} %bitcast.152, bf16[2048,64]{0,1:T(8,128)(2,1)} %copy-done.26, bf16[2048,64]{0,1:T(8,128)(2,1)S(1)} %get-tuple-element.89, bf16[2048,640]{0,1:T(8,128)(2,1)} %get-tuple-element.88, bf16[2048,640]{0,1:T(8,128)(2,1)S(1)} %get-tuple-element.87), kind=kOutput, calls=%fused_computation.1 | convolution fusion | flops 11838423040 | bytes 19922944 | tf_op jit(solution)/shard_map/dot_general | solution.py:767
  421.5 1.3 dynamic_slice.37
  423.3 6.7 copy.100
  430.9 39.9 %shard_map.241 = f32[256,2048]{1,0:T(8,128)S(1)} custom-call(bf16[8,256,2048]{2,1,0:T(8,128)(2,1)S(1)} %bitcast.113), custom_call_target="tpu_custom_call" | custom-call | flops 40000000000 | tf_op jit(solution)/shard_map/pallas_call | solution.py:420
  470.8 1.3 multiply_reduce_fusion
  472.1 2.1 fusion
  474.3 1.1 copy-done.5
  475.4 3.8 fusion.16.x_ref
  479.2 2.4 convert_element_type.138
  481.6 39.3 %shard_map.242 = bf16[8,256,2048]{2,1,0:T(8,128)(2,1)} custom-call(bf16[256,2048]{1,0:T(8,128)(2,1)} %fusion.16.x_ref), custom_call_target="tpu_custom_call" | custom-call | flops 40000000000 | tf_op jit(solution)/shard_map/pallas_call | solution.py:356
  520.9 10.0 %fusion.26.grad_ref = f32[2048,512]{1,0:T(8,128)} fusion(bf16[2048,2048]{1,0:T(8,128)(2,1)} %bitcast.157, bf16[512,2048]{1,0:T(8,128)(2,1)S(1)} %copy-done.49), kind=kOutput, calls=%fused_computation.99 | convolution fusion | flops 4294967296 | bytes 14680064 | tf_op jit(solution)/shard_map/dot_general | solution.py:767
  530.9 5.7 convolution_convert_fusion.7
  536.6 50.1 %shard_map.243 = (bf16[2048,1664]{1,0:T(8,128)(2,1)}, f32[4,1024]{1,0:T(4,128)}, f32[1,256]{1,0:T(1,128)}, f32[2,128]{1,0:T(2,128)}) custom-call(f32[2048,1664]{1,0:T(8,128)} %fusion.24.proj_ref, f32[4,1024]{1,0:T(4,128)} %copy-done.9, f32[2,128]{1,0:T(2,128)} %copy-done.10, f32[1,256]{1,0:T(1,128)} %bitcast.109, ...), custom_call_target="tpu_custom_call" | custom-call | flops 49999998976 | tf_op jit(solution)/shard_map/pallas_call | solution.py:285
  587.6 20.5 %convolution_convert_fusion.4 = bf16[2048,1664]{1,0:T(8,128)(2,1)S(1)} fusion(bf16[2048,2048]{1,0:T(8,128)(2,1)} %bitcast.112, bf16[2048,1664]{1,0:T(8,128)(2,1)} %get-tuple-element.67), kind=kOutput, calls=%fused_computation.4 | convolution fusion | flops 13962051584 | bytes 22020096 | tf_op jit(solution)/shard_map/dot_general | solution.py:767
  608.1 3.3 copy.101
  611.4 19.0 %convolution_convert_fusion.3 = bf16[2048,2048]{1,0:T(8,128)(2,1)} fusion(bf16[2048,1664]{1,0:T(8,128)(2,1)S(1)} %bitcast.161, bf16[2048,1664]{1,0:T(8,128)(2,1)} %bitcast.118), kind=kOutput, calls=%fused_computation.3 | convolution fusion | flops 13962838016 | bytes 22020096 | tf_op jit(solution)/shard_map/dot_general | solution.py:767
  630.5 3.4 copy-done.15
  633.8 39.4 %shard_map.244 = f32[256,2048]{1,0:T(8,128)S(1)} custom-call(bf16[8,256,2048]{2,1,0:T(8,128)(2,1)S(1)} %bitcast.114), custom_call_target="tpu_custom_call" | custom-call | flops 40000000000 | tf_op jit(solution)/shard_map/pallas_call | solution.py:420
  674.7 58.2 %shard_map.246 = f32[32,72,128]{2,1,0:T(8,128)} custom-call(f32[72,128]{1,0:T(8,128)} %pad_bitcast_fusion.x_ref), custom_call_target="tpu_custom_call" | custom-call | flops 15000000512 | tf_op jit(solution)/shard_map/pallas_call | solution.py:748
  732.9 1.5 copy.131
  736.2 2.0 reshape.257
  738.2 1.4 reduce_sum.89
  739.6 4.3 all-to-all-start.1
  743.9 2.1 convert_element_type.135
  746.0 1.1 slice_reduce_fusion
  749.3 9.4 %convolution_convert_fusion = bf16[2048,2048]{1,0:T(8,128)(2,1)S(1)} fusion(bf16[2048,704]{0,1:T(8,128)(2,1)} %fusion, bf16[704,2048]{1,0:T(8,128)(2,1)} %all-gather.7.cloned.1.call-done), kind=kOutput, calls=%fused_computation | convolution fusion | flops 5909774336 | bytes 14155776 | tf_op jit(solution)/shard_map/dot_general | solution.py:767
  758.8 40.5 %shard_map.245 = f32[256,2048]{1,0:T(8,128)S(1)} custom-call(bf16[8,256,2048]{2,1,0:T(8,128)(2,1)S(1)} %bitcast.115), custom_call_target="tpu_custom_call" | custom-call | flops 40000000000 | tf_op jit(solution)/shard_map/pallas_call | solution.py:420
  800.5 3.8 fusion.8
  804.3 1.6 convert_bitcast_fusion.1
  806.0 1.4 fusion.18
  807.4 3.9 all-to-all-start
  812.3 1.7 reshape.264
  814.0 1.4 pad_maximum_fusion.5
  816.4 1.7 reshape.265
  818.1 3.6 pad_maximum_fusion.3
  821.7 11.9 %all-to-all-done = bf16[8,64,1664]{2,1,0:T(8,128)(2,1)S(1)} async-done(((bf16[8,64,1664]{2,1,0:T(8,128)(2,1)}), bf16[8,64,1664]{2,1,0:T(8,128)(2,1)S(1)}, u32[]{:S(2)}, u32[]{:S(2)}) %all-to-all-start) | async-done | bytes 1703968 | tf_op jit(solution)/shard_map/all_to_all | solution.py:953
  835.1 1.1 copy.106
  837.2 1.9 pad_maximum_fusion.2
  (212 shorter events, 32.0 us)
Async XLA Ops:
  7.2 226.6 %all-gather.5.cloned.1.call-start = ((), (), s32[]{:S(2)}) async-start(), calls=%async_computation.6 | async-start | bytes 2621440 | tf_op jit(solution)/shard_map/all_gather | solution.py:877
  8.6 2.8 copy-start.50
  8.7 4.7 copy-start.44
  8.7 4.7 copy-start.41
  15.0 4.2 copy-start.24
  15.0 4.2 copy-start.25
  15.0 8.1 copy-start.48
  15.0 8.8 %copy-start.2 = (bf16[256,2048]{1,0:T(8,128)(2,1)S(1)}, bf16[256,2048]{1,0:T(8,128)(2,1)}, u32[]{:S(2)}) copy-start(bf16[256,2048]{1,0:T(8,128)(2,1)} %t_ref.1) | copy-start | bytes 3145732
  15.0 8.8 %copy-start.4 = (bf16[256,2048]{1,0:T(8,128)(2,1)S(1)}, bf16[256,2048]{1,0:T(8,128)(2,1)}, u32[]{:S(2)}) copy-start(bf16[256,2048]{1,0:T(8,128)(2,1)} %c_ref.1) | copy-start | bytes 3145732
  23.8 0.9 copy-start.7
  24.7 1.4 copy-start.11
  143.8 0.7 copy-start.8
  144.5 3.3 copy-start.13
  147.8 2.8 copy-start.16
  150.6 7.9 copy-start.46
  150.6 7.9 copy-start.47
  150.7 176.1 %all-gather.9.cloned.1.call-start = ((), (), s32[]{:S(2)}) async-start(), calls=%async_computation.12 | async-start | bytes 7208960 | tf_op jit(solution)/shard_map/all_gather | solution.py:832
  151.4 214.6 %all-gather.7.cloned.1.call-start = ((), (), s32[]{:S(2)}) async-start(), calls=%async_computation.7 | async-start | bytes 3604480 | tf_op jit(solution)/shard_map/all_gather | solution.py:879
  152.1 327.1 %reduce-scatter.5.cloned.1.call-start = ((), (), s32[]{:S(2)}) async-start(), calls=%async_computation.8 | async-start | bytes 3604480 | tf_op jit(solution)/shard_map/reduce_scatter | solution.py:946
  158.5 127.3 %copy-start.27 = (f32[2048]{0:T(1024)}, f32[2048]{0:T(1024)S(1)}, u32[]{:S(2)}) copy-start(f32[2048]{0:T(1024)S(1)} %reshape.266) | copy-start | bytes 24580
  158.6 21.6 %copy-start.10 = (f32[2,128]{1,0:T(2,128)}, f32[2,128]{1,0:T(2,128)S(1)}, u32[]{:S(2)}) copy-start(f32[2,128]{1,0:T(2,128)S(1)} %select_maximum_fusion.decay_ref) | copy-start | bytes 3076
  158.7 21.6 %copy-start.12 = (f32[256]{0:T(256)S(1)}, f32[256]{0:T(256)}, u32[]{:S(2)}) copy-start(f32[256]{0:T(256)} %param.23) | copy-start | bytes 3076
  233.1 0.6 copy-start.9
  233.7 7.1 copy-start.17
  285.8 1.3 copy-start.19
  285.8 1.3 copy-start.33
  347.1 7.3 copy-start.42
  352.1 2.3 copy-start.22
  376.9 6.8 copy-start.26
  401.7 19.1 %copy-start.31 = (f32[32,64]{1,0:T(8,128)S(1)}, f32[32,64]{1,0:T(8,128)}, u32[]{:S(2)}) copy-start(f32[32,64]{1,0:T(8,128)} %get-tuple-element.83) | copy-start | bytes 24580
  401.7 21.0 %copy-start.43 = (f32[256]{0:T(256)S(1)}, f32[256]{0:T(256)}, u32[]{:S(2)}) copy-start(f32[256]{0:T(256)} %get-tuple-element.105) | copy-start | bytes 3076
  420.7 166.8 %reduce-scatter.7.cloned.1.call-start = ((), (), s32[]{:S(2)}) async-start(), calls=%async_computation.9 | async-start | bytes 7208960 | tf_op jit(solution)/shard_map/reduce_scatter | solution.py:950
  423.3 7.6 copy-start.14
  430.0 42.1 %slice-start = ((s8[5242880]{0:T(1024)(128)(4,1)}), s8[4194304]{0:T(1024)(128)(4,1)S(1)}, s32[]{:S(2)}) async-start(s8[5242880]{0:T(1024)(128)(4,1)} %bitcast.121), calls=%async_computation.13 | async-start | bytes 8388608
  430.9 39.9 %copy-start.20 = (f32[256,2048]{1,0:T(8,128)S(1)}, f32[256,2048]{1,0:T(8,128)}, u32[]{:S(2)}) copy-start(f32[256,2048]{1,0:T(8,128)} %copy-done.19) | copy-start | bytes 6291460
  430.9 39.9 %copy-start.28 = (f32[2048]{0:T(1024)S(1)}, f32[2048]{0:T(1024)}, u32[]{:S(2)}) copy-start(f32[2048]{0:T(1024)} %copy-done.27) | copy-start | bytes 24580
  430.9 39.9 %copy-start.34 = (f32[256]{0:T(256)S(1)}, f32[256]{0:T(256)}, u32[]{:S(2)}) copy-start(f32[256]{0:T(256)} %copy-done.33) | copy-start | bytes 3076
  430.9 41.2 %slice-start.1 = ((s8[5242880]{0:T(1024)(128)(4,1)}), s8[1048576]{0:T(1024)(128)(4,1)S(1)}, s32[]{:S(2)}) async-start(s8[5242880]{0:T(1024)(128)(4,1)} %bitcast.121), calls=%async_computation.14 | async-start | bytes 2097152
  470.8 3.4 copy-start
  472.1 2.2 copy-start.39
  474.2 1.2 copy-start.5
  474.2 156.3 %reduce-scatter.9.cloned.1.call-start = ((), (), s32[]{:S(2)}) async-start(), calls=%async_computation.10 | async-start | bytes 2621440 | tf_op jit(solution)/shard_map/reduce_scatter | solution.py:946
  481.6 39.3 %copy-start.49 = (bf16[512,2048]{1,0:T(8,128)(2,1)S(1)}, bf16[512,2048]{1,0:T(8,128)(2,1)}, u32[]{:S(2)}) copy-start(bf16[512,2048]{1,0:T(8,128)(2,1)} %all-gather.5.cloned.1.call-done) | copy-start | bytes 6291460
  520.9 10.1 %copy-start.18 = (bf16[2048,512]{1,0:T(8,128)(2,1)S(1)}, bf16[2048,512]{1,0:T(8,128)(2,1)}, u32[]{:S(2)}) copy-start(bf16[2048,512]{1,0:T(8,128)(2,1)} %copy-done.17) | copy-start | bytes 6291460
  520.9 10.0 %copy-start.51 = (bf16[8,256,2048]{2,1,0:T(8,128)(2,1)S(1)}, bf16[8,256,2048]{2,1,0:T(8,128)(2,1)}, u32[]{:S(2)}) copy-start(bf16[8,256,2048]{2,1,0:T(8,128)(2,1)} %shard_map.242) | copy-start | bytes 25165828
  587.5 24.0 %slice-start.2 = ((s8[6815744]{0:T(1024)(128)(4,1)}), s8[2621440]{0:T(1024)(128)(4,1)S(1)}, s32[]{:S(2)}) async-start(s8[6815744]{0:T(1024)(128)(4,1)} %bitcast.160), calls=%async_computation.15 | async-start | bytes 5242880
  587.5 219.9 %reduce-scatter.11.cloned.1.call-start = ((), (), s32[]{:S(2)}) async-start(), calls=%async_computation.11 | async-start | bytes 8519680 | tf_op jit(solution)/shard_map/reduce_scatter | solution.py:950
  587.6 23.9 %slice-start.3 = ((s8[6815744]{0:T(1024)(128)(4,1)}), s8[4194304]{0:T(1024)(128)(4,1)S(1)}, s32[]{:S(2)}) async-start(s8[6815744]{0:T(1024)(128)(4,1)} %bitcast.160), calls=%async_computation.16 | async-start | bytes 8388608
  630.5 3.4 copy-start.15
  633.8 39.4 %copy-start.3 = (bf16[256,2048]{1,0:T(8,128)(2,1)S(1)}, bf16[256,2048]{1,0:T(8,128)(2,1)}, u32[]{:S(2)}) copy-start(bf16[256,2048]{1,0:T(8,128)(2,1)} %t_ref.1) | copy-start | bytes 3145732
  633.8 39.4 %copy-start.30 = (f32[2048]{0:T(1024)S(1)}, f32[2048]{0:T(1024)}, u32[]{:S(2)}) copy-start(f32[2048]{0:T(1024)} %reshape.268) | copy-start | bytes 24580
  633.8 39.4 %copy-start.38 = (f32[256]{0:T(256)S(1)}, f32[256]{0:T(256)}, u32[]{:S(2)}) copy-start(f32[256]{0:T(256)} %add_rsqrt_fusion) | copy-start | bytes 3076
  673.3 0.7 copy-start.32
  673.3 0.7 copy-start.45
  673.3 0.7 copy-start.37
  734.4 1.0 copy-start.23
  739.6 64.7 %all-to-all-start.1 = ((bf16[8,64,1408]{2,1,0:T(8,128)(2,1)}), bf16[8,64,1408]{2,1,0:T(8,128)(2,1)}, u32[]{:S(2)}, u32[]{:S(2)}) async-start(bf16[8,64,1408]{2,1,0:T(8,128)(2,1)} %bitcast.132), calls=%async_computation.5 | async-start | bytes 2883584 | tf_op jit(solution)/shard_map/all_to_all | solution.py:953
  758.7 41.7 %copy-start.1 = (f32[256,2048]{1,0:T(8,128)S(1)}, f32[256,2048]{1,0:T(8,128)}, u32[]{:S(2)}) copy-start(f32[256,2048]{1,0:T(8,128)} %copy-done) | copy-start | bytes 6291460
  758.7 41.7 %copy-start.6 = (bf16[256,2048]{1,0:T(8,128)(2,1)S(1)}, bf16[256,2048]{1,0:T(8,128)(2,1)}, u32[]{:S(2)}) copy-start(bf16[256,2048]{1,0:T(8,128)(2,1)} %c_ref.1) | copy-start | bytes 3145732
  758.7 41.7 %copy-start.21 = (f32[256,2048]{1,0:T(8,128)S(1)}, f32[256,2048]{1,0:T(8,128)}, u32[]{:S(2)}) copy-start(f32[256,2048]{1,0:T(8,128)} %copy-done.19) | copy-start | bytes 6291460
  758.7 41.7 %copy-start.29 = (f32[2048]{0:T(1024)S(1)}, f32[2048]{0:T(1024)}, u32[]{:S(2)}) copy-start(f32[2048]{0:T(1024)} %copy-done.27) | copy-start | bytes 24580
  758.7 41.7 %copy-start.35 = (f32[256]{0:T(256)S(1)}, f32[256]{0:T(256)}, u32[]{:S(2)}) copy-start(f32[256]{0:T(256)} %copy-done.33) | copy-start | bytes 3076
  758.7 41.7 %copy-start.40 = (f32[256]{0:T(256)S(1)}, f32[256]{0:T(256)}, u32[]{:S(2)}) copy-start(f32[256]{0:T(256)} %copy-done.39) | copy-start | bytes 3076
  807.4 26.2 %all-to-all-start = ((bf16[8,64,1664]{2,1,0:T(8,128)(2,1)}), bf16[8,64,1664]{2,1,0:T(8,128)(2,1)S(1)}, u32[]{:S(2)}, u32[]{:S(2)}) async-start(bf16[8,64,1664]{2,1,0:T(8,128)(2,1)} %bitcast.131), calls=%async_computation.4 | async-start | bytes 3407872 | tf_op jit(solution)/shard_map/all_to_all | solution.py:953
  (1 other events, 0.6 us)
Sparse Core Ops, SparseCore 0:
  150.8 48.7 all-gather.4
  201.2 105.7 all-gather.8
  308.5 57.4 all-gather.6
  420.8 54.8 reduce-scatter.4
  477.9 102.1 reduce-scatter.6
  587.6 41.2 reduce-scatter.8
  631.3 137.5 reduce-scatter.10

commit v3 on v2

--- a/solution.py
+++ b/solution.py
@@ -707,6 +707,334 @@
     )(weight, decays, ups, tokens, cotangent, small)
 
 
+def relay(left, first, second, first_dims, second_dims, gain, extras, norm_back, cid):
+    _, rows, depth = left.shape
+    width = gain.shape[1]
+    multiply = second is not None
+    out_cols = 0 if not multiply else second.shape[1] if second_dims == NN else second.shape[0]
+    chunks = 4
+    part = rows // chunks
+    tile = 512
+    out_tiles = [(a, min(a + tile, out_cols)) for a in range(0, out_cols, tile)]
+
+    def kernel(left_ref, first_ref, gain_ref, *refs):
+        extra_refs, refs = refs[: len(extras)], refs[len(extras) :]
+        if multiply:
+            second_ref, *refs = refs
+        rows_out, all_out, *refs = refs
+        if multiply:
+            prod_out, *refs = refs
+        if norm_back:
+            gain_grad, *refs = refs
+        if multiply:
+            *refs, w2, stage = refs
+        (T, A, B, R, S, lsem, sa, ra, sb, rb, x_send, x_recv, d_send, d_recv, f_send, f_recv) = refs
+        me, z, core, cx, cy = _place(8)
+
+        def dev(dx, dy, c):
+            return 2 * (2 * lax.rem(cy + dy, 2) + lax.rem(cx + dx, 2)) + c
+
+        def remote(src, dst, send, recv, device):
+            return pltpu.make_async_remote_copy(src, dst, send, recv, device_id=(device, z), device_id_type=MESH)
+
+        sib = dev(0, 0, 1 - core)
+        nf, ng, across = dev(1 - core, core, core), dev(core, 1 - core, core), dev(1, 1, core)
+        bar = pltpu.get_barrier_semaphore()
+        for d in (sib, nf, ng):
+            pl.semaphore_signal(bar, inc=1, device_id=(d, z), device_id_type=MESH)
+        if multiply:
+            load = pltpu.make_async_copy(second_ref, w2, lsem.at[2])
+            load.start()
+
+        mine = (across, ng, nf, me)
+        theirs = (dev(1, 1, 1 - core), dev(1 - core, core, 1 - core), dev(core, 1 - core, 1 - core), sib)
+
+        def partial(q, write):
+            def some(n, _):
+                cols = pl.ds(pl.multiple_of(n * tile, tile), tile)
+                w = first_ref[:, cols] if first_dims == NN else first_ref[cols, :]
+                write(cols, lax.dot_general(left_ref[q], w, first_dims, preferred_element_type=F32))
+                return 0
+
+            lax.fori_loop(0, width // tile, some, 0)
+
+        def give(k):
+            def write(cols, v):
+                T[k, :, cols] = v.astype(BF16)
+
+            partial(theirs[k], write)
+            remote(T.at[k], A.at[k], sa.at[k], ra.at[k], sib).start()
+
+        def got(k):
+            remote(T.at[k], A.at[k], sa.at[k], ra.at[k], sib).wait_recv()
+
+        def cut(c):
+            return pl.ds(c * part, part)
+
+        def ship(k, c, d):
+            return remote(B.at[k, cut(c)], R.at[k, cut(c)], sb.at[k, c], rb.at[k, c], d)
+
+        def send_sum(k):
+            got(k)
+
+            def write(cols, v):
+                B[k, :, cols] = (v + A[k, :, cols].astype(F32)).astype(BF16)
+
+            partial(mine[k], write)
+            for c in range(chunks):
+                ship(k, c, nf).start()
+
+        def keep_sum(k, out):
+            got(k)
+
+            def write(cols, v):
+                out[:, cols] = v + A[k, :, cols].astype(F32)
+
+            partial(mine[k], write)
+
+        pl.semaphore_wait(bar, 3)
+        give(0)
+        give(2)
+        send_sum(0)
+        give(1)
+        send_sum(2)
+        give(3)
+        keep_sum(1, S)
+        for c in range(chunks):
+            ship(0, c, nf).wait_recv()
+            B[1, cut(c)] = (S[cut(c)] + R[0, cut(c)].astype(F32)).astype(BF16)
+            ship(1, c, ng).start()
+        keep_sum(3, S)
+
+        source, other = nf, ng
+
+        def at(q, c):
+            return all_out.at[q, cut(c)]
+
+        def step(k, c):
+            return remote(at(me, c), at(me, c), x_send.at[k, c], x_recv.at[k, c], (dev(1, 0, core), dev(0, 1, core))[k])
+
+        def twin(k, q, c):
+            return remote(at(q, c), at(q, c), f_send.at[k, c], f_recv.at[k, c], sib)
+
+        def second_step(c):
+            return remote(at(source, c), at(source, c), d_send.at[c], d_recv.at[c], other)
+
+        gains = gain_ref[...]
+        if norm_back:
+            gain_grad[...] = jnp.zeros_like(gain_grad)
+        for c in range(chunks):
+            ship(2, c, nf).wait_recv()
+            ship(1, c, ng).wait_recv()
+            for h in range(2):
+                sl = pl.ds(c * part + h * (part // 2), part // 2)
+                total = S[sl] + R[2, sl].astype(F32) + R[1, sl].astype(F32)
+                if norm_back:
+                    v = extra_refs[0][sl]
+                    root = lax.rsqrt(jnp.mean(v * v, axis=-1, keepdims=True) + EPSILON)
+                    hat = v * root
+                    scaled = total * gains
+                    gain_grad[...] += jnp.sum(total * hat, axis=0, keepdims=True)
+                    done = extra_refs[1][sl] + root * (scaled - hat * jnp.mean(scaled * hat, axis=-1, keepdims=True))
+                    low = done
+                else:
+                    done = extra_refs[0][sl].astype(F32) + total
+                    low = done * lax.rsqrt(jnp.mean(done * done, axis=-1, keepdims=True) + EPSILON) * gains
+                rows_out[sl] = done
+                all_out[me, sl] = low.astype(BF16)
+            for k in range(2):
+                step(k, c).start()
+            twin(0, me, c).start()
+        if multiply:
+            load.wait()
+
+        flushes = []
+
+        def product(q):
+            if not multiply:
+                return
+            slot = len(flushes) % 2
+            if len(flushes) > 1:
+                flushes[-2].wait()
+            for a, b in out_tiles:
+                w = w2[:, a:b] if second_dims == NN else w2[a:b, :]
+                stage[slot, :, a:b] = lax.dot_general(all_out[q], w, second_dims, preferred_element_type=F32)
+            flush = pltpu.make_async_copy(stage.at[slot], prod_out.at[q], lsem.at[slot])
+            flush.start()
+            flushes.append(flush)
+
+        def twin_got(k):
+            for c in range(chunks):
+                twin(k, theirs_at[k], c).wait_recv()
+
+        theirs_at = (sib, dev(core, 1 - core, 1 - core), dev(1 - core, core, 1 - core), dev(1, 1, 1 - core))
+        product(me)
+        for c in range(chunks):
+            remote(at(source, c), at(source, c), x_send.at[core, c], x_recv.at[core, c], sib).wait_recv()
+            second_step(c).start()
+            twin(1, source, c).start()
+            remote(at(other, c), at(other, c), x_send.at[1 - core, c], x_recv.at[1 - core, c], sib).wait_recv()
+            twin(2, other, c).start()
+            if c == 0:
+                twin_got(0)
+                product(sib)
+        product(source)
+        product(other)
+        for c in range(chunks):
+            remote(at(across, c), at(across, c), d_send.at[c], d_recv.at[c], sib).wait_recv()
+            twin(3, across, c).start()
+            if c == 0:
+                twin_got(1)
+                product(theirs_at[1])
+            if c == 1:
+                twin_got(2)
+                product(theirs_at[2])
+        product(across)
+        twin_got(3)
+        product(theirs_at[3])
+
+        for k in range(4):
+            remote(T.at[k], A.at[k], sa.at[k], ra.at[k], sib).wait_send()
+        for c in range(chunks):
+            for k in range(3):
+                ship(k, c, nf).wait_send()
+            for k in range(2):
+                step(k, c).wait_send()
+            second_step(c).wait_send()
+            for k, q in enumerate((me, source, other, across)):
+                twin(k, q, c).wait_send()
+        for flush in flushes[-2:]:
+            flush.wait()
+
+    dma = pltpu.SemaphoreType.DMA
+    anywhere, vmem = pl.BlockSpec(memory_space=pl.ANY), pl.BlockSpec(memory_space=pltpu.VMEM)
+    block = lambda n: pltpu.VMEM((n, rows, width), BF16)
+    out_shape = [
+        jax.ShapeDtypeStruct((rows, width), F32),
+        jax.ShapeDtypeStruct((8, rows, width), BF16),
+    ]
+    out_specs = [vmem, vmem]
+    operands = [left, first, gain, *extras]
+    in_specs = [vmem] * len(operands)
+    later = []
+    if multiply:
+        out_shape.append(jax.ShapeDtypeStruct((8, rows, out_cols), F32))
+        out_specs.append(anywhere)
+        operands.append(second)
+        in_specs.append(anywhere)
+        later = [pltpu.VMEM(second.shape, BF16), pltpu.VMEM((2, rows, out_cols), F32)]
+    if norm_back:
+        out_shape.append(jax.ShapeDtypeStruct((1, width), F32))
+        out_specs.append(vmem)
+    return pl.pallas_call(
+        kernel,
+        out_shape=out_shape,
+        in_specs=in_specs,
+        out_specs=out_specs,
+        scratch_shapes=[
+            block(4),
+            block(4),
+            block(3),
+            block(3),
+            pltpu.VMEM((rows, width), F32),
+            dma((3,)),
+            dma((4,)),
+            dma((4,)),
+            dma((3, chunks)),
+            dma((3, chunks)),
+            dma((2, chunks)),
+            dma((2, chunks)),
+            dma((chunks,)),
+            dma((chunks,)),
+            dma((4, chunks)),
+            dma((4, chunks)),
+            *later,
+        ],
+        cost_estimate=busy(80),
+        compiler_params=pltpu.CompilerParams(
+            collective_id=cid, has_side_effects=True, vmem_limit_bytes=58 << 20
+        ),
+    )(*operands)
+
+
+def unit_pairs(a, main):
+    tail = a[:, 2 * main :]
+    size = tail.shape[1]
+    turned = pltpu.roll(tail, size // 2, 1)
+    left = lax.broadcasted_iota(jnp.int32, tail.shape, 1) < size // 2
+    return (a[:, :main], a[:, main : 2 * main]), (jnp.where(left, tail, turned), jnp.where(left, turned, tail)), left
+
+
+def units_forward(x, weight, scales, units, main):
+    blocks, rows, width = x.shape
+    cols = weight.shape[1]
+
+    def kernel(x_ref, w_ref, s_ref, up_ref, hidden_ref, scaled_ref):
+        scale = s_ref[pl.ds(pl.program_id(0), 1), :][:, 0:1]
+        for a in range(0, cols, 512):
+            b = min(a + 512, cols)
+            up_ref[:, a:b] = jnp.dot(x_ref[...], w_ref[:, a:b], preferred_element_type=F32)
+        (g, u), (g_tail, u_tail), _ = unit_pairs(up_ref[...], main)
+        hidden = g * sigmoid(g) * u
+        tail = (g_tail * sigmoid(g_tail) * u_tail)[:, : units - main]
+        hidden_ref[:, :main] = hidden.astype(BF16)
+        hidden_ref[:, main:] = tail.astype(BF16)
+        scaled_ref[:, :main] = (hidden * scale).astype(BF16)
+        scaled_ref[:, main:] = (tail * scale).astype(BF16)
+
+    row = lambda n: pl.BlockSpec((rows, n), lambda i: (i, 0))
+    whole = lambda a: pl.BlockSpec(a.shape, lambda i: (0, 0))
+    tokens = blocks * rows
+    return pl.pallas_call(
+        kernel,
+        grid=(blocks,),
+        in_specs=[row(width), whole(weight), whole(scales)],
+        out_specs=[row(cols), row(units), row(units)],
+        out_shape=[
+            jax.ShapeDtypeStruct((tokens, cols), F32),
+            jax.ShapeDtypeStruct((tokens, units), BF16),
+            jax.ShapeDtypeStruct((tokens, units), BF16),
+        ],
+        cost_estimate=busy(20),
+        compiler_params=pltpu.CompilerParams(vmem_limit_bytes=48 << 20),
+    )(x.reshape(tokens, width), weight, scales)
+
+
+def units_backward(cot, weight, upgate, scales, units, main):
+    blocks, rows, width = cot.shape
+    cols = upgate.shape[1]
+
+    def kernel(c_ref, w_ref, up_ref, s_ref, low_ref):
+        scale = s_ref[pl.ds(pl.program_id(0), 1), :][:, 0:1]
+        pair, pair_tail, left = unit_pairs(up_ref[...], main)
+        tail_rows = w_ref[main:, :]
+        grad = dot(c_ref[...], w_ref[:main, :], NT) * scale
+        grad_tail = dot(c_ref[...], jnp.concatenate([tail_rows, tail_rows], axis=0), NT) * scale
+
+        def both(g, u, grad):
+            s = sigmoid(g)
+            return grad * u * s * (1.0 + g * (1.0 - s)), grad * g * s
+
+        gate_grad, up_grad = both(*pair, grad)
+        low_ref[:, :main] = gate_grad.astype(BF16)
+        low_ref[:, main : 2 * main] = up_grad.astype(BF16)
+        gate_grad, up_grad = both(*pair_tail, grad_tail)
+        low_ref[:, 2 * main :] = jnp.where(left, gate_grad, up_grad).astype(BF16)
+
+    row = lambda n: pl.BlockSpec((rows, n), lambda i: (i, 0))
+    whole = lambda a: pl.BlockSpec(a.shape, lambda i: (0, 0))
+    tokens = blocks * rows
+    return pl.pallas_call(
+        kernel,
+        grid=(blocks,),
+        in_specs=[row(width), whole(weight), row(cols), whole(scales)],
+        out_specs=row(cols),
+        out_shape=jax.ShapeDtypeStruct((tokens, cols), BF16),
+        cost_estimate=busy(12),
+        compiler_params=pltpu.CompilerParams(vmem_limit_bytes=48 << 20),
+    )(cot.reshape(tokens, width), weight, upgate, scales)
+
+
 def gather_small(x, n_dp, n_z, cid):
     rows, cols = x.shape
     count = n_dp * n_z
@@ -738,6 +1066,54 @@
 
         lax.fori_loop(1, count, greet, 0)
         local = pltpu.make_async_copy(x_ref, o_ref.at[flat], lsem)
+        local.start()
+        pl.semaphore_wait(bar, count - 1)
+        lax.fori_loop(1, count, send, 0)
+        lax.fori_loop(1, count, wait, 0)
+        local.wait()
+
+    dma = pltpu.SemaphoreType.DMA
+    return pl.pallas_call(
+        kernel,
+        out_shape=jax.ShapeDtypeStruct((count, rows, cols), x.dtype),
+        in_specs=[pl.BlockSpec(memory_space=pl.ANY)],
+        out_specs=pl.BlockSpec(memory_space=pl.ANY),
+        scratch_shapes=[dma, dma((count - 1,)), dma((count - 1,))],
+        cost_estimate=busy(15),
+        compiler_params=pltpu.CompilerParams(collective_id=cid, has_side_effects=True),
+    )(x)
+
+
+def scatter_small(x, n_dp, n_z, cid):
+    count, rows, cols = x.shape
+
+    def kernel(x_ref, o_ref, lsem, ssem, rsem):
+        flat = lax.axis_index("dp") * n_z + lax.axis_index("fsdp")
+        bar = pltpu.get_barrier_semaphore()
+
+        def device(o):
+            other = lax.rem(flat + o, count)
+            return (other // n_z, lax.rem(other, n_z))
+
+        def copy(o):
+            return pltpu.make_async_remote_copy(
+                x_ref.at[lax.rem(flat + o, count)], o_ref.at[flat], ssem.at[o - 1], rsem.at[o - 1], device_id=device(o), device_id_type=MESH
+            )
+
+        def greet(o, _):
+            pl.semaphore_signal(bar, inc=1, device_id=device(o), device_id_type=MESH)
+            return 0
+
+        def send(o, _):
+            copy(o).start()
+            return 0
+
+        def wait(o, _):
+            copy(o).wait()
+            return 0
+
+        lax.fori_loop(1, count, greet, 0)
+        local = pltpu.make_async_copy(x_ref.at[flat], o_ref.at[flat], lsem)
         local.start()
         pl.semaphore_wait(bar, count - 1)
         lax.fori_loop(1, count, send, 0)
@@ -837,15 +1213,10 @@
     first_root = lax.rsqrt(jnp.mean(inputs * inputs, axis=-1, keepdims=True) + EPSILON)
     if square:
         small = jnp.concatenate(
-            [
-                jnp.tile(norm_first, 128 // own_d)[None],
-                jnp.tile(norm_second, 128 // own_d)[None],
-                jnp.broadcast_to(group_ids.astype(BF16)[:, None], (1, 128)),
-                jnp.zeros((5, 128), BF16),
-                conv_weight.reshape(8, 128),
-            ],
-            axis=0,
-        )
+            [norm_first] * (128 // own_d)
+            + [norm_second] * (128 // own_d)
+            + [jnp.broadcast_to(group_ids.astype(BF16), (128,)), jnp.zeros((640,), BF16), conv_weight.reshape(-1)]
+        ).reshape(16, 128)
         in_full, up_plane, normed_all, cot_all, small = begin(
             input_weight, decay_cols, up_mine, tokens, cotangent, small, bounds, n_z, 1
         )
@@ -884,6 +1255,7 @@
     scales = 1.0 / jnp.sum((every_id[:, None] == every_id[None, :]).astype(F32), axis=0).reshape(n_dp, n_z)
     scales = lax.dynamic_index_in_dim(scales, lax.axis_index("fsdp"), axis=1, keepdims=False)
     seed = cotangent.astype(F32) * lax.dynamic_index_in_dim(scales, here, axis=0, keepdims=False)
+    lanes_of_scales = jnp.broadcast_to(scales[:, None], (n_dp, 128))
     scales = jnp.broadcast_to(scales[:, None, None], (n_dp, rows, 1)).reshape(n_dp * rows, 1)
     if not square:
         normed_all = spread((inputs * first_root * first_full).astype(BF16), 2)
@@ -908,30 +1280,40 @@
 
     projected = dot(normed_all, in_full)
     mixed, inverse, solved, core = mixer_forward(projected, conv_mine, decay_mine, gain, heads, rows)
-    middle = inputs + total(dot(mixed, out_full, out=BF16), 4)
-    second_root = lax.rsqrt(jnp.mean(middle * middle, axis=-1, keepdims=True) + EPSILON)
-    second_all = spread((middle * second_root * second_full).astype(BF16), 5)
-    upgate = dot(second_all, up_full)
-
-    def halves_of(a):
-        return (a[:, :main], a[:, main : 2 * main]), (a[:, 2 * main : main + units], a[:, main + units :])
-
-    acts = [(g, u, jax.nn.sigmoid(g)) for g, u in halves_of(upgate)]
-    hidden = jnp.concatenate([g * s * u for g, u, s in acts], axis=1)
-    hidden_seed = (hidden * scales).astype(BF16)
-    hidden = hidden.astype(BF16)
+    if square:
+        middle, second_all = relay(
+            mixed.reshape(n_dp, rows, value), out_full, None, NN, NN, second_full, (tokens,), False, 4
+        )
+        upgate, hidden, hidden_seed = units_forward(second_all, up_full, lanes_of_scales, units, main)
+        second_all = second_all.reshape(n_dp * rows, width)
+    else:
+        middle = inputs + total(dot(mixed, out_full, out=BF16), 4)
+        second_root = lax.rsqrt(jnp.mean(middle * middle, axis=-1, keepdims=True) + EPSILON)
+        second_all = spread((middle * second_root * second_full).astype(BF16), 5)
+        upgate = dot(second_all, up_full)
+
+        def halves_of(a):
+            return (a[:, :main], a[:, main : 2 * main]), (a[:, 2 * main : main + units], a[:, main + units :])
+
+        acts = [(g, u, jax.nn.sigmoid(g)) for g, u in halves_of(upgate)]
+        hidden = jnp.concatenate([g * s * u for g, u, s in acts], axis=1)
+        hidden_seed = (hidden * scales).astype(BF16)
+        hidden = hidden.astype(BF16)
 
     down_grad = dot(hidden_seed, cot_all, TN, out=BF16)
     down_grad, cot_all = lax.optimization_barrier((down_grad, cot_all))
-    hidden_grad = dot(cot_all, down_full, NT) * scales
-    parts = list(zip(acts, (hidden_grad[:, :main], hidden_grad[:, main:])))
-    upgate_low = jnp.concatenate(
-        [x for (g, u, s), grad in parts for x in (grad * u * s * (1.0 + g * (1.0 - s)), grad * g * s)], axis=1
-    ).astype(BF16)
-    back_two = dot(upgate_low, up_full, NT, out=BF16)
+    if square:
+        upgate_low = units_backward(
+            cot_all.reshape(n_dp, rows, width), down_full, upgate, lanes_of_scales, units, main
+        )
+    else:
+        hidden_grad = dot(cot_all, down_full, NT) * scales
+        parts = list(zip(acts, (hidden_grad[:, :main], hidden_grad[:, main:])))
+        upgate_low = jnp.concatenate(
+            [x for (g, u, s), grad in parts for x in (grad * u * s * (1.0 + g * (1.0 - s)), grad * g * s)], axis=1
+        ).astype(BF16)
     upgate_grad = dot(second_all, upgate_low, TN, out=BF16)
-    back_two, down_grad, upgate_grad = lax.optimization_barrier((back_two, down_grad, upgate_grad))
-    normed_two_grad = total(back_two, 6)
+    upgate_low, upgate_grad = lax.optimization_barrier((upgate_low, upgate_grad))
 
     def norm_back(v, root, gain_row, grad):
         hat = v * root
@@ -939,9 +1321,6 @@
         gain_grad = jnp.sum(grad * hat, axis=0)
         return root * (scaled - hat * jnp.mean(scaled * hat, axis=-1, keepdims=True)), gain_grad
 
-    middle_part, second_grad = norm_back(middle, second_root, second_full, normed_two_grad)
-    middle_grad = seed + middle_part
-
     def owned_rows(a):
         return lax.psum_scatter(a, "fsdp", scatter_dimension=0, tiled=True)
 
@@ -954,21 +1333,30 @@
         return a.transpose(1, 0, 2).astype(F32)
 
     down_total = owned_rows(down_grad)
-    middle_low, down_total = lax.optimization_barrier((middle_grad.astype(BF16), down_total))
-    middle_all = spread(middle_low, 8)
+    upgate_low, upgate_grad, down_total = lax.optimization_barrier((upgate_low, upgate_grad, down_total))
     upgate_sum = owned_parts(upgate_grad)
-    mixed_grad = dot(middle_all, out_full, NT)
+    if square:
+        middle_grad, middle_all, mixed_grad, second_grad = relay(
+            upgate_low.reshape(n_dp, rows, 2 * units), up_full, out_full, NT, NT, second_full, (middle, seed), True, 6
+        )
+        middle_all = middle_all.reshape(n_dp * rows, width)
+        mixed_grad = mixed_grad.reshape(n_dp * rows, value)
+    else:
+        normed_two_grad = total(dot(upgate_low, up_full, NT, out=BF16), 6)
+        middle_part, second_grad = norm_back(middle, second_root, second_full, normed_two_grad)
+        middle_grad = seed + middle_part
+        middle_all = spread(middle_grad.astype(BF16), 8)
+        mixed_grad = dot(middle_all, out_full, NT)
     output_grad = dot(mixed, middle_all, TN, out=BF16)
-    mixed_grad, output_grad = lax.optimization_barrier((mixed_grad, output_grad))
+    mixed_grad, output_grad, upgate_sum = lax.optimization_barrier((mixed_grad, output_grad, upgate_sum))
+    output_total = owned_rows(output_grad)
     projected_low, conv_grad, gain_grad, decay_grad = mixer_backward(
         projected, conv_mine, decay_mine, gain, inverse, solved, core, mixed_grad, heads, rows
     )
-    projected_low, upgate_sum = lax.optimization_barrier((projected_low, upgate_sum))
-    output_total = owned_rows(output_grad)
+    projected_low, output_total = lax.optimization_barrier((projected_low, output_total))
     in_grad = dot(normed_all, projected_low, TN, out=BF16)
     projected_low, in_grad = lax.optimization_barrier((projected_low, in_grad))
     back_one = dot(projected_low, in_full, NT, out=BF16)
-    back_one, output_total = lax.optimization_barrier((back_one, output_total))
     in_sum = owned_parts(in_grad)
     normed_one_grad = total(back_one, 9)
     hidden, normed_one_grad = lax.optimization_barrier((hidden, normed_one_grad))
@@ -1002,28 +1390,38 @@
         axis=1,
     )
 
-    sizes = (first_grad.size, second_grad.size, gain_grad.size, conv_grad.size, 2 * heads)
-    shared = gather_small(
-        pack((first_grad, second_grad, gain_grad, conv_grad, decay_grad[:, :heads]), 8), n_dp, n_z, 10
-    ).reshape(count, -1)
-    edges = [0]
-    for size in sizes:
-        edges.append(edges[-1] + size)
-    summed = jnp.sum(shared[:, : edges[3]], axis=0)
-    first_total = lax.dynamic_slice_in_dim(summed, flat * own_d, own_d)
-    second_total = lax.dynamic_slice_in_dim(summed, edges[1] + flat * own_d, own_d)
-    gain_total = summed[edges[2] : edges[3]]
-    by_plane = jnp.sum(shared[:, edges[3] : edges[5]].reshape(n_dp, n_z, -1), axis=1)
-    conv_all = by_plane[:, : sizes[3]].reshape(n_dp, taps, 2 * key + value)
-    conv_row = jnp.concatenate(
+    share = key // own_conv, value // own_conv
+    owner = jnp.concatenate(
         [
-            conv_all[:, :, a:b].transpose(1, 0, 2).reshape(taps, -1)
-            for a, b in ((0, key), (key, 2 * key), (2 * key, 2 * key + value))
+            here * share[0] + jnp.arange(share[0]),
+            (n_dp + here) * share[0] + jnp.arange(share[0]),
+            2 * n_dp * share[0] + here * share[1] + jnp.arange(share[1]),
+        ]
+    )
+    blocks = conv_grad.reshape(taps, -1, own_conv).transpose(1, 0, 2).reshape(-1, taps * own_conv)
+    for_owner = owner[None, :] == jnp.arange(count)[:, None]
+    everyone = jnp.concatenate([gain_grad.reshape(-1), decay_grad[:, :heads].reshape(-1)])
+    packets = jnp.concatenate(
+        [
+            first_grad.reshape(count, own_d),
+            second_grad.reshape(count, own_d),
+            jnp.sum(jnp.where(for_owner[:, :, None], blocks[None], 0.0), axis=1),
+            jnp.broadcast_to(everyone[None], (count, everyone.size)),
         ],
         axis=1,
     )
-    conv_total = lax.dynamic_slice_in_dim(conv_row, flat * own_conv, own_conv, axis=1)
-    scale_bias = by_plane[:, sizes[3] :].reshape(n_dp, 2, heads)
+    size = packets.shape[1]
+    lines = -(-size // 1024) * 8
+    packets = jnp.pad(packets, ((0, 0), (0, lines * 128 - size))).reshape(count, lines, 128)
+    shared = scatter_small(packets, n_dp, n_z, 10).reshape(count, -1)
+    summed = jnp.sum(shared, axis=0)
+    first_total = summed[:own_d]
+    second_total = summed[own_d : 2 * own_d]
+    start = 2 * own_d + taps * own_conv
+    conv_total = summed[2 * own_d : start].reshape(taps, own_conv)
+    gain_total = summed[start : start + gain_grad.size]
+    start += gain_grad.size
+    scale_bias = jnp.sum(shared[:, start : start + 2 * heads].reshape(n_dp, n_z, 2, heads), axis=1)
     scale_total = scale_bias[:, 0].reshape(-1)
     bias_total = scale_bias[:, 1].reshape(-1)
     return (

time: 856 us -> 805 us (0.940)
  matrix products: 170 us -> 106 us
  waiting for transfers between devices: 14 us -> 48 us
  other arithmetic: 50.1 us -> 30 us
  Pallas kernels: 520 us -> 533 us
    pallas_call x3 -> x5, Pallas kernels: 136 us -> 232 us  [the longest x2 182 us: relay(): pl.pallas_call(kernel, out_shape=out_shape, in_specs=in_specs, out_specs=...]
    pallas_call x4 -> x2, Pallas kernels: 164 us -> 79.8 us  [rs_square(): pl.pallas_call(kernel, out_shape=jax.ShapeDtypeStruct((rows, cols), F32),...]
    dot_general x12 -> x7, matrix products: 170 us -> 106 us  [dot(): return lax.dot_general(a, b, dims, preferred_element_type=F32).astype(out)]
    reduce_scatter x2, waiting for transfers between devices: 0.02 us -> 20.5 us  [owned_rows(): return lax.psum_scatter(a, 'fsdp', scatter_dimension=0, tiled=True)]
    all_gather x1, waiting for transfers between devices: 0.57 us -> 11.7 us  [local(): down_full = lax.all_gather(down_weight, 'fsdp', axis=0, tiled=True)]
    unnamed x131 -> x76, local copies, waits for them, and re-layouts: 27.3 us -> 19.3 us
  transfers between devices with their start and end apart: 9 -> 9, of which waited for: 2 -> 3; matrix products, arithmetic and copies ran while one was open for 23% -> 17% of each run, Pallas kernels for 48% -> 52%
where the time goes in v3:
time: 805 us; the launch traced here: 800 us
  Pallas kernels  533 us (66%)
  matrix products  106 us (13%)
  local copies, waits for them, and re-layouts  58.8 us (7%)
  waiting for transfers between devices  48 us (6%)
  other arithmetic  30 us (4%)
  between operations  15.6 us (2%)
  starting transfers between devices  8.18 us (1%)
    pallas_call x2, Pallas kernels, relay(): pl.pallas_call(kernel, out_shape=out_shape, in_specs=in_specs, out_specs=...  182 us
    pallas_call x1, Pallas kernels, begin(): pl.pallas_call(kernel, out_shape=[jax.ShapeDtypeStruct((8, n_z, own, cols...  118 us
    dot_general x7, matrix products, dot(): return lax.dot_general(a, b, dims, preferred_element_type=F32).astype(out)  106 us
    pallas_call x2, Pallas kernels, rs_square(): pl.pallas_call(kernel, out_shape=jax.ShapeDtypeStruct((rows, cols), F32),...  79.8 us
    pallas_call x1, Pallas kernels, mixer_forward(): pl.pallas_call(functools.partial(mixer_forward_kernel, heads), grid=(seqs...  52.7 us
    pallas_call x1, Pallas kernels, mixer_backward(): pl.pallas_call(functools.partial(mixer_backward_kernel, heads), grid=(seq...  50.9 us
    reduce_scatter x2, waiting for transfers between devices, owned_rows(): return lax.psum_scatter(a, 'fsdp', scatter_dimension=0, tiled=True)  20.5 us
    pallas_call x1, Pallas kernels, units_forward(): pl.pallas_call(kernel, grid=(blocks,), in_specs=[row(width), whole(weight...  19.8 us
  transfers between devices with their start and end apart: 9, of which 3 were waited for; matrix products, arithmetic and copies ran while one was open for 17% of the time, Pallas kernels for 52%

profile of v3, /device:TPU:0, one launch (start us, length us, event | category | flops | bytes accessed | tf_op | source)
XLA Modules:
  0.0 799.9 jit_solution(9603331173064239164)
XLA Ops:
  7.2 1.4 fusion.12
  10.5 0.9 copy.102
  11.5 0.9 copy.103
  14.5 0.8 maximum_bitcast_fusion.dec_ref
  15.3 2.6 concatenate.37
  18.4 2.1 concatenate.38
  20.4 0.9 copy-done.4
  21.4 1.4 copy-done.10
  22.8 117.7 %shard_map.237 = (bf16[8,4,64,1664]{3,2,1,0:T(8,128)(2,1)S(1)}, bf16[8,64,1408]{2,1,0:T(8,128)(2,1)}, bf16[8,256,2048]{2,1,0:T(8,128)(2,1)S(1)}, bf16[8,256,2048]{2,1,0:T(8,128)(2,1)}, bf16[32,16,128]{2,1,0:T(8,128)(2,1)S(1)}) custom-call(bf16[64,12288]{1,0:T(8,128)(2,1)S(1)} %copy-done.10, bf16[8,64,128]{2,1,0:T(8,128)(2,1)S(1)} %copy-done.4, ...), custom_call_target="tpu_custom_call" | custom-call | flops 149999992832 | tf_op jit(solution)/shard_map/pallas_call | solution.py:672
  141.2 3.2 copy-done.12
  144.4 2.8 copy-done.13
  148.7 0.8 slice.102
  149.6 1.6 convert_reduce_fusion
  151.2 1.5 convert_reduce_fusion.1
  153.7 22.0 %fusion.16.proj_ref = f32[2048,1664]{1,0:T(8,128)} fusion(bf16[2048,2048]{1,0:T(8,128)(2,1)} %bitcast.97, bf16[2048,1664]{1,0:T(8,128)(2,1)} %bitcast.101), kind=kOutput, calls=%fused_computation.60 | convolution fusion | flops 13958643712 | bytes 28835840 | tf_op jit(solution)/shard_map/dot_general | solution.py:1143
  176.1 52.7 %shard_map.238 = (bf16[2048,512]{1,0:T(8,128)(2,1)S(1)}, f32[8,2,256,256]{3,2,1,0:T(8,128)}, f32[2048,512]{1,0:T(8,128)}, f32[2048,512]{1,0:T(8,128)}) custom-call(f32[2048,1664]{1,0:T(8,128)} %fusion.16.proj_ref, f32[4,1024]{1,0:T(4,128)S(1)} %maximum_convert_fusion.taps_ref, f32[2,128]{1,0:T(2,128)S(1)} %select_maximum_fusion.decay_ref, f32[1,256]{1,0:T(1,128)S(1)} %bitcast.96), custom_call_target="tpu_custom_call" | custom-call | flops 54999998464 | tf_op jit(solution)/shard_map/pallas_call | solution.py:162
  229.5 1.3 copy-done.14
  230.8 88.7 %shard_map.239 = (f32[256,2048]{1,0:T(8,128)}, bf16[8,256,2048]{2,1,0:T(8,128)(2,1)}) custom-call(bf16[8,256,512]{2,1,0:T(8,128)(2,1)} %bitcast.103, bf16[512,2048]{1,0:T(8,128)(2,1)} %all-gather.5.cloned.1.call-done.first_ref.refs_2_, f32[1,2048]{1,0:T(1,128)} %reshape.271.gain_ref, bf16[256,2048]{1,0:T(8,128)(2,1)} %refs_0_.1), custom_call_target="tpu_custom_call" | custom-call | flops 80000000000 | tf_op jit(solution)/shard_map/pallas_call | solution.py:929
  319.6 19.8 %shard_map.240 = (f32[2048,1408]{1,0:T(8,128)}, bf16[2048,704]{1,0:T(8,128)(2,1)S(1)}, bf16[2048,704]{1,0:T(8,128)(2,1)}) custom-call(bf16[2048,2048]{1,0:T(8,128)(2,1)} %bitcast.132, bf16[2048,1408]{1,0:T(8,128)(2,1)} %bitcast.128, f32[8,128]{1,0:T(8,128)S(1)} %broadcast_in_dim.69.s_ref), custom_call_target="tpu_custom_call" | custom-call | flops 20000000000 | tf_op jit(solution)/shard_map/pallas_call | solution.py:988
  339.4 1.6 copy-done.16
  341.0 9.4 %convolution_convert_fusion.4 = bf16[704,2048]{1,0:T(8,128)(2,1)} fusion(bf16[2048,704]{1,0:T(8,128)(2,1)} %get-tuple-element.67, bf16[2048,2048]{1,0:T(8,128)(2,1)S(1)} %bitcast.131), kind=kOutput, calls=%fused_computation.5 | convolution fusion | flops 5907021824 | bytes 14155776 | tf_op jit(solution)/shard_map/dot_general | solution.py:1143
  350.5 11.7 %all-gather.7.cloned.1.call-done.w_ref = bf16[704,2048]{1,0:T(8,128)(2,1)} async-done(((bf16[176,2048]{1,0:T(8,128)(2,1)}), bf16[704,2048]{1,0:T(8,128)(2,1)}) %all-gather.7.cloned.1.call-update) | async-done | bytes 2883600 | tf_op jit(solution)/shard_map/all_gather | solution.py:1250
  362.1 1.8 copy-done.8
  364.0 16.2 %shard_map.241 = bf16[2048,1408]{1,0:T(8,128)(2,1)} custom-call(bf16[2048,2048]{1,0:T(8,128)(2,1)} %bitcast.130, bf16[704,2048]{1,0:T(8,128)(2,1)S(1)} %copy-done.8, f32[2048,1408]{1,0:T(8,128)} %get-tuple-element.71.up_ref, f32[8,128]{1,0:T(8,128)S(1)} %broadcast_in_dim.69.s_ref), custom_call_target="tpu_custom_call" | custom-call | flops 12000000000 | tf_op jit(solution)/shard_map/pallas_call | solution.py:1027
  380.2 19.1 %convolution_convert_fusion.3 = bf16[2048,1408]{1,0:T(8,128)(2,1)} fusion(bf16[2048,2048]{1,0:T(8,128)(2,1)} %bitcast.133, bf16[2048,1408]{1,0:T(8,128)(2,1)} %shard_map.241), kind=kOutput, calls=%fused_computation.3 | convolution fusion | flops 11814043648 | bytes 19922944 | tf_op jit(solution)/shard_map/dot_general | solution.py:1143
  399.3 20.5 %reduce-scatter.5.cloned.1.call-done = bf16[176,2048]{1,0:T(8,128)(2,1)} async-done(((bf16[704,2048]{1,0:T(8,128)(2,1)}), bf16[176,2048]{1,0:T(8,128)(2,1)}) %reduce-scatter.5.cloned.1.call-update) | async-done | bytes 720912 | tf_op jit(solution)/shard_map/reduce_scatter | solution.py:1325
  419.8 5.6 copy.88
  426.8 1.3 dynamic_slice.29
  429.0 2.2 convert_multiply_fusion.2.refs_1_
  431.3 93.3 %shard_map.242 = (f32[256,2048]{1,0:T(8,128)}, bf16[8,256,2048]{2,1,0:T(8,128)(2,1)}, f32[8,256,512]{2,1,0:T(8,128)}, f32[1,2048]{1,0:T(1,128)}) custom-call(bf16[8,256,1408]{2,1,0:T(8,128)(2,1)} %bitcast.135, bf16[2048,1408]{1,0:T(8,128)(2,1)} %bitcast.129, f32[1,2048]{1,0:T(1,128)} %reshape.271.gain_ref, f32[256,2048]{1,0:T(8,128)} %get-tuple-element.60.refs_0_, ...), custom_call_target="tpu_custom_call" | custom-call | flops 80000000000 | tf_op jit(solution)/shard_map/pallas_call | solution.py:929
  525.1 1.4 reduce.16
  527.1 1.3 convert_element_type.107
  528.4 9.1 %convolution_convert_fusion.5 = bf16[512,2048]{1,0:T(8,128)(2,1)} fusion(bf16[2048,512]{1,0:T(8,128)(2,1)S(1)} %copy-done.15, bf16[2048,2048]{1,0:T(8,128)(2,1)} %bitcast.134), kind=kOutput, calls=%fused_computation.7 | convolution fusion | flops 4296015872 | bytes 12582912 | tf_op jit(solution)/shard_map/dot_general | solution.py:1143
  537.5 3.6 all-to-all-start.1
  541.1 50.9 %shard_map.243 = (bf16[2048,1664]{1,0:T(8,128)(2,1)}, f32[4,1024]{1,0:T(4,128)}, f32[1,256]{1,0:T(1,128)}, f32[2,128]{1,0:T(2,128)}) custom-call(f32[2048,1664]{1,0:T(8,128)} %fusion.16.proj_ref, f32[4,1024]{1,0:T(4,128)} %copy-done.6, f32[2,128]{1,0:T(2,128)} %copy-done.7, f32[1,256]{1,0:T(1,128)} %bitcast.95, ...), custom_call_target="tpu_custom_call" | custom-call | flops 49999998976 | tf_op jit(solution)/shard_map/pallas_call | solution.py:285
  592.8 0.8 reshape.254
  593.5 1.3 pad_maximum_fusion.5
  594.8 0.8 select_reduce_fusion
  595.9 1.2 fusion.10
  597.3 0.9 copy.100
  598.8 1.4 pad_maximum_fusion.2
  600.3 0.9 copy.99
  601.2 1.7 reshape.269
  602.9 3.1 pad_maximum_fusion.1
  606.0 19.9 %convolution_convert_fusion.2 = bf16[2048,1664]{1,0:T(8,128)(2,1)S(1)} fusion(bf16[2048,2048]{1,0:T(8,128)(2,1)} %bitcast.98, bf16[2048,1664]{1,0:T(8,128)(2,1)} %get-tuple-element.83), kind=kOutput, calls=%fused_computation.2 | convolution fusion | flops 13962051584 | bytes 22020096 | tf_op jit(solution)/shard_map/dot_general | solution.py:1143
  626.0 3.4 copy.89
  629.4 19.6 %convolution_convert_fusion.1 = bf16[2048,2048]{1,0:T(8,128)(2,1)S(1)} fusion(bf16[2048,1664]{1,0:T(8,128)(2,1)} %get-tuple-element.83, bf16[2048,1664]{1,0:T(8,128)(2,1)} %bitcast.102), kind=kOutput, calls=%fused_computation.1 | convolution fusion | flops 13962838016 | bytes 22020096 | tf_op jit(solution)/shard_map/dot_general | solution.py:1143
  649.0 40.5 %shard_map.244 = f32[256,2048]{1,0:T(8,128)S(1)} custom-call(bf16[8,256,2048]{2,1,0:T(8,128)(2,1)S(1)} %bitcast.99), custom_call_target="tpu_custom_call" | custom-call | flops 40000000000 | tf_op jit(solution)/shard_map/pallas_call | solution.py:420
  689.6 7.3 convolution_convert_fusion
  696.9 39.2 %shard_map.245 = f32[256,2048]{1,0:T(8,128)S(1)} custom-call(bf16[8,256,2048]{2,1,0:T(8,128)(2,1)S(1)} %bitcast.100), custom_call_target="tpu_custom_call" | custom-call | flops 40000000000 | tf_op jit(solution)/shard_map/pallas_call | solution.py:420
  736.2 1.7 add.75
  739.2 0.8 concatenate.42
  740.1 0.8 copy.112
  740.8 13.7 %shard_map.246 = f32[32,16,128]{2,1,0:T(8,128)} custom-call(f32[32,16,128]{2,1,0:T(8,128)} %bitcast.115), custom_call_target="tpu_custom_call" | custom-call | flops 15000000512 | tf_op jit(solution)/shard_map/pallas_call | solution.py:1124
  754.5 2.3 copy.101
  756.8 1.0 reduce_sum.70
  759.3 4.3 all-to-all-start
  764.9 2.1 convert_element_type.104
  768.2 3.5 fusion.6
  771.7 14.3 %all-to-all-done = bf16[8,64,1664]{2,1,0:T(8,128)(2,1)} async-done(((bf16[8,64,1664]{2,1,0:T(8,128)(2,1)}), bf16[8,64,1664]{2,1,0:T(8,128)(2,1)}, u32[]{:S(2)}, u32[]{:S(2)}) %all-to-all-start) | async-done | bytes 1703968 | tf_op jit(solution)/shard_map/all_to_all | solution.py:1332
  786.0 1.7 convert_bitcast_fusion
  788.0 0.8 fusion.9
  789.1 1.1 copy.95
  790.9 1.9 pad_maximum_fusion
  (147 shorter events, 20.0 us)
Async XLA Ops:
  7.2 223.6 %all-gather.5.cloned.1.call-start = ((), (), s32[]{:S(2)}) async-start(), calls=%async_computation.6 | async-start | bytes 2621440 | tf_op jit(solution)/shard_map/all_gather | solution.py:1248
  8.6 1.5 copy-start.27
  10.1 4.3 copy-start.28
  11.4 6.9 copy-start.29
  11.4 9.0 %copy-start = (bf16[256,2048]{1,0:T(8,128)(2,1)S(1)}, bf16[256,2048]{1,0:T(8,128)(2,1)}, u32[]{:S(2)}) copy-start(bf16[256,2048]{1,0:T(8,128)(2,1)} %refs_0_.1) | copy-start | bytes 3145732
  11.5 9.0 %copy-start.3 = (bf16[256,2048]{1,0:T(8,128)(2,1)S(1)}, bf16[256,2048]{1,0:T(8,128)(2,1)}, u32[]{:S(2)}) copy-start(bf16[256,2048]{1,0:T(8,128)(2,1)} %c_ref.1) | copy-start | bytes 3145732
  20.4 0.9 copy-start.4
  21.4 1.4 copy-start.10
  140.5 0.7 copy-start.5
  141.2 3.2 copy-start.12
  144.4 2.8 copy-start.13
  147.2 172.3 %all-gather.9.cloned.1.call-start = ((), (), s32[]{:S(2)}) async-start(), calls=%async_computation.12 | async-start | bytes 7208960 | tf_op jit(solution)/shard_map/all_gather | solution.py:1208
  148.0 214.2 %all-gather.7.cloned.1.call-start = ((), (), s32[]{:S(2)}) async-start(), calls=%async_computation.7 | async-start | bytes 3604480 | tf_op jit(solution)/shard_map/all_gather | solution.py:1250
  148.7 271.1 %reduce-scatter.5.cloned.1.call-start = ((), (), s32[]{:S(2)}) async-start(), calls=%async_computation.8 | async-start | bytes 3604480 | tf_op jit(solution)/shard_map/reduce_scatter | solution.py:1325
  153.7 22.2 %copy-start.24 = (f32[8,4]{1,0:T(8,128)}, f32[8,4]{1,0:T(8,128)S(1)}, u32[]{:S(2)}) copy-start(f32[8,4]{1,0:T(8,128)S(1)} %div.17) | copy-start | bytes 388
  153.7 22.1 %copy-start.30 = (f32[16]{0:T(128)S(1)}, f32[16]{0:T(128)}, u32[]{:S(2)}) copy-start(f32[16]{0:T(128)} %param.22) | copy-start | bytes 196
  153.7 22.1 %copy-start.31 = (f32[16]{0:T(128)S(1)}, f32[16]{0:T(128)}, u32[]{:S(2)}) copy-start(f32[16]{0:T(128)} %param.21) | copy-start | bytes 196
  153.7 22.4 %copy-start.11 = (f32[256]{0:T(256)S(1)}, f32[256]{0:T(256)}, u32[]{:S(2)}) copy-start(f32[256]{0:T(256)} %param.23) | copy-start | bytes 3076
  175.9 52.9 %copy-start.7 = (f32[2,128]{1,0:T(2,128)}, f32[2,128]{1,0:T(2,128)S(1)}, u32[]{:S(2)}) copy-start(f32[2,128]{1,0:T(2,128)S(1)} %select_maximum_fusion.decay_ref) | copy-start | bytes 3076
  228.9 0.6 copy-start.6
  229.5 1.3 copy-start.14
  319.6 21.5 %copy-start.32 = (bf16[8,256,2048]{2,1,0:T(8,128)(2,1)S(1)}, bf16[8,256,2048]{2,1,0:T(8,128)(2,1)}, u32[]{:S(2)}) copy-start(bf16[8,256,2048]{2,1,0:T(8,128)(2,1)} %get-tuple-element.68) | copy-start | bytes 25165828
  339.4 1.6 copy-start.16
  350.4 187.0 %reduce-scatter.7.cloned.1.call-start = ((), (), s32[]{:S(2)}) async-start(), calls=%async_computation.9 | async-start | bytes 7208960 | tf_op jit(solution)/shard_map/reduce_scatter | solution.py:1329
  362.1 1.8 copy-start.8
  425.4 0.7 copy-start.23
  425.4 2.7 copy-start.1
  425.4 180.6 %reduce-scatter.9.cloned.1.call-start = ((), (), s32[]{:S(2)}) async-start(), calls=%async_computation.10 | async-start | bytes 2621440 | tf_op jit(solution)/shard_map/reduce_scatter | solution.py:1325
  431.3 95.8 %copy-start.19 = (bf16[176,2048]{1,0:T(8,128)(2,1)S(1)}, bf16[176,2048]{1,0:T(8,128)(2,1)}, u32[]{:S(2)}) copy-start(bf16[176,2048]{1,0:T(8,128)(2,1)} %reduce-scatter.5.cloned.1.call-done) | copy-start | bytes 2162692
  431.3 97.1 %copy-start.15 = (bf16[2048,512]{1,0:T(8,128)(2,1)S(1)}, bf16[2048,512]{1,0:T(8,128)(2,1)}, u32[]{:S(2)}) copy-start(bf16[2048,512]{1,0:T(8,128)(2,1)} %copy-done.14) | copy-start | bytes 6291460
  537.5 58.1 %all-to-all-start.1 = ((bf16[8,64,1408]{2,1,0:T(8,128)(2,1)}), bf16[8,64,1408]{2,1,0:T(8,128)(2,1)S(1)}, u32[]{:S(2)}, u32[]{:S(2)}) async-start(bf16[8,64,1408]{2,1,0:T(8,128)(2,1)} %bitcast.113), calls=%async_computation.5 | async-start | bytes 2883584 | tf_op jit(solution)/shard_map/all_to_all | solution.py:1332
  541.1 218.2 %reduce-scatter.11.cloned.1.call-start = ((), (), s32[]{:S(2)}) async-start(), calls=%async_computation.11 | async-start | bytes 8519680 | tf_op jit(solution)/shard_map/reduce_scatter | solution.py:1329
  649.0 40.6 %copy-start.9 = (bf16[704,2048]{1,0:T(8,128)(2,1)S(1)}, bf16[704,2048]{1,0:T(8,128)(2,1)}, u32[]{:S(2)}) copy-start(bf16[704,2048]{1,0:T(8,128)(2,1)} %all-gather.7.cloned.1.call-done.w_ref) | copy-start | bytes 8650756
  649.0 40.6 %copy-start.17 = (bf16[2048,704]{1,0:T(8,128)(2,1)S(1)}, bf16[2048,704]{1,0:T(8,128)(2,1)}, u32[]{:S(2)}) copy-start(bf16[2048,704]{1,0:T(8,128)(2,1)} %copy-done.16) | copy-start | bytes 8650756
  696.9 39.3 %copy-start.18 = (f32[256,2048]{1,0:T(8,128)S(1)}, f32[256,2048]{1,0:T(8,128)}, u32[]{:S(2)}) copy-start(f32[256,2048]{1,0:T(8,128)} %get-tuple-element.60.refs_0_) | copy-start | bytes 6291460
  736.2 1.7 copy-start.2
  736.2 1.7 copy-start.21
  736.2 1.7 copy-start.25
  737.9 1.4 copy-start.26
  737.9 1.4 copy-start.20
  737.9 1.4 copy-start.22
  759.3 26.8 %all-to-all-start = ((bf16[8,64,1664]{2,1,0:T(8,128)(2,1)}), bf16[8,64,1664]{2,1,0:T(8,128)(2,1)}, u32[]{:S(2)}, u32[]{:S(2)}) async-start(bf16[8,64,1664]{2,1,0:T(8,128)(2,1)} %bitcast.112), calls=%async_computation.4 | async-start | bytes 3407872 | tf_op jit(solution)/shard_map/all_to_all | solution.py:1332
Sparse Core Ops, SparseCore 0:
  147.3 48.7 all-gather.4
  197.6 105.4 all-gather.8
  304.7 57.4 all-gather.6
  364.9 54.8 reduce-scatter.4
  425.6 102.1 reduce-scatter.6
  537.6 43.1 reduce-scatter.8
  629.5 122.4 reduce-scatter.10

commit v4 on v3

--- a/solution.py
+++ b/solution.py
@@ -1035,6 +1035,468 @@
     )(cot.reshape(tokens, width), weight, upgate, scales)
 
 
+def conclude(grad, left, weight, block, ups, tokens, middle, middle_grad, gain, lines, conv, bounds, cid):
+    n_z = 4
+    _, _, own, cols = grad.shape
+    units = ups.shape[2]
+    rows, width = tokens.shape
+    count = 8 * n_z
+    per = 128 * count // width
+    conv_cols = conv.shape[1] // count
+    chunks = 2
+    part = rows // chunks
+    tile = 512
+    last = n_z - 1
+
+    def kernel(
+        g_ref, l_ref, w_ref, b_ref, u_ref, t_ref, m_ref, mg_ref, gain_ref, lines_ref, conv_ref,
+        result, tg, in_out, dec_out, u_out, lines_out, conv_out,
+        W, L, own_buf, UD, T, A, B, R, S, A7, B7, R7, X7, line_buf,
+        lsem, wsem, osem, mine_sem, us, ur, ds, dr, i_send, i_recv, u_send, u_recv, p_send, p_recv, c_send, c_recv,
+        sa, ra, sb, rb, sa7, ra7, sb7, rb7,
+    ):
+        me, z, core, cx, cy = _place(8)
+        flat = me * n_z + z
+
+        def dev(dx, dy, c):
+            return 2 * (2 * lax.rem(cy + dy, 2) + lax.rem(cx + dx, 2)) + c
+
+        sib = dev(0, 0, 1 - core)
+        nf, ng, across = dev(1 - core, core, core), dev(core, 1 - core, core), dev(1, 1, core)
+
+        def partner(o):
+            return dev(o // 4, lax.rem(o // 2, 2), lax.rem(core + o, 2))
+
+        def anyone(o):
+            other = lax.rem(flat + o, count)
+            return (other // n_z, lax.rem(other, n_z))
+
+        def remote(src, dst, send, recv, device):
+            return pltpu.make_async_remote_copy(src, dst, send, recv, device_id=device, device_id_type=MESH)
+
+        def loop(first, end, body):
+            def step(o, _):
+                body(o)
+                return 0
+
+            lax.fori_loop(first, end, step, 0)
+
+        bar = pltpu.get_barrier_semaphore()
+        loop(1, count, lambda o: pl.semaphore_signal(bar, inc=1, device_id=anyone(o), device_id_type=MESH))
+
+        mine = (across, ng, nf, me)
+        theirs = (dev(1, 1, 1 - core), dev(1 - core, core, 1 - core), dev(core, 1 - core, 1 - core), sib)
+        turns = (theirs[0], theirs[2], mine[0], theirs[1], mine[2], theirs[3], mine[1], mine[3])
+
+        def load_left(i):
+            return pltpu.make_async_copy(l_ref.at[turns[i]], L.at[i % 2], lsem.at[i % 2])
+
+        load_weight = pltpu.make_async_copy(w_ref, W, wsem.at[0])
+        load_middle = pltpu.make_async_copy(m_ref, result, wsem.at[1])
+        load_grad = pltpu.make_async_copy(mg_ref, tg, wsem.at[2])
+
+        def load_own(zz):
+            return pltpu.make_async_copy(g_ref.at[:, zz], own_buf.at[zz], osem.at[zz])
+
+        load_left(0).start()
+        load_weight.start()
+        for zz in (0, 3, 2, 1):
+            load_own(zz).start()
+        load_left(1).start()
+        load_middle.start()
+        load_grad.start()
+        pl.semaphore_wait(bar, count - 1)
+
+        def up_slot(s, o):
+            return s * 8 + o
+
+        def down_slot(s, o):
+            return 39 - (s * 8 + o)
+
+        def up(s, o, src):
+            return remote(src, UD.at[up_slot(s, o)], us.at[s, o], ur.at[s, o], (me, z + 1))
+
+        def down(s, o, src):
+            return remote(src, UD.at[down_slot(s, o)], ds.at[s, o], dr.at[s, o], (me, z - 1))
+
+        def start_line(s, o):
+            q = partner(o)
+
+            @pl.when(z == 0)
+            def _():
+                up(s, o, g_ref.at[q, last - s]).start()
+
+            @pl.when(z == last)
+            def _():
+                down(s, o, g_ref.at[q, s]).start()
+
+        for s in range(last):
+            loop(0, 8, functools.partial(start_line, s))
+        for zz in range(n_z):
+            load_own(zz).wait()
+
+        def sections(q):
+            for a, b in zip(bounds[:-1], bounds[1:]):
+                at = pl.multiple_of(8 * a + q * (b - a), 128)
+                yield pl.ds(a, b - a), in_out.at[:, pl.ds(at, b - a)]
+            yield pl.ds(bounds[-1], 128), dec_out.at[q]
+
+        def deliver(o, slot):
+            @pl.when(o == 0)
+            def _():
+                for src, dst in sections(me):
+                    pltpu.make_async_copy(UD.at[slot, :, src], dst, wsem.at[3]).start()
+
+            @pl.when(o > 0)
+            def _():
+                for src, dst in sections(me):
+                    remote(UD.at[slot, :, src], dst, i_send.at[o - 1], i_recv.at[o - 1], (partner(o), z)).start()
+
+        def add(slot, *others):
+            total = UD[slot].astype(F32)
+            for other in others:
+                total = total + other.astype(F32)
+            UD[slot] = total.astype(BF16)
+
+        def up_tick(i):
+            s, o = i // 8, lax.rem(i, 8)
+            q, u = partner(o), up_slot(s, o)
+
+            @pl.when((z >= 1) & (z <= last - s))
+            def _():
+                remote(UD.at[u], UD.at[u], us.at[s, o], ur.at[s, o], (sib, z)).wait_recv()
+
+            @pl.when((z >= 1) & (z < last - s))
+            def _():
+                add(u, own_buf[last - s, q])
+                up(s, o, UD.at[u]).start()
+
+            @pl.when((z == last) & (s == 0))
+            def _():
+                add(u, own_buf[last, q])
+                deliver(o, u)
+
+            @pl.when((z == 1) & (s == 2))
+            def _():
+                add(u, UD[down_slot(1, o)], own_buf[1, q])
+                deliver(o, u)
+
+        def down_tick(i):
+            s, o = i // 8, lax.rem(i, 8)
+            q, d = partner(o), down_slot(s, o)
+
+            @pl.when((z <= last - 1) & (z >= s))
+            def _():
+                remote(UD.at[d], UD.at[d], ds.at[s, o], dr.at[s, o], (sib, z)).wait_recv()
+
+            @pl.when((z <= last - 1) & (z > s))
+            def _():
+                add(d, own_buf[s, q])
+                down(s, o, UD.at[d]).start()
+
+            @pl.when((z == 0) & (s == 0))
+            def _():
+                add(d, own_buf[0, q])
+                deliver(o, d)
+
+            @pl.when((z == 2) & (s == 2))
+            def _():
+                add(d, UD[up_slot(1, o)], own_buf[2, q])
+                deliver(o, d)
+
+        lag = 4
+        low = 1 - z // 2
+
+        def tick(i):
+            at_up, at_down = i - lag * (1 - low), i - lag * low
+
+            @pl.when((at_up >= 0) & (at_up < 24))
+            def _():
+                up_tick(at_up)
+
+            @pl.when((at_down >= 0) & (at_down < 24))
+            def _():
+                down_tick(at_down)
+
+        def cut(c):
+            return pl.ds(c * part, part)
+
+        def partial(i, write):
+            load_left(i).wait()
+
+            def some(n, _):
+                at = pl.ds(pl.multiple_of(n * tile, tile), tile)
+                write(at, lax.dot_general(L[i % 2], W[at, :], NT, preferred_element_type=F32))
+                return 0
+
+            lax.fori_loop(0, width // tile, some, 0)
+            if i + 2 < 8:
+                load_left(i + 2).start()
+
+        def give(i, k, slot, before):
+            if before is not None:
+                remote(T.at[slot], A.at[before], sa.at[before], ra.at[before], (sib, z)).wait_send()
+
+            def write(at, v):
+                T[slot, :, at] = v.astype(BF16)
+
+            partial(i, write)
+            remote(T.at[slot], A.at[k], sa.at[k], ra.at[k], (sib, z)).start()
+
+        def got(k):
+            remote(T.at[0], A.at[k], sa.at[k], ra.at[k], (sib, z)).wait_recv()
+
+        def ship(k, c, d):
+            return remote(B.at[k, cut(c)], R.at[k, cut(c)], sb.at[k, c], rb.at[k, c], (d, z))
+
+        def ship7(k, c, d):
+            return remote(B7.at[k, cut(c)], R7.at[k, cut(c)], sb7.at[k, c], rb7.at[k, c], (d, z))
+
+        def send_sum(i, k):
+            got(k)
+
+            def write(at, v):
+                B[k, :, at] = (v + A[k, :, at].astype(F32)).astype(BF16)
+
+            partial(i, write)
+            for c in range(chunks):
+                ship(k, c, nf).start()
+
+        def keep_sum(i, k):
+            got(k)
+
+            def write(at, v):
+                S[:, at] = v + A[k, :, at].astype(F32)
+
+            partial(i, write)
+
+        def second_hop():
+            for c in range(chunks):
+                ship(0, c, nf).wait_recv()
+                B[1, cut(c)] = (S[cut(c)] + R[0, cut(c)].astype(F32)).astype(BF16)
+                ship(1, c, ng).start()
+
+        def give7(k):
+            return remote(b_ref.at[theirs[k]], A7.at[k], sa7.at[k], ra7.at[k], (sib, z))
+
+        def mine7(k):
+            return pltpu.make_async_copy(b_ref.at[mine[k]], X7 if k == 3 else B7.at[k], mine_sem.at[k])
+
+        def start7():
+            for k in (0, 2, 1, 3):
+                give7(k).start()
+                mine7(k).start()
+
+        def send7(k):
+            mine7(k).wait()
+            give7(k).wait_recv()
+            for c in range(chunks):
+                B7[k, cut(c)] = (B7[k, cut(c)].astype(F32) + A7[k, cut(c)].astype(F32)).astype(BF16)
+                ship7(k, c, nf).start()
+
+        def second_hop7():
+            mine7(1).wait()
+            give7(1).wait_recv()
+            for c in range(chunks):
+                ship7(0, c, nf).wait_recv()
+                sl = cut(c)
+                B7[1, sl] = (B7[1, sl].astype(F32) + A7[1, sl].astype(F32) + R7[0, sl].astype(F32)).astype(BF16)
+                ship7(1, c, ng).start()
+
+        small = 32
+
+        def finish_rows():
+            load_grad.wait()
+            line_buf[...] = lines_ref[...]
+            line_buf[0:1] = jnp.zeros((1, width), F32)
+            gains = gain_ref[...]
+            for c in range(chunks):
+                ship(2, c, nf).wait_recv()
+                ship(1, c, ng).wait_recv()
+
+                def some(r, _):
+                    sl = pl.ds(pl.multiple_of(c * part + r * small, small), small)
+                    total = S[sl] + R[2, sl].astype(F32) + R[1, sl].astype(F32)
+                    v = t_ref[sl].astype(F32)
+                    root = lax.rsqrt(jnp.mean(v * v, axis=-1, keepdims=True) + EPSILON)
+                    hat = v * root
+                    scaled = total * gains
+                    line_buf[0:1] += jnp.sum(total * hat, axis=0, keepdims=True)
+                    tg[sl] += root * (scaled - hat * jnp.mean(scaled * hat, axis=-1, keepdims=True))
+                    return 0
+
+                lax.fori_loop(0, part // small, some, 0)
+
+        def finish7():
+            load_middle.wait()
+            mine7(3).wait()
+            give7(3).wait_recv()
+            for c in range(chunks):
+                ship7(2, c, nf).wait_recv()
+                ship7(1, c, ng).wait_recv()
+
+                def some(r, _):
+                    sl = pl.ds(pl.multiple_of(c * part + r * small, small), small)
+                    result[sl] += (
+                        X7[sl].astype(F32) + A7[3, sl].astype(F32) + R7[2, sl].astype(F32) + R7[1, sl].astype(F32)
+                    )
+                    return 0
+
+                lax.fori_loop(0, part // small, some, 0)
+
+        def line_part(d):
+            return line_buf.at[:, pl.ds(pl.multiple_of((d // per) * 128, 128), 128)]
+
+        def conv_part(d):
+            return conv_ref.at[:, pl.ds(pl.multiple_of(d * conv_cols, conv_cols), conv_cols)]
+
+        def packet(o):
+            d = lax.rem(flat + o, count)
+            return remote(line_part(d), lines_out.at[flat], p_send.at[o - 1], p_recv.at[o - 1], anyone(o))
+
+        def conv_packet(o):
+            d = lax.rem(flat + o, count)
+            return remote(conv_part(d), conv_out.at[flat], c_send.at[o - 1], c_recv.at[o - 1], anyone(o))
+
+        keep_line = pltpu.make_async_copy(line_part(flat), lines_out.at[flat], wsem.at[4])
+        keep_conv = pltpu.make_async_copy(conv_part(flat), conv_out.at[flat], wsem.at[5])
+        keep_up = pltpu.make_async_copy(u_ref.at[me], u_out.at[me], wsem.at[6])
+
+        def unit_piece(o):
+            q = partner(o)
+            return remote(u_ref.at[q], u_out.at[me], u_send.at[o - 1], u_recv.at[o - 1], (q, z))
+
+        def send_packets():
+            keep_line.start()
+            loop(1, count, lambda o: packet(o).start())
+
+        def others():
+            keep_conv.start()
+            keep_up.start()
+            loop(1, count, lambda o: conv_packet(o).start())
+
+        def first_work():
+            load_weight.wait()
+            give(0, 0, 0, None)
+            give(1, 2, 1, None)
+
+        work = (
+            first_work,
+            lambda: (send_sum(2, 0), give(3, 1, 0, 0)),
+            lambda: (send_sum(4, 2), give(5, 3, 1, 2), start7()),
+            lambda: (keep_sum(6, 1), others()),
+            lambda: (second_hop(), keep_sum(7, 3)),
+            lambda: (send7(0), send7(2)),
+            lambda: finish_rows(),
+            lambda: (send_packets(), loop(1, 8, lambda o: unit_piece(o).start())),
+            lambda: second_hop7(),
+            lambda: None,
+            lambda: finish7(),
+            lambda: None,
+            lambda: None,
+            lambda: None,
+        )
+        for g, item in enumerate(work):
+            item()
+            loop(2 * g, 2 * g + 2, tick)
+
+        def line_sent(s, o):
+            @pl.when(z < last - s)
+            def _():
+                up(s, o, UD.at[up_slot(s, o)]).wait_send()
+
+            @pl.when(z > s)
+            def _():
+                down(s, o, UD.at[down_slot(s, o)]).wait_send()
+
+        for s in range(last):
+            loop(0, 8, functools.partial(line_sent, s))
+        for k, slot in ((1, 0), (3, 1)):
+            remote(T.at[slot], A.at[k], sa.at[k], ra.at[k], (sib, z)).wait_send()
+        for k in range(4):
+            give7(k).wait_send()
+        for c in range(chunks):
+            for k in range(3):
+                ship(k, c, nf).wait_send()
+                ship7(k, c, nf).wait_send()
+        piece = UD.at[0]
+
+        def arrived(o):
+            remote(piece, piece, i_send.at[o - 1], i_recv.at[o - 1], (sib, z)).wait()
+
+        pltpu.make_async_copy(piece, piece, wsem.at[3]).wait()
+        loop(1, 8, arrived)
+        loop(1, 8, lambda o: unit_piece(o).wait())
+        loop(1, count, lambda o: packet(o).wait())
+        loop(1, count, lambda o: conv_packet(o).wait())
+        keep_line.wait()
+        keep_conv.wait()
+        keep_up.wait()
+
+    dma = pltpu.SemaphoreType.DMA
+    anywhere, vmem = pl.BlockSpec(memory_space=pl.ANY), pl.BlockSpec(memory_space=pltpu.VMEM)
+    blocks = lambda n: pltpu.VMEM((n, rows, width), BF16)
+    f32_rows = jax.ShapeDtypeStruct((rows, width), F32)
+    return pl.pallas_call(
+        kernel,
+        out_shape=[
+            f32_rows,
+            f32_rows,
+            jax.ShapeDtypeStruct((own, 8 * bounds[-1]), BF16),
+            jax.ShapeDtypeStruct((8, own, 128), BF16),
+            jax.ShapeDtypeStruct((8, own, units), BF16),
+            jax.ShapeDtypeStruct((count, 8, 128), F32),
+            jax.ShapeDtypeStruct((count, conv.shape[0], conv_cols), F32),
+        ],
+        in_specs=[anywhere] * 5 + [vmem, anywhere, anywhere, vmem, vmem, anywhere],
+        out_specs=[vmem, vmem] + [anywhere] * 5,
+        scratch_shapes=[
+            pltpu.VMEM((width, cols), BF16),
+            pltpu.VMEM((2, rows, cols), BF16),
+            pltpu.VMEM((n_z, 8, own, cols), BF16),
+            pltpu.VMEM((40, own, cols), BF16),
+            blocks(2),
+            blocks(4),
+            blocks(3),
+            blocks(3),
+            pltpu.VMEM((rows, width), F32),
+            blocks(4),
+            blocks(3),
+            blocks(3),
+            pltpu.VMEM((rows, width), BF16),
+            pltpu.VMEM((8, width), F32),
+            dma((2,)),
+            dma((7,)),
+            dma((n_z,)),
+            dma((4,)),
+            dma((3, 8)),
+            dma((3, 8)),
+            dma((3, 8)),
+            dma((3, 8)),
+            dma((7,)),
+            dma((7,)),
+            dma((7,)),
+            dma((7,)),
+            dma((count - 1,)),
+            dma((count - 1,)),
+            dma((count - 1,)),
+            dma((count - 1,)),
+            dma((4,)),
+            dma((4,)),
+            dma((3, chunks)),
+            dma((3, chunks)),
+            dma((4,)),
+            dma((4,)),
+            dma((3, chunks)),
+            dma((3, chunks)),
+        ],
+        cost_estimate=busy(120),
+        compiler_params=pltpu.CompilerParams(
+            collective_id=cid, has_side_effects=True, vmem_limit_bytes=60 << 20
+        ),
+    )(grad, left, weight, block, ups, tokens, middle, middle_grad, gain, lines, conv)
+
+
 def gather_small(x, n_dp, n_z, cid):
     rows, cols = x.shape
     count = n_dp * n_z
@@ -1328,12 +1790,11 @@
         a = a.reshape(n_dp, n_z, own_d, a.shape[-1]).transpose(1, 0, 2, 3)
         return lax.psum_scatter(a.reshape(width, -1), "fsdp", scatter_dimension=0, tiled=True)
 
-    def to_owners(a):
-        a = lax.all_to_all(a.reshape(n_dp, own_d, -1), "dp", 0, 0, tiled=True)
-        return a.transpose(1, 0, 2).astype(F32)
-
     down_total = owned_rows(down_grad)
-    upgate_low, upgate_grad, down_total = lax.optimization_barrier((upgate_low, upgate_grad, down_total))
+    block_part = dot(hidden, down_full, out=BF16)
+    upgate_low, upgate_grad, down_total, block_part = lax.optimization_barrier(
+        (upgate_low, upgate_grad, down_total, block_part)
+    )
     upgate_sum = owned_parts(upgate_grad)
     if square:
         middle_grad, middle_all, mixed_grad, second_grad = relay(
@@ -1354,76 +1815,126 @@
         projected, conv_mine, decay_mine, gain, inverse, solved, core, mixed_grad, heads, rows
     )
     projected_low, output_total = lax.optimization_barrier((projected_low, output_total))
+    def upgate_rows(a):
+        return jnp.concatenate(
+            [
+                jnp.concatenate([x, y], axis=2).transpose(1, 0, 2).reshape(own_d, -1)
+                for x, y in (
+                    (a[:, :, :main], a[:, :, 2 * main : main + units]),
+                    (a[:, :, main : 2 * main], a[:, :, main + units :]),
+                )
+            ],
+            axis=1,
+        ).astype(F32)
+
+    def decay_rows(a):
+        a = a.transpose(1, 0, 2).astype(F32)
+        return jnp.concatenate(
+            [a[:, :, :heads].reshape(own_d, -1), a[:, :, heads : 2 * heads].reshape(own_d, -1)], axis=1
+        )
+
     in_grad = dot(normed_all, projected_low, TN, out=BF16)
-    projected_low, in_grad = lax.optimization_barrier((projected_low, in_grad))
-    back_one = dot(projected_low, in_full, NT, out=BF16)
-    in_sum = owned_parts(in_grad)
-    normed_one_grad = total(back_one, 9)
-    hidden, normed_one_grad = lax.optimization_barrier((hidden, normed_one_grad))
-    result = middle + total(dot(hidden, down_full, out=BF16), 7)
-    input_part, first_grad = norm_back(inputs, first_root, first_full, normed_one_grad)
-    tokens_grad = middle_grad + input_part
-
     down_total = down_total.astype(F32)
     output_total = output_total.astype(F32)
-    up_total = to_owners(upgate_sum)
-    upgate_total = jnp.concatenate(
-        [
-            jnp.concatenate([a, b], axis=2).reshape(own_d, -1)
-            for a, b in (
-                (up_total[:, :, :main], up_total[:, :, 2 * main : main + units]),
-                (up_total[:, :, main : 2 * main], up_total[:, :, main + units :]),
-            )
-        ],
-        axis=1,
-    )
-    in_total = to_owners(in_sum)
-    input_total = jnp.concatenate(
-        [in_total[:, :, a:b].reshape(own_d, -1) for a, b in zip(bounds[:-1], bounds[1:])], axis=1
-    )
-    start = bounds[-1]
-    decay_total = jnp.concatenate(
-        [
-            in_total[:, :, start : start + heads].reshape(own_d, -1),
-            in_total[:, :, start + heads : start + 2 * heads].reshape(own_d, -1),
-        ],
-        axis=1,
-    )
-
-    share = key // own_conv, value // own_conv
-    owner = jnp.concatenate(
-        [
-            here * share[0] + jnp.arange(share[0]),
-            (n_dp + here) * share[0] + jnp.arange(share[0]),
-            2 * n_dp * share[0] + here * share[1] + jnp.arange(share[1]),
-        ]
-    )
-    blocks = conv_grad.reshape(taps, -1, own_conv).transpose(1, 0, 2).reshape(-1, taps * own_conv)
-    for_owner = owner[None, :] == jnp.arange(count)[:, None]
-    everyone = jnp.concatenate([gain_grad.reshape(-1), decay_grad[:, :heads].reshape(-1)])
-    packets = jnp.concatenate(
-        [
-            first_grad.reshape(count, own_d),
-            second_grad.reshape(count, own_d),
-            jnp.sum(jnp.where(for_owner[:, :, None], blocks[None], 0.0), axis=1),
-            jnp.broadcast_to(everyone[None], (count, everyone.size)),
-        ],
-        axis=1,
-    )
-    size = packets.shape[1]
-    lines = -(-size // 1024) * 8
-    packets = jnp.pad(packets, ((0, 0), (0, lines * 128 - size))).reshape(count, lines, 128)
-    shared = scatter_small(packets, n_dp, n_z, 10).reshape(count, -1)
-    summed = jnp.sum(shared, axis=0)
-    first_total = summed[:own_d]
-    second_total = summed[own_d : 2 * own_d]
-    start = 2 * own_d + taps * own_conv
-    conv_total = summed[2 * own_d : start].reshape(taps, own_conv)
-    gain_total = summed[start : start + gain_grad.size]
-    start += gain_grad.size
-    scale_bias = jnp.sum(shared[:, start : start + 2 * heads].reshape(n_dp, n_z, 2, heads), axis=1)
-    scale_total = scale_bias[:, 0].reshape(-1)
-    bias_total = scale_bias[:, 1].reshape(-1)
+    if square:
+        lines = jnp.concatenate(
+            [
+                jnp.zeros((1, width), F32),
+                second_grad.reshape(1, width),
+                jnp.tile(gain_grad[:, :128], (1, width // 128)),
+                jnp.tile(gain_grad[:, 128:], (1, width // 128)),
+                jnp.tile(jnp.pad(decay_grad[:, :heads].reshape(1, -1), ((0, 0), (0, 128 - 2 * heads))), (1, width // 128)),
+                jnp.zeros((3, width), F32),
+            ],
+            axis=0,
+        )
+        conv_lines = jnp.zeros((8, n_dp * (2 * key + value)), F32)
+        for at, a, b in (
+            (here * key, 0, key),
+            (n_dp * key + here * key, key, 2 * key),
+            (2 * n_dp * key + here * value, 2 * key, 2 * key + value),
+        ):
+            conv_lines = lax.dynamic_update_slice(conv_lines, conv_grad[:, a:b], (0, at))
+        result, tokens_grad, input_total, decay_total, up_total, lines, conv_lines = conclude(
+            in_grad.reshape(n_dp, n_z, own_d, cols),
+            projected_low.reshape(n_dp, rows, cols),
+            in_full,
+            block_part.reshape(n_dp, rows, width),
+            upgate_sum.reshape(n_dp, own_d, 2 * units),
+            tokens,
+            middle,
+            middle_grad,
+            first_full,
+            lines,
+            conv_lines,
+            bounds,
+            9,
+        )
+        input_total = input_total.astype(F32)
+        decay_total = decay_rows(decay_total)
+        upgate_total = upgate_rows(up_total)
+        summed = jnp.sum(lines, axis=0)
+        per = 128 // own_d
+        place = lax.rem(flat, per) * own_d
+        first_total = lax.dynamic_slice_in_dim(summed[0], place, own_d)
+        second_total = lax.dynamic_slice_in_dim(summed[1], place, own_d)
+        gain_total = summed[2:4].reshape(-1)
+        scale_bias = jnp.sum(lines[:, 4, : 2 * heads].reshape(n_dp, n_z, 2, heads), axis=1)
+        scale_total = scale_bias[:, 0].reshape(-1)
+        bias_total = scale_bias[:, 1].reshape(-1)
+        conv_total = jnp.sum(conv_lines, axis=0)[:taps]
+    else:
+        projected_low, in_grad = lax.optimization_barrier((projected_low, in_grad))
+        back_one = dot(projected_low, in_full, NT, out=BF16)
+        in_sum = owned_parts(in_grad)
+        normed_one_grad = total(back_one, 9)
+        result = middle + total(block_part, 7)
+        input_part, first_grad = norm_back(inputs, first_root, first_full, normed_one_grad)
+        tokens_grad = middle_grad + input_part
+
+        up_total = lax.all_to_all(upgate_sum.reshape(n_dp, own_d, -1), "dp", 0, 0, tiled=True)
+        upgate_total = upgate_rows(up_total)
+        in_total = lax.all_to_all(in_sum.reshape(n_dp, own_d, -1), "dp", 0, 0, tiled=True)
+        decay_total = decay_rows(in_total[:, :, bounds[-1] :])
+        in_total = in_total.transpose(1, 0, 2).astype(F32)
+        input_total = jnp.concatenate(
+            [in_total[:, :, a:b].reshape(own_d, -1) for a, b in zip(bounds[:-1], bounds[1:])], axis=1
+        )
+
+        share = key // own_conv, value // own_conv
+        owner = jnp.concatenate(
+            [
+                here * share[0] + jnp.arange(share[0]),
+                (n_dp + here) * share[0] + jnp.arange(share[0]),
+                2 * n_dp * share[0] + here * share[1] + jnp.arange(share[1]),
+            ]
+        )
+        blocks = conv_grad.reshape(taps, -1, own_conv).transpose(1, 0, 2).reshape(-1, taps * own_conv)
+        for_owner = owner[None, :] == jnp.arange(count)[:, None]
+        everyone = jnp.concatenate([gain_grad.reshape(-1), decay_grad[:, :heads].reshape(-1)])
+        packets = jnp.concatenate(
+            [
+                first_grad.reshape(count, own_d),
+                second_grad.reshape(count, own_d),
+                jnp.sum(jnp.where(for_owner[:, :, None], blocks[None], 0.0), axis=1),
+                jnp.broadcast_to(everyone[None], (count, everyone.size)),
+            ],
+            axis=1,
+        )
+        size = packets.shape[1]
+        lines = -(-size // 1024) * 8
+        packets = jnp.pad(packets, ((0, 0), (0, lines * 128 - size))).reshape(count, lines, 128)
+        shared = scatter_small(packets, n_dp, n_z, 10).reshape(count, -1)
+        summed = jnp.sum(shared, axis=0)
+        first_total = summed[:own_d]
+        second_total = summed[own_d : 2 * own_d]
+        start = 2 * own_d + taps * own_conv
+        conv_total = summed[2 * own_d : start].reshape(taps, own_conv)
+        gain_total = summed[start : start + gain_grad.size]
+        start += gain_grad.size
+        scale_bias = jnp.sum(shared[:, start : start + 2 * heads].reshape(n_dp, n_z, 2, heads), axis=1)
+        scale_total = scale_bias[:, 0].reshape(-1)
+        bias_total = scale_bias[:, 1].reshape(-1)
     return (
         result,
         tokens_grad,

time: 805 us -> 781 us (0.970)
  Pallas kernels: 533 us -> 579 us
  waiting for transfers between devices: 48 us -> 27.3 us
  other arithmetic: 30 us -> 11.6 us
  matrix products: 106 us -> 89.1 us
    pallas_call x3 -> x1, Pallas kernels: 93.5 us -> 140 us  [conclude(): pl.pallas_call(kernel, out_shape=[f32_rows, f32_rows, jax.ShapeDtypeStruc...]
    dot_general x7 -> x6, matrix products: 106 us -> 89.1 us  [dot(): return lax.dot_general(a, b, dims, preferred_element_type=F32).astype(out)]
    reshape x15 -> x4, local copies, waits for them, and re-layouts: 17.3 us -> 2.81 us  [the longest x2 1.48 us: upgate_rows(): jnp.concatenate([x, y], axis=2).transpose(1, 0, 2).reshape(own_d, -1)]
    all_to_all x2 -> x0, waiting for transfers between devices: 14.3 us -> none  [to_owners(): a = lax.all_to_all(a.reshape(n_dp, own_d, -1), 'dp', 0, 0, tiled=True)]
    reduce_scatter x2, waiting for transfers between devices: 20.5 us -> 11.5 us  [owned_rows(): return lax.psum_scatter(a, 'fsdp', scatter_dimension=0, tiled=True)]
    unnamed x76 -> x74, local copies, waits for them, and re-layouts: 19.3 us -> 21 us
  transfers between devices with their start and end apart: 9 -> 6, of which waited for: 3 -> 2; matrix products, arithmetic and copies ran while one was open for 17% -> 10% of each run, Pallas kernels for 52% -> 41%
where the time goes in v4:
time: 781 us; the launch traced here: 775 us
  Pallas kernels  579 us (74%)
  matrix products  89.1 us (11%)
  local copies, waits for them, and re-layouts  52.4 us (7%)
  waiting for transfers between devices  27.3 us (3%)
  between operations  15.5 us (2%)
  other arithmetic  11.6 us (1%)
    pallas_call x2, Pallas kernels, relay(): pl.pallas_call(kernel, out_shape=out_shape, in_specs=in_specs, out_specs=...  182 us
    pallas_call x1, Pallas kernels, conclude(): pl.pallas_call(kernel, out_shape=[f32_rows, f32_rows, jax.ShapeDtypeStruc...  140 us
    pallas_call x1, Pallas kernels, begin(): pl.pallas_call(kernel, out_shape=[jax.ShapeDtypeStruct((8, n_z, own, cols...  118 us
    dot_general x6, matrix products, dot(): return lax.dot_general(a, b, dims, preferred_element_type=F32).astype(out)  89.1 us
    pallas_call x1, Pallas kernels, mixer_forward(): pl.pallas_call(functools.partial(mixer_forward_kernel, heads), grid=(seqs...  52.7 us
    pallas_call x1, Pallas kernels, mixer_backward(): pl.pallas_call(functools.partial(mixer_backward_kernel, heads), grid=(seq...  50.3 us
    unnamed x74, local copies, waits for them, and re-layouts  21 us
    pallas_call x1, Pallas kernels, units_forward(): pl.pallas_call(kernel, grid=(blocks,), in_specs=[row(width), whole(weight...  20 us
  transfers between devices with their start and end apart: 6, of which 2 were waited for; matrix products, arithmetic and copies ran while one was open for 10% of the time, Pallas kernels for 41%

profile of v4, /device:TPU:0, one launch (start us, length us, event | category | flops | bytes accessed | tf_op | source)
XLA Modules:
  0.0 775.1 jit_solution(14659243575119348618)
XLA Ops:
  7.2 1.4 fusion.4
  8.7 0.7 reshape.181
  9.4 0.7 slice.126
  10.1 0.7 reshape.182
  10.8 0.7 slice.127
  11.6 0.8 copy.58
  12.5 0.9 copy.74
  13.5 1.6 copy.76
  15.9 2.7 concatenate.28
  18.8 1.4 copy-done.4
  20.2 1.2 copy-done.5
  21.4 117.7 %shard_map.237 = (bf16[8,4,64,1664]{3,2,1,0:T(8,128)(2,1)S(1)}, bf16[8,64,1408]{2,1,0:T(8,128)(2,1)}, bf16[8,256,2048]{2,1,0:T(8,128)(2,1)S(1)}, bf16[8,256,2048]{2,1,0:T(8,128)(2,1)}, bf16[32,16,128]{2,1,0:T(8,128)(2,1)S(1)}) custom-call(bf16[64,12288]{1,0:T(8,128)(2,1)S(1)} %copy-done.4, bf16[8,64,128]{2,1,0:T(8,128)(2,1)S(1)} %maximum_bitcast_fusion.2.dec_ref, ...), custom_call_target="tpu_custom_call" | custom-call | flops 149999992832 | tf_op jit(solution)/shard_map/pallas_call | solution.py:672
  139.1 3.2 copy-done.7
  142.4 2.8 copy-done.8
  145.2 0.7 all-gather.9.cloned.1.call-update
  145.9 0.7 all-gather.7.cloned.1.call-update
  146.7 0.7 convert_reduce_fusion
  147.4 0.7 convert_reduce_fusion.1
  148.2 0.7 reshape.208.gain_ref
  149.1 21.5 %fusion.9.proj_ref = f32[2048,1664]{1,0:T(8,128)} fusion(bf16[2048,2048]{1,0:T(8,128)(2,1)} %bitcast.83, bf16[2048,1664]{1,0:T(8,128)(2,1)} %bitcast.85), kind=kOutput, calls=%fused_computation.44 | convolution fusion | flops 13958643712 | bytes 28835840 | tf_op jit(solution)/shard_map/dot_general | solution.py:1605
  170.9 52.7 %shard_map.238 = (bf16[2048,512]{1,0:T(8,128)(2,1)S(1)}, f32[8,2,256,256]{3,2,1,0:T(8,128)}, f32[2048,512]{1,0:T(8,128)}, f32[2048,512]{1,0:T(8,128)}) custom-call(f32[2048,1664]{1,0:T(8,128)} %fusion.9.proj_ref, f32[4,1024]{1,0:T(4,128)S(1)} %maximum_convert_fusion.1.taps_ref, f32[2,128]{1,0:T(2,128)S(1)} %select_maximum_fusion.decay_ref, f32[1,256]{1,0:T(1,128)S(1)} %bitcast.82), custom_call_target="tpu_custom_call" | custom-call | flops 54999998464 | tf_op jit(solution)/shard_map/pallas_call | solution.py:162
  223.6 0.6 copy-done.1
  224.2 1.3 copy-done.9
  225.5 89.1 %shard_map.239 = (f32[256,2048]{1,0:T(8,128)}, bf16[8,256,2048]{2,1,0:T(8,128)(2,1)}) custom-call(bf16[8,256,512]{2,1,0:T(8,128)(2,1)} %bitcast.87, bf16[512,2048]{1,0:T(8,128)(2,1)} %all-gather.5.cloned.1.call-done.first_ref.refs_2_, f32[1,2048]{1,0:T(1,128)} %reshape.208.gain_ref, bf16[256,2048]{1,0:T(8,128)(2,1)} %t_ref.3), custom_call_target="tpu_custom_call" | custom-call | flops 80000000000 | tf_op jit(solution)/shard_map/pallas_call | solution.py:929
  314.8 20.0 %shard_map.240 = (f32[2048,1408]{1,0:T(8,128)}, bf16[2048,704]{1,0:T(8,128)(2,1)S(1)}, bf16[2048,704]{1,0:T(8,128)(2,1)}) custom-call(bf16[2048,2048]{1,0:T(8,128)(2,1)} %bitcast.108, bf16[2048,1408]{1,0:T(8,128)(2,1)} %bitcast.102, f32[8,128]{1,0:T(8,128)S(1)} %broadcast_in_dim.45.s_ref), custom_call_target="tpu_custom_call" | custom-call | flops 20000000000 | tf_op jit(solution)/shard_map/pallas_call | solution.py:988
  334.8 1.7 copy-done.11
  336.4 9.4 %convolution_convert_fusion.3 = bf16[704,2048]{1,0:T(8,128)(2,1)} fusion(bf16[2048,704]{1,0:T(8,128)(2,1)} %get-tuple-element.69, bf16[2048,2048]{1,0:T(8,128)(2,1)S(1)} %bitcast.106), kind=kOutput, calls=%fused_computation.3 | convolution fusion | flops 5907021824 | bytes 14155776 | tf_op jit(solution)/shard_map/dot_general | solution.py:1605
  345.9 14.3 %all-gather.7.cloned.1.call-done.w_ref = bf16[704,2048]{1,0:T(8,128)(2,1)} async-done(((bf16[176,2048]{1,0:T(8,128)(2,1)}), bf16[704,2048]{1,0:T(8,128)(2,1)}) %all-gather.7.cloned.1.call-update) | async-done | bytes 2883600 | tf_op jit(solution)/shard_map/all_gather | solution.py:1712
  360.2 1.8 copy-done.3
  362.0 16.2 %shard_map.241 = bf16[2048,1408]{1,0:T(8,128)(2,1)} custom-call(bf16[2048,2048]{1,0:T(8,128)(2,1)} %bitcast.105, bf16[704,2048]{1,0:T(8,128)(2,1)S(1)} %copy-done.3, f32[2048,1408]{1,0:T(8,128)} %get-tuple-element.73.up_ref, f32[8,128]{1,0:T(8,128)S(1)} %broadcast_in_dim.45.s_ref), custom_call_target="tpu_custom_call" | custom-call | flops 12000000000 | tf_op jit(solution)/shard_map/pallas_call | solution.py:1027
  378.2 19.2 %convolution_convert_fusion.2 = bf16[2048,1408]{1,0:T(8,128)(2,1)} fusion(bf16[2048,2048]{1,0:T(8,128)(2,1)} %bitcast.109, bf16[2048,1408]{1,0:T(8,128)(2,1)} %shard_map.241), kind=kOutput, calls=%fused_computation.2 | convolution fusion | flops 11814043648 | bytes 19922944 | tf_op jit(solution)/shard_map/dot_general | solution.py:1605
  397.4 8.9 %convolution_convert_fusion = bf16[2048,2048]{1,0:T(8,128)(2,1)} fusion(bf16[2048,704]{1,0:T(8,128)(2,1)S(1)} %copy-done.12, bf16[704,2048]{1,0:T(8,128)(2,1)S(1)} %copy-done.3), kind=kOutput, calls=%fused_computation | convolution fusion | flops 5909774336 | bytes 14155776 | tf_op jit(solution)/shard_map/dot_general | solution.py:1605
  406.2 11.5 %reduce-scatter.4.cloned.1.call-done = bf16[176,2048]{1,0:T(8,128)(2,1)} async-done(((bf16[704,2048]{1,0:T(8,128)(2,1)}), bf16[176,2048]{1,0:T(8,128)(2,1)}) %reduce-scatter.4.cloned.1.call-update) | async-done | bytes 720912 | tf_op jit(solution)/shard_map/reduce_scatter | solution.py:1787
  417.8 5.7 copy.65
  423.6 0.6 copy-done.23
  424.2 0.7 reshape.210.gain_ref
  424.9 1.3 dynamic_slice.39
  426.2 2.2 convert_multiply_fusion.refs_1_
  428.4 1.3 convert_element_type.93
  429.7 93.1 %shard_map.242 = (f32[256,2048]{1,0:T(8,128)}, bf16[8,256,2048]{2,1,0:T(8,128)(2,1)}, f32[8,256,512]{2,1,0:T(8,128)}, f32[1,2048]{1,0:T(1,128)}) custom-call(bf16[8,256,1408]{2,1,0:T(8,128)(2,1)} %bitcast.113, bf16[2048,1408]{1,0:T(8,128)(2,1)} %bitcast.103, f32[1,2048]{1,0:T(1,128)} %reshape.208.gain_ref, f32[256,2048]{1,0:T(8,128)} %get-tuple-element.79.refs_0_.m_ref, ...), custom_call_target="tpu_custom_call" | custom-call | flops 80000000000 | tf_op jit(solution)/shard_map/pallas_call | solution.py:929
  522.7 9.2 %convolution_convert_fusion.4 = bf16[512,2048]{1,0:T(8,128)(2,1)} fusion(bf16[2048,512]{1,0:T(8,128)(2,1)S(1)} %copy-done.10, bf16[2048,2048]{1,0:T(8,128)(2,1)} %bitcast.110), kind=kOutput, calls=%fused_computation.4 | convolution fusion | flops 4296015872 | bytes 12582912 | tf_op jit(solution)/shard_map/dot_general | solution.py:1605
  532.0 50.3 %shard_map.243 = (bf16[2048,1664]{1,0:T(8,128)(2,1)}, f32[4,1024]{1,0:T(4,128)}, f32[1,256]{1,0:T(1,128)}, f32[2,128]{1,0:T(2,128)}) custom-call(f32[2048,1664]{1,0:T(8,128)} %fusion.9.proj_ref, f32[4,1024]{1,0:T(4,128)} %copy-done.1, f32[2,128]{1,0:T(2,128)} %copy-done.2, f32[1,256]{1,0:T(1,128)} %bitcast.81, f32[8,2,256,256]{3,2,1,0:T(8,128)} %get-tuple-element.61.inv_ref, ...), custom_call_target="tpu_custom_call" | custom-call | flops 49999998976 | tf_op jit(solution)/shard_map/pallas_call | solution.py:285
  582.3 0.8 reshape.202
  583.1 0.7 slice_bitcast_fusion.1
  583.8 0.7 concatenate.31.lines_ref
  584.5 0.7 slice_dynamic-update-slice_fusion.2
  585.2 0.7 slice_dynamic-update-slice_fusion.1
  585.9 0.7 slice_dynamic-update-slice_fusion.conv_ref
  586.6 21.1 %convolution_convert_fusion.1 = bf16[2048,1664]{1,0:T(8,128)(2,1)} fusion(bf16[2048,2048]{1,0:T(8,128)(2,1)} %bitcast.84, bf16[2048,1664]{1,0:T(8,128)(2,1)} %get-tuple-element.86), kind=kOutput, calls=%fused_computation.1 | convolution fusion | flops 13962051584 | bytes 22020096 | tf_op jit(solution)/shard_map/dot_general | solution.py:1605
  607.7 139.8 %shard_map.244 = (f32[256,2048]{1,0:T(8,128)}, f32[256,2048]{1,0:T(8,128)}, bf16[64,12288]{1,0:T(8,128)(2,1)}, bf16[8,64,128]{2,1,0:T(8,128)(2,1)}, bf16[8,64,14...) custom-call(bf16[8,4,64,1664]{3,2,1,0:T(8,128)(2,1)} %bitcast.112, ...), custom_call_target="tpu_custom_call" | custom-call | flops 120000004096 | tf_op jit(solution)/shard_map/pallas_call | solution.py:1440
  747.5 0.9 reduce_sum.37
  748.4 1.0 slice.115
  750.0 1.1 fusion.3
  751.1 1.4 fusion.2
  752.6 1.9 convert_element_type.88
  755.9 0.6 reshape_squeeze.12
  757.2 1.1 convert_element_type.91
  760.0 0.7 reshape.207
  761.2 0.7 reshape.206
  762.0 0.6 pad_maximum_fusion
  762.6 1.8 maximum_convert_fusion
  764.4 1.3 copy.87
  765.7 1.0 copy-done.13
  766.7 1.3 copy.88
  (125 shorter events, 6.6 us)
Async XLA Ops:
  7.2 218.3 %all-gather.5.cloned.1.call-start = ((), (), s32[]{:S(2)}) async-start(), calls=%async_computation.3 | async-start | bytes 2621440 | tf_op jit(solution)/shard_map/all_gather | solution.py:1710
  8.6 2.8 copy-start.26
  10.1 5.7 copy-start.27
  10.7 2.7 copy-start.18
  12.5 3.4 copy-start.19
  12.5 6.2 copy-start.28
  12.5 6.2 copy-start.29
  12.5 6.3 copy-start
  18.8 1.4 copy-start.4
  20.2 1.2 copy-start.5
  139.1 3.2 copy-start.7
  142.4 2.8 copy-start.8
  145.2 169.5 %all-gather.9.cloned.1.call-start = ((), (), s32[]{:S(2)}) async-start(), calls=%async_computation.8 | async-start | bytes 7208960 | tf_op jit(solution)/shard_map/all_gather | solution.py:1670
  145.9 214.3 %all-gather.7.cloned.1.call-start = ((), (), s32[]{:S(2)}) async-start(), calls=%async_computation.4 | async-start | bytes 3604480 | tf_op jit(solution)/shard_map/all_gather | solution.py:1712
  146.6 271.1 %reduce-scatter.4.cloned.1.call-start = ((), (), s32[]{:S(2)}) async-start(), calls=%async_computation.5 | async-start | bytes 3604480 | tf_op jit(solution)/shard_map/reduce_scatter | solution.py:1787
  149.0 21.6 %copy-start.24 = (f32[8,4]{1,0:T(8,128)}, f32[8,4]{1,0:T(8,128)S(1)}, u32[]{:S(2)}) copy-start(f32[8,4]{1,0:T(8,128)S(1)} %div.11) | copy-start | bytes 388
  149.0 21.5 %copy-start.30 = (f32[16]{0:T(128)S(1)}, f32[16]{0:T(128)}, u32[]{:S(2)}) copy-start(f32[16]{0:T(128)} %param.22) | copy-start | bytes 196
  149.0 21.5 %copy-start.31 = (f32[16]{0:T(128)S(1)}, f32[16]{0:T(128)}, u32[]{:S(2)}) copy-start(f32[16]{0:T(128)} %param.21) | copy-start | bytes 196
  149.0 21.8 %copy-start.6 = (f32[256]{0:T(256)S(1)}, f32[256]{0:T(256)}, u32[]{:S(2)}) copy-start(f32[256]{0:T(256)} %param.23) | copy-start | bytes 3076
  170.7 52.9 %copy-start.2 = (f32[2,128]{1,0:T(2,128)}, f32[2,128]{1,0:T(2,128)S(1)}, u32[]{:S(2)}) copy-start(f32[2,128]{1,0:T(2,128)S(1)} %select_maximum_fusion.decay_ref) | copy-start | bytes 3076
  223.6 0.6 copy-start.1
  224.2 1.3 copy-start.9
  314.7 21.7 %copy-start.32 = (bf16[8,256,2048]{2,1,0:T(8,128)(2,1)S(1)}, bf16[8,256,2048]{2,1,0:T(8,128)(2,1)}, u32[]{:S(2)}) copy-start(bf16[8,256,2048]{2,1,0:T(8,128)(2,1)} %get-tuple-element.70) | copy-start | bytes 25165828
  334.8 1.7 copy-start.11
  345.8 186.1 %reduce-scatter.6.cloned.1.call-start = ((), (), s32[]{:S(2)}) async-start(), calls=%async_computation.6 | async-start | bytes 7208960 | tf_op jit(solution)/shard_map/reduce_scatter | solution.py:1791
  360.2 1.8 copy-start.3
  378.2 19.2 %copy-start.12 = (bf16[2048,704]{1,0:T(8,128)(2,1)S(1)}, bf16[2048,704]{1,0:T(8,128)(2,1)}, u32[]{:S(2)}) copy-start(bf16[2048,704]{1,0:T(8,128)(2,1)} %copy-done.11) | copy-start | bytes 8650756
  423.5 0.7 copy-start.23
  423.5 4.9 copy-start.16
  423.6 163.1 %reduce-scatter.8.cloned.1.call-start = ((), (), s32[]{:S(2)}) async-start(), calls=%async_computation.7 | async-start | bytes 2621440 | tf_op jit(solution)/shard_map/reduce_scatter | solution.py:1787
  429.7 93.1 %copy-start.10 = (bf16[2048,512]{1,0:T(8,128)(2,1)S(1)}, bf16[2048,512]{1,0:T(8,128)(2,1)}, u32[]{:S(2)}) copy-start(bf16[2048,512]{1,0:T(8,128)(2,1)} %copy-done.9) | copy-start | bytes 6291460
  532.0 51.8 %copy-start.25 = (f32[1,2048]{1,0:T(1,128)S(1)}, f32[1,2048]{1,0:T(1,128)}, u32[]{:S(2)}) copy-start(f32[1,2048]{1,0:T(1,128)} %get-tuple-element.90) | copy-start | bytes 24580
  586.6 21.1 %copy-start.21 = (f32[8,8192]{1,0:T(8,128)}, f32[8,8192]{1,0:T(8,128)S(1)}, u32[]{:S(2)}) copy-start(f32[8,8192]{1,0:T(8,128)S(1)} %slice_dynamic-update-slice_fusion.conv_ref) | copy-start | bytes 786436
  748.4 4.2 copy-start.15
  751.1 3.4 copy-start.22
  752.6 2.3 copy-start.20
  752.6 4.6 copy-start.17
  762.0 2.4 copy-start.14
  764.4 2.3 copy-start.13
Sparse Core Ops, SparseCore 0:
  145.3 48.7 all-gather.4
  195.7 105.4 all-gather.8
  302.7 57.4 all-gather.6
  362.9 54.8 reduce-scatter.3
  423.7 102.1 reduce-scatter.5
  532.1 43.2 reduce-scatter.7

commit v5 on v4

--- a/solution.py
+++ b/solution.py
@@ -40,33 +40,42 @@
     return total
 
 
-def dot6(a, b, dims=NN):
-    return lax.dot_general(a, b, dims, precision=lax.Precision.HIGHEST, preferred_element_type=F32)
-
-
-def shift_down(v, n, rows):
-    if n == 0:
-        return v
-    return jnp.where(rows >= n, pltpu.roll(v, n, 0), 0.0)
-
-
-def shift_up(v, n, rows):
-    if n == 0:
-        return v
+def sum_rows(mask, b):
+    mask = jnp.where(mask, 1.0, 0.0).astype(BF16)
+    high = b.astype(BF16)
+    rest = b - high.astype(F32)
+    middle = rest.astype(BF16)
+    low = (rest - middle.astype(F32)).astype(BF16)
+    return dot1(mask, high) + (dot1(mask, middle) + dot1(mask, low))
+
+
+def shift_down(v, n):
+    turned = pltpu.roll(v, n, 0)
+    places = lax.broadcasted_iota(jnp.int32, (8, 1), 0)
+    return jnp.concatenate([jnp.where(places >= n, turned[:8], 0.0), turned[8:]], axis=0)
+
+
+def shift_up(v, n):
     length = v.shape[0]
-    return jnp.where(rows < length - n, pltpu.roll(v, length - n, 0), 0.0)
-
-
-def conv(c, taps, rows):
+    turned = pltpu.roll(v, length - n, 0)
+    places = lax.broadcasted_iota(jnp.int32, (8, 1), 0)
+    return jnp.concatenate([turned[:-8], jnp.where(places < 8 - n, turned[-8:], 0.0)], axis=0)
+
+
+def conv(c, taps):
     count = taps.shape[0]
     total = c * taps[count - 1 : count]
     for j in range(count - 1):
-        total = total + shift_down(c, count - 1 - j, rows) * taps[j : j + 1]
+        total = total + shift_down(c, count - 1 - j) * taps[j : j + 1]
     return total
 
 
 def sigmoid(v):
     return 1.0 / (1.0 + jnp.exp(-v))
+
+
+def gate_of(v):
+    return 0.5 * jnp.tanh(0.5 * v) + 0.5
 
 
 def softplus(v):
@@ -94,17 +103,16 @@
     return inverses
 
 
-def common(proj, decay, heads, length):
+def common(raw, decay, heads, length):
     rows = lax.broadcasted_iota(jnp.int32, (length, 1), 0)
     row_ids = lax.broadcasted_iota(jnp.int32, (length, length), 0)
     col_ids = lax.broadcasted_iota(jnp.int32, (length, length), 1)
-    raw = proj[:, heads * 768 :]
     lanes = lax.broadcasted_iota(jnp.int32, raw.shape, 1)
     shifted = raw + decay[1:2]
     rate = jnp.where(lanes < heads, -jnp.exp(decay[0:1]) * softplus(shifted), 0.0)
     beta = sigmoid(raw)
-    cumulated = dot6(jnp.where(row_ids >= col_ids, 1.0, 0.0), rate)
-    return rows, row_ids, col_ids, raw, lanes, shifted, rate, beta, cumulated, cumulated.T
+    cumulated = sum_rows(row_ids >= col_ids, rate)
+    return rows, row_ids, col_ids, lanes, shifted, rate, beta, cumulated, cumulated.T
 
 
 def head_parts(h, heads):
@@ -115,16 +123,16 @@
     return key, keyk, val, gat
 
 
-def mixer_forward_kernel(heads, proj_ref, taps_ref, decay_ref, gain_ref, mixed_ref, inv_ref, solved_ref, core_ref):
+def mixer_forward_kernel(heads, proj_ref, raw_ref, taps_ref, decay_ref, gain_ref, mixed_ref, inv_ref, solved_ref, core_ref, conv_ref):
     length = proj_ref.shape[0]
     decay = decay_ref[...]
     gain = gain_ref[...]
-    rows, row_ids, col_ids, raw, lanes, shifted, rate, beta, cumulated, cum_t = common(
-        proj_ref[...], decay, heads, length
-    )
+    raw = raw_ref[...]
+    rows, row_ids, col_ids, lanes, shifted, rate, beta, cumulated, cum_t = common(raw, decay, heads, length)
     def active(cols):
-        y = conv(proj_ref[:, cols], taps_ref[:, cols], rows)
-        return y * sigmoid(y)
+        y = conv(proj_ref[:, cols], taps_ref[:, cols])
+        conv_ref[:, cols] = y
+        return y * gate_of(y)
 
     parts = [head_parts(h, heads) for h in range(heads)]
     queries, keys, values, growths, betas, lowers = [], [], [], [], [], []
@@ -150,10 +158,10 @@
         core_ref[:, h * DV : (h + 1) * DV] = core
         gate = proj_ref[:, gs]
         normed = core * lax.rsqrt(jnp.mean(core * core, axis=-1, keepdims=True) + EPSILON) * gain
-        mixed_ref[:, h * DV : (h + 1) * DV] = (normed * (gate * sigmoid(gate))).astype(BF16)
-
-
-def mixer_forward(proj, taps, decay, gain, heads, length):
+        mixed_ref[:, h * DV : (h + 1) * DV] = (normed * (gate * gate_of(gate))).astype(BF16)
+
+
+def mixer_forward(proj, raw, taps, decay, gain, heads, length):
     tokens, width = proj.shape
     seqs = tokens // length
     hv = heads * DV
@@ -162,29 +170,29 @@
     return pl.pallas_call(
         functools.partial(mixer_forward_kernel, heads),
         grid=(seqs,),
-        in_specs=[row(width), whole(taps), whole(decay), whole(gain)],
-        out_specs=[row(hv), pl.BlockSpec((None, heads, length, length), lambda s: (s, 0, 0, 0)), row(hv), row(hv)],
+        in_specs=[row(width), row(128), whole(taps), whole(decay), whole(gain)],
+        out_specs=[row(hv), pl.BlockSpec((None, heads, length, length), lambda s: (s, 0, 0, 0)), row(hv), row(hv), row(taps.shape[1])],
         out_shape=[
             jax.ShapeDtypeStruct((tokens, hv), BF16),
             jax.ShapeDtypeStruct((seqs, heads, length, length), F32),
             jax.ShapeDtypeStruct((tokens, hv), F32),
             jax.ShapeDtypeStruct((tokens, hv), F32),
+            jax.ShapeDtypeStruct((tokens, taps.shape[1]), F32),
         ],
         cost_estimate=busy(55), compiler_params=pltpu.CompilerParams(vmem_limit_bytes=48 << 20),
-    )(proj, taps, decay, gain)
+    )(proj, raw, taps, decay, gain)
 
 
 def mixer_backward_kernel(
-    heads, proj_ref, taps_ref, decay_ref, gain_ref, inv_ref, solved_ref, core_ref, grad_ref,
-    low_ref, conv_ref, gain_grad_ref, decay_grad_ref,
+    heads, proj_ref, raw_ref, taps_ref, decay_ref, gain_ref, inv_ref, solved_ref, core_ref, pre_ref, grad_ref,
+    low_ref, raw_low_ref, conv_ref, gain_grad_ref, decay_grad_ref,
 ):
     length = proj_ref.shape[0]
     count = taps_ref.shape[0]
     decay = decay_ref[...]
     gain = gain_ref[...]
-    rows, row_ids, col_ids, raw, lanes, shifted, rate, beta, cumulated, cum_t = common(
-        proj_ref[...], decay, heads, length
-    )
+    raw = raw_ref[...]
+    rows, row_ids, col_ids, lanes, shifted, rate, beta, cumulated, cum_t = common(raw, decay, heads, length)
     within = row_ids >= col_ids
     strict = row_ids > col_ids
 
@@ -201,8 +209,8 @@
         hs = slice(h * DV, (h + 1) * DV)
 
         def active(cols):
-            y = conv(proj_ref[:, cols], taps_ref[:, cols], rows)
-            s = sigmoid(y)
+            y = pre_ref[:, cols]
+            s = gate_of(y)
             return y * s, s * (1.0 + y * (1.0 - s))
 
         def conv_back(cols, grad):
@@ -211,13 +219,14 @@
             conv_ref[count - 1 : count, cols] += jnp.sum(grad * c, axis=0, keepdims=True)
             for j in range(count - 1):
                 n = count - 1 - j
-                total = total + shift_up(grad, n, rows) * taps_ref[j : j + 1, cols]
-                conv_ref[j : j + 1, cols] += jnp.sum(grad * shift_down(c, n, rows), axis=0, keepdims=True)
+                later = shift_up(grad, n)
+                total = total + later * taps_ref[j : j + 1, cols]
+                conv_ref[j : j + 1, cols] += jnp.sum(later * c, axis=0, keepdims=True)
             low_ref[:, cols] = total.astype(BF16)
 
         core = core_ref[:, hs]
         gate = proj_ref[:, gs]
-        gate_sig = sigmoid(gate)
+        gate_sig = gate_of(gate)
         grad = grad_ref[:, hs]
         root = lax.rsqrt(jnp.mean(core * core, axis=-1, keepdims=True) + EPSILON)
         normed = core * root
@@ -244,10 +253,11 @@
         weights = growth * dot1(q, k, NT)
         inverse = inv_ref[h]
         solved = solved_ref[:, hs]
-        solved_grad = dot3(weights, core_grad, TN)
-        weights_grad = dot3(core_grad, solved, NT)
-        value_grad = dot3(inverse, solved_grad, TN)
-        lower_grad = jnp.where(strict, -dot3(value_grad, solved, NT), 0.0)
+        core_low = core_grad.astype(BF16)
+        solved_grad = dot3(weights, core_low, TN)
+        weights_grad = dot3(core_low, solved, NT)
+        value_grad = dot3(inverse, solved_grad.astype(BF16), TN)
+        lower_grad = jnp.where(strict, -dot3(value_grad.astype(BF16), solved, NT), 0.0)
         gap_part = lower_grad * decayed_gram
         beta_col = jnp.sum(gap_part, axis=-1, keepdims=True) + jnp.sum(value_grad * v, axis=-1, keepdims=True)
         gap_grad = gap_part * beta_h + weights_grad * weights
@@ -268,15 +278,15 @@
         conv_back(ks, k_grad * k_slope)
         conv_back(vs, value_grad * beta_h * v_slope)
 
-    rate_grad = dot6(jnp.where(col_ids >= row_ids, 1.0, 0.0), cum_grad)
+    rate_grad = sum_rows(col_ids >= row_ids, cum_grad)
     bias_part = rate_grad * -jnp.exp(decay[0:1]) * sigmoid(shifted)
     raw_grad = jnp.where(lanes < heads, bias_part, beta_grad * beta * (1.0 - beta))
-    low_ref[:, heads * 768 :] = raw_grad.astype(BF16)
+    raw_low_ref[...] = raw_grad.astype(BF16)
     decay_grad_ref[0:1] += jnp.sum(jnp.where(lanes < heads, rate_grad * rate, 0.0), axis=0, keepdims=True)
     decay_grad_ref[1:2] += jnp.sum(jnp.where(lanes < heads, bias_part, 0.0), axis=0, keepdims=True)
 
 
-def mixer_backward(proj, taps, decay, gain, inverse, solved, core, grad, heads, length):
+def mixer_backward(proj, raw, taps, decay, gain, inverse, solved, core, pre, grad, heads, length):
     tokens, width = proj.shape
     seqs = tokens // length
     hv = heads * DV
@@ -285,17 +295,18 @@
     return pl.pallas_call(
         functools.partial(mixer_backward_kernel, heads),
         grid=(seqs,),
-        in_specs=[row(width), whole(taps), whole(decay), whole(gain),
-                  pl.BlockSpec((None, heads, length, length), lambda s: (s, 0, 0, 0)), row(hv), row(hv), row(hv)],
-        out_specs=[row(width), whole(taps), whole(gain), whole(decay)],
+        in_specs=[row(width), row(128), whole(taps), whole(decay), whole(gain),
+                  pl.BlockSpec((None, heads, length, length), lambda s: (s, 0, 0, 0)), row(hv), row(hv), row(taps.shape[1]), row(hv)],
+        out_specs=[row(width), row(128), whole(taps), whole(gain), whole(decay)],
         out_shape=[
             jax.ShapeDtypeStruct((tokens, width), BF16),
+            jax.ShapeDtypeStruct((tokens, 128), BF16),
             jax.ShapeDtypeStruct(taps.shape, F32),
             jax.ShapeDtypeStruct(gain.shape, F32),
             jax.ShapeDtypeStruct(decay.shape, F32),
         ],
         cost_estimate=busy(50), compiler_params=pltpu.CompilerParams(vmem_limit_bytes=56 << 20),
-    )(proj, taps, decay, gain, inverse, solved, core, grad)
+    )(proj, raw, taps, decay, gain, inverse, solved, core, pre, grad)
 
 
 def busy(us):
@@ -422,9 +433,9 @@
         scratch_shapes=[V(4),V(4),V(3),V(3), D((4,chunks)), D((4,chunks)), D((4,chunks)), D((3,chunks)), D((3,chunks))],
         cost_estimate=busy(40), compiler_params=pltpu.CompilerParams(collective_id=cid, has_side_effects=True, vmem_limit_bytes=40<<20))(x)
 
-def begin(weight, decays, ups, tokens, cotangent, small, bounds, n_z, cid):
+def begin(weight, ups, tokens, cotangent, small, bounds, n_z, cid):
     own = weight.shape[0]
-    cols = bounds[-1] + 128
+    cols = bounds[-1]
     units = ups.shape[2]
     rows, width = tokens.shape
     count = 8 * n_z
@@ -432,7 +443,7 @@
     part = rows // chunks
 
     def kernel(
-        w_ref, dec_ref, u_ref, t_ref, c_ref, small_ref, w_out, u_out, n_out, c_out, small_out,
+        w_ref, u_ref, t_ref, c_ref, small_ref, w_out, u_out, n_out, c_out, small_out,
         toks, lsem, a_send, a_recv, g_send, g_recv, up_send, up_recv, down_send, down_recv,
         small_send, small_recv, x_send, x_recv, d_send, d_recv, f_send, f_recv,
     ):
@@ -467,7 +478,6 @@
                 size = last - first
                 at = pl.multiple_of(8 * first + q * size, 128)
                 yield w_ref.at[:, pl.ds(at, size)], w_out.at[me, z, :, pl.ds(first, size)]
-            yield dec_ref.at[q], w_out.at[me, z, :, pl.ds(bounds[-1], 128)]
 
         def send_piece(o):
             q = partner(o)
@@ -678,7 +688,7 @@
             plane,
             jax.ShapeDtypeStruct((count,) + small.shape, BF16),
         ],
-        in_specs=[anywhere] * 6,
+        in_specs=[anywhere] * 5,
         out_specs=[anywhere, anywhere, vmem, anywhere, vmem],
         scratch_shapes=[
             pltpu.VMEM((8, rows, width), BF16),
@@ -702,9 +712,9 @@
         ],
         cost_estimate=busy(150),
         compiler_params=pltpu.CompilerParams(
-            collective_id=cid, has_side_effects=True, vmem_limit_bytes=32 << 20
+            collective_id=cid, has_side_effects=True, vmem_limit_bytes=58 << 20
         ),
-    )(weight, decays, ups, tokens, cotangent, small)
+    )(weight, ups, tokens, cotangent, small)
 
 
 def relay(left, first, second, first_dims, second_dims, gain, extras, norm_back, cid):
@@ -721,14 +731,14 @@
         extra_refs, refs = refs[: len(extras)], refs[len(extras) :]
         if multiply:
             second_ref, *refs = refs
-        rows_out, all_out, *refs = refs
+        rows_out, all_ref, *refs = refs
         if multiply:
             prod_out, *refs = refs
         if norm_back:
             gain_grad, *refs = refs
         if multiply:
             *refs, w2, stage = refs
-        (T, A, B, R, S, lsem, sa, ra, sb, rb, x_send, x_recv, d_send, d_recv, f_send, f_recv) = refs
+        (L, W, plane, T, A, B, R, S, msem, fsem, lsem, sa, ra, sb, rb, x_send, x_recv, d_send, d_recv, f_send, f_recv) = refs
         me, z, core, cx, cy = _place(8)
 
         def dev(dx, dy, c):
@@ -746,23 +756,36 @@
             load = pltpu.make_async_copy(second_ref, w2, lsem.at[2])
             load.start()
 
+        load_first = pltpu.make_async_copy(first_ref, W, lsem.at[3])
+        load_first.start()
+
         mine = (across, ng, nf, me)
         theirs = (dev(1, 1, 1 - core), dev(1 - core, core, 1 - core), dev(core, 1 - core, 1 - core), sib)
 
-        def partial(q, write):
+        turns = (theirs[0], mine[0], theirs[2], mine[2], theirs[1], theirs[3], mine[1], mine[3])
+
+        def load_left(i):
+            return pltpu.make_async_copy(left_ref.at[turns[i]], L.at[i], msem.at[i])
+
+        for i in range(8):
+            load_left(i).start()
+
+        def partial(i, write):
+            load_left(i).wait()
+
             def some(n, _):
                 cols = pl.ds(pl.multiple_of(n * tile, tile), tile)
-                w = first_ref[:, cols] if first_dims == NN else first_ref[cols, :]
-                write(cols, lax.dot_general(left_ref[q], w, first_dims, preferred_element_type=F32))
+                w = W[:, cols] if first_dims == NN else W[cols, :]
+                write(cols, lax.dot_general(L[i], w, first_dims, preferred_element_type=F32))
                 return 0
 
             lax.fori_loop(0, width // tile, some, 0)
 
-        def give(k):
+        def give(i, k):
             def write(cols, v):
                 T[k, :, cols] = v.astype(BF16)
 
-            partial(theirs[k], write)
+            partial(i, write)
             remote(T.at[k], A.at[k], sa.at[k], ra.at[k], sib).start()
 
         def got(k):
@@ -774,42 +797,43 @@
         def ship(k, c, d):
             return remote(B.at[k, cut(c)], R.at[k, cut(c)], sb.at[k, c], rb.at[k, c], d)
 
-        def send_sum(k):
+        def send_sum(i, k):
+            def write(cols, v):
+                S[:, cols] = v
+
+            partial(i, write)
             got(k)
+            for c in range(chunks):
+                B[k, cut(c)] = (S[cut(c)] + A[k, cut(c)].astype(F32)).astype(BF16)
+                ship(k, c, nf).start()
+
+        def keep_sum(i, k):
+            got(k)
 
             def write(cols, v):
-                B[k, :, cols] = (v + A[k, :, cols].astype(F32)).astype(BF16)
-
-            partial(mine[k], write)
-            for c in range(chunks):
-                ship(k, c, nf).start()
-
-        def keep_sum(k, out):
-            got(k)
-
-            def write(cols, v):
-                out[:, cols] = v + A[k, :, cols].astype(F32)
-
-            partial(mine[k], write)
+                S[:, cols] = v + A[k, :, cols].astype(F32)
+
+            partial(i, write)
 
         pl.semaphore_wait(bar, 3)
-        give(0)
-        give(2)
-        send_sum(0)
-        give(1)
-        send_sum(2)
-        give(3)
-        keep_sum(1, S)
+        load_first.wait()
+        give(0, 0)
+        send_sum(1, 0)
+        give(2, 2)
+        send_sum(3, 2)
+        give(4, 1)
+        give(5, 3)
+        keep_sum(6, 1)
         for c in range(chunks):
             ship(0, c, nf).wait_recv()
             B[1, cut(c)] = (S[cut(c)] + R[0, cut(c)].astype(F32)).astype(BF16)
             ship(1, c, ng).start()
-        keep_sum(3, S)
+        keep_sum(7, 3)
 
         source, other = nf, ng
 
         def at(q, c):
-            return all_out.at[q, cut(c)]
+            return plane.at[q, cut(c)]
 
         def step(k, c):
             return remote(at(me, c), at(me, c), x_send.at[k, c], x_recv.at[k, c], (dev(1, 0, core), dev(0, 1, core))[k])
@@ -841,7 +865,7 @@
                     done = extra_refs[0][sl].astype(F32) + total
                     low = done * lax.rsqrt(jnp.mean(done * done, axis=-1, keepdims=True) + EPSILON) * gains
                 rows_out[sl] = done
-                all_out[me, sl] = low.astype(BF16)
+                plane[me, sl] = low.astype(BF16)
             for k in range(2):
                 step(k, c).start()
             twin(0, me, c).start()
@@ -850,7 +874,12 @@
 
         flushes = []
 
+        kept = []
+
         def product(q):
+            keep = pltpu.make_async_copy(plane.at[q], all_ref.at[q], fsem.at[len(kept)])
+            keep.start()
+            kept.append(keep)
             if not multiply:
                 return
             slot = len(flushes) % 2
@@ -858,7 +887,7 @@
                 flushes[-2].wait()
             for a, b in out_tiles:
                 w = w2[:, a:b] if second_dims == NN else w2[a:b, :]
-                stage[slot, :, a:b] = lax.dot_general(all_out[q], w, second_dims, preferred_element_type=F32)
+                stage[slot, :, a:b] = lax.dot_general(plane[q], w, second_dims, preferred_element_type=F32)
             flush = pltpu.make_async_copy(stage.at[slot], prod_out.at[q], lsem.at[slot])
             flush.start()
             flushes.append(flush)
@@ -903,7 +932,7 @@
             second_step(c).wait_send()
             for k, q in enumerate((me, source, other, across)):
                 twin(k, q, c).wait_send()
-        for flush in flushes[-2:]:
+        for flush in flushes[-2:] + kept:
             flush.wait()
 
     dma = pltpu.SemaphoreType.DMA
@@ -913,9 +942,9 @@
         jax.ShapeDtypeStruct((rows, width), F32),
         jax.ShapeDtypeStruct((8, rows, width), BF16),
     ]
-    out_specs = [vmem, vmem]
+    out_specs = [vmem, anywhere]
     operands = [left, first, gain, *extras]
-    in_specs = [vmem] * len(operands)
+    in_specs = [anywhere, anywhere] + [vmem] * (1 + len(extras))
     later = []
     if multiply:
         out_shape.append(jax.ShapeDtypeStruct((8, rows, out_cols), F32))
@@ -932,12 +961,17 @@
         in_specs=in_specs,
         out_specs=out_specs,
         scratch_shapes=[
+            pltpu.VMEM(left.shape, BF16),
+            pltpu.VMEM(first.shape, BF16),
+            block(8),
             block(4),
             block(4),
             block(3),
             block(3),
             pltpu.VMEM((rows, width), F32),
-            dma((3,)),
+            dma((8,)),
+            dma((8,)),
+            dma((4,)),
             dma((4,)),
             dma((4,)),
             dma((3, chunks)),
@@ -1035,7 +1069,7 @@
     )(cot.reshape(tokens, width), weight, upgate, scales)
 
 
-def conclude(grad, left, weight, block, ups, tokens, middle, middle_grad, gain, lines, conv, bounds, cid):
+def conclude(grad, left, raw_left, weight, raw_weight, block, ups, tokens, middle, middle_grad, gain, lines, conv, bounds, cid):
     n_z = 4
     _, _, own, cols = grad.shape
     units = ups.shape[2]
@@ -1049,9 +1083,9 @@
     last = n_z - 1
 
     def kernel(
-        g_ref, l_ref, w_ref, b_ref, u_ref, t_ref, m_ref, mg_ref, gain_ref, lines_ref, conv_ref,
-        result, tg, in_out, dec_out, u_out, lines_out, conv_out,
-        W, L, own_buf, UD, T, A, B, R, S, A7, B7, R7, X7, line_buf,
+        g_ref, l_ref, lr_ref, w_ref, wr_ref, b_ref, u_ref, t_ref, m_ref, mg_ref, gain_ref, lines_ref, conv_ref,
+        result, tg, in_out, u_out, line_sum, line_planes, conv_sum, conv_planes,
+        lines_out, conv_out, W, L, own_buf, UD, T, A, B, R, S, A7, B7, R7, X7, line_buf,
         lsem, wsem, osem, mine_sem, us, ur, ds, dr, i_send, i_recv, u_send, u_recv, p_send, p_recv, c_send, c_recv,
         sa, ra, sb, rb, sa7, ra7, sb7, rb7,
     ):
@@ -1089,20 +1123,35 @@
         turns = (theirs[0], theirs[2], mine[0], theirs[1], mine[2], theirs[3], mine[1], mine[3])
 
         def load_left(i):
-            return pltpu.make_async_copy(l_ref.at[turns[i]], L.at[i % 2], lsem.at[i % 2])
-
-        load_weight = pltpu.make_async_copy(w_ref, W, wsem.at[0])
+            q, slot = turns[i], i % 2
+            return (
+                pltpu.make_async_copy(l_ref.at[q], L.at[slot, :, pl.ds(0, cols)], lsem.at[slot]),
+                pltpu.make_async_copy(lr_ref.at[q], L.at[slot, :, pl.ds(cols, 128)], lsem.at[2 + slot]),
+            )
+
+        def start(copies):
+            for copy in copies:
+                copy.start()
+
+        def wait(copies):
+            for copy in copies:
+                copy.wait()
+
+        load_weight = (
+            pltpu.make_async_copy(w_ref, W.at[:, pl.ds(0, cols)], wsem.at[0]),
+            pltpu.make_async_copy(wr_ref, W.at[:, pl.ds(cols, 128)], wsem.at[7]),
+        )
         load_middle = pltpu.make_async_copy(m_ref, result, wsem.at[1])
         load_grad = pltpu.make_async_copy(mg_ref, tg, wsem.at[2])
 
         def load_own(zz):
             return pltpu.make_async_copy(g_ref.at[:, zz], own_buf.at[zz], osem.at[zz])
 
-        load_left(0).start()
-        load_weight.start()
+        start(load_left(0))
+        start(load_weight)
         for zz in (0, 3, 2, 1):
             load_own(zz).start()
-        load_left(1).start()
+        start(load_left(1))
         load_middle.start()
         load_grad.start()
         pl.semaphore_wait(bar, count - 1)
@@ -1139,7 +1188,6 @@
             for a, b in zip(bounds[:-1], bounds[1:]):
                 at = pl.multiple_of(8 * a + q * (b - a), 128)
                 yield pl.ds(a, b - a), in_out.at[:, pl.ds(at, b - a)]
-            yield pl.ds(bounds[-1], 128), dec_out.at[q]
 
         def deliver(o, slot):
             @pl.when(o == 0)
@@ -1222,7 +1270,7 @@
             return pl.ds(c * part, part)
 
         def partial(i, write):
-            load_left(i).wait()
+            wait(load_left(i))
 
             def some(n, _):
                 at = pl.ds(pl.multiple_of(n * tile, tile), tile)
@@ -1231,7 +1279,7 @@
 
             lax.fori_loop(0, width // tile, some, 0)
             if i + 2 < 8:
-                load_left(i + 2).start()
+                start(load_left(i + 2))
 
         def give(i, k, slot, before):
             if before is not None:
@@ -1376,7 +1424,7 @@
             loop(1, count, lambda o: conv_packet(o).start())
 
         def first_work():
-            load_weight.wait()
+            wait(load_weight)
             give(0, 0, 0, None)
             give(1, 2, 1, None)
 
@@ -1432,6 +1480,14 @@
         keep_line.wait()
         keep_conv.wait()
         keep_up.wait()
+        all_lines, all_conv = lines_out[0], conv_out[0]
+        for d in range(1, count):
+            all_lines, all_conv = all_lines + lines_out[d], all_conv + conv_out[d]
+        line_sum[...] = all_lines
+        conv_sum[...] = all_conv
+        for d in range(8):
+            line_planes[d : d + 1] = sum(lines_out[d * n_z + i, 4:5] for i in range(n_z))
+            conv_planes[d : d + 1] = sum(conv_out[d * n_z + i, 4:5] for i in range(n_z))
 
     dma = pltpu.SemaphoreType.DMA
     anywhere, vmem = pl.BlockSpec(memory_space=pl.ANY), pl.BlockSpec(memory_space=pltpu.VMEM)
@@ -1443,16 +1499,19 @@
             f32_rows,
             f32_rows,
             jax.ShapeDtypeStruct((own, 8 * bounds[-1]), BF16),
-            jax.ShapeDtypeStruct((8, own, 128), BF16),
             jax.ShapeDtypeStruct((8, own, units), BF16),
-            jax.ShapeDtypeStruct((count, 8, 128), F32),
-            jax.ShapeDtypeStruct((count, conv.shape[0], conv_cols), F32),
+            jax.ShapeDtypeStruct((8, 128), F32),
+            jax.ShapeDtypeStruct((8, 128), F32),
+            jax.ShapeDtypeStruct((8, conv_cols), F32),
+            jax.ShapeDtypeStruct((8, conv_cols), F32),
         ],
-        in_specs=[anywhere] * 5 + [vmem, anywhere, anywhere, vmem, vmem, anywhere],
-        out_specs=[vmem, vmem] + [anywhere] * 5,
+        in_specs=[anywhere] * 7 + [vmem, anywhere, anywhere, vmem, vmem, anywhere],
+        out_specs=[vmem, vmem, anywhere, anywhere] + [vmem] * 4,
         scratch_shapes=[
-            pltpu.VMEM((width, cols), BF16),
-            pltpu.VMEM((2, rows, cols), BF16),
+            pltpu.VMEM((count, 8, 128), F32),
+            pltpu.VMEM((count, 8, conv_cols), F32),
+            pltpu.VMEM((width, cols + 128), BF16),
+            pltpu.VMEM((2, rows, cols + 128), BF16),
             pltpu.VMEM((n_z, 8, own, cols), BF16),
             pltpu.VMEM((40, own, cols), BF16),
             blocks(2),
@@ -1465,8 +1524,8 @@
             blocks(3),
             pltpu.VMEM((rows, width), BF16),
             pltpu.VMEM((8, width), F32),
-            dma((2,)),
-            dma((7,)),
+            dma((4,)),
+            dma((8,)),
             dma((n_z,)),
             dma((4,)),
             dma((3, 8)),
@@ -1494,7 +1553,7 @@
         compiler_params=pltpu.CompilerParams(
             collective_id=cid, has_side_effects=True, vmem_limit_bytes=60 << 20
         ),
-    )(grad, left, weight, block, ups, tokens, middle, middle_grad, gain, lines, conv)
+    )(grad, left, raw_left, weight, raw_weight, block, ups, tokens, middle, middle_grad, gain, lines, conv)
 
 
 def gather_small(x, n_dp, n_z, cid):
@@ -1632,7 +1691,7 @@
     own_d = norm_first.shape[0]
     units = upgate_weight.shape[1] // (2 * n_dp)
     key, value = heads * DK, heads * DV
-    cols = 2 * key + 2 * value + 128
+    cols = 2 * key + 2 * value
     square = n_dp == 8 and n_z == 4
     here = lax.axis_index("dp")
     flat = here * n_z + lax.axis_index("fsdp")
@@ -1657,15 +1716,6 @@
     up_mine = jnp.concatenate(
         [gates[:, :, :main], ups[:, :, :main], gates[:, :, main:], ups[:, :, main:]], axis=2
     ).transpose(1, 0, 2)
-    decay_cols = jnp.concatenate(
-        [
-            by_dp(decay_weight[:, :all_heads], heads),
-            by_dp(decay_weight[:, all_heads:], heads),
-            jnp.zeros((own_d, n_dp, 128 - 2 * heads), BF16),
-        ],
-        axis=2,
-    ).transpose(1, 0, 2)
-
     def whole_rows(a):
         a = lax.all_gather(a[:, None], "fsdp", axis=1, tiled=True)
         return a.reshape(width, a.shape[-1])
@@ -1678,14 +1728,16 @@
             [norm_first] * (128 // own_d)
             + [norm_second] * (128 // own_d)
             + [jnp.broadcast_to(group_ids.astype(BF16), (128,)), jnp.zeros((640,), BF16), conv_weight.reshape(-1)]
-        ).reshape(16, 128)
+            + [decay_weight.reshape(-1)]
+        ).reshape(32, 128)
         in_full, up_plane, normed_all, cot_all, small = begin(
-            input_weight, decay_cols, up_mine, tokens, cotangent, small, bounds, n_z, 1
+            input_weight, up_mine, tokens, cotangent, small, bounds, n_z, 1
         )
         in_full = in_full.reshape(width, cols)
         normed_all = normed_all.reshape(n_dp * rows, width)
         cot_all = cot_all.reshape(n_dp * rows, width)
-        conv_full = small[:, 8:].reshape(count, taps, own_conv)
+        conv_full = small[:, 8:16].reshape(count, taps, own_conv)
+        decay_full = small[:, 16:].reshape(width, 2 * all_heads)
         first_full = small[:, 0, :own_d]
         second_full = small[:, 1, :own_d]
         every_id = small[:, 2, 0]
@@ -1697,7 +1749,8 @@
             by_dp(input_weight[:, n_dp * a : n_dp * b], b - a).transpose(1, 0, 2)
             for a, b in zip(bounds[:-1], bounds[1:])
         ]
-        in_mine = jnp.concatenate(in_mine + [decay_cols], axis=2)
+        in_mine = jnp.concatenate(in_mine, axis=2)
+        decay_full = lax.all_gather(decay_weight, ("dp", "fsdp"), axis=0, tiled=True)
         in_full = whole_rows(lax.all_to_all(in_mine, "dp", 0, 0, tiled=True))
         up_plane = lax.all_to_all(up_mine, "dp", 0, 0, tiled=True)
         small = gather_small(
@@ -1740,8 +1793,15 @@
     )
     gain = output_gain[None, :]
 
+    raw_weight = jnp.pad(
+        jnp.concatenate(
+            [lax.dynamic_slice_in_dim(decay_full, i * all_heads + here * heads, heads, axis=1) for i in range(2)], axis=1
+        ),
+        ((0, 0), (0, 128 - 2 * heads)),
+    )
     projected = dot(normed_all, in_full)
-    mixed, inverse, solved, core = mixer_forward(projected, conv_mine, decay_mine, gain, heads, rows)
+    raw = dot(normed_all, raw_weight)
+    mixed, inverse, solved, core, before_silu = mixer_forward(projected, raw, conv_mine, decay_mine, gain, heads, rows)
     if square:
         middle, second_all = relay(
             mixed.reshape(n_dp, rows, value), out_full, None, NN, NN, second_full, (tokens,), False, 4
@@ -1787,13 +1847,15 @@
         return lax.psum_scatter(a, "fsdp", scatter_dimension=0, tiled=True)
 
     def owned_parts(a):
-        a = a.reshape(n_dp, n_z, own_d, a.shape[-1]).transpose(1, 0, 2, 3)
-        return lax.psum_scatter(a.reshape(width, -1), "fsdp", scatter_dimension=0, tiled=True)
+        return lax.psum_scatter(a, "fsdp", scatter_dimension=0, tiled=True)
+
+    def by_plane(a):
+        return a.reshape(n_dp, n_z, own_d, a.shape[-1]).transpose(1, 0, 2, 3).reshape(width, -1)
 
     down_total = owned_rows(down_grad)
     block_part = dot(hidden, down_full, out=BF16)
-    upgate_low, upgate_grad, down_total, block_part = lax.optimization_barrier(
-        (upgate_low, upgate_grad, down_total, block_part)
+    upgate_low, upgate_grad, down_total, block_part, seed = lax.optimization_barrier(
+        (upgate_low, by_plane(upgate_grad), down_total, block_part, seed)
     )
     upgate_sum = owned_parts(upgate_grad)
     if square:
@@ -1811,8 +1873,8 @@
     output_grad = dot(mixed, middle_all, TN, out=BF16)
     mixed_grad, output_grad, upgate_sum = lax.optimization_barrier((mixed_grad, output_grad, upgate_sum))
     output_total = owned_rows(output_grad)
-    projected_low, conv_grad, gain_grad, decay_grad = mixer_backward(
-        projected, conv_mine, decay_mine, gain, inverse, solved, core, mixed_grad, heads, rows
+    projected_low, raw_low, conv_grad, gain_grad, decay_grad = mixer_backward(
+        projected, raw, conv_mine, decay_mine, gain, inverse, solved, core, before_silu, mixed_grad, heads, rows
     )
     projected_low, output_total = lax.optimization_barrier((projected_low, output_total))
     def upgate_rows(a):
@@ -1827,13 +1889,8 @@
             axis=1,
         ).astype(F32)
 
-    def decay_rows(a):
-        a = a.transpose(1, 0, 2).astype(F32)
-        return jnp.concatenate(
-            [a[:, :, :heads].reshape(own_d, -1), a[:, :, heads : 2 * heads].reshape(own_d, -1)], axis=1
-        )
-
     in_grad = dot(normed_all, projected_low, TN, out=BF16)
+    raw_grad = dot(normed_all, raw_low, TN)[:, : 2 * heads]
     down_total = down_total.astype(F32)
     output_total = output_total.astype(F32)
     if square:
@@ -1855,10 +1912,13 @@
             (2 * n_dp * key + here * value, 2 * key, 2 * key + value),
         ):
             conv_lines = lax.dynamic_update_slice(conv_lines, conv_grad[:, a:b], (0, at))
-        result, tokens_grad, input_total, decay_total, up_total, lines, conv_lines = conclude(
+        conv_lines = lax.dynamic_update_slice(conv_lines, raw_grad.reshape(1, -1), (taps, 0))
+        result, tokens_grad, input_total, up_total, summed, planes, conv_total, raw_planes = conclude(
             in_grad.reshape(n_dp, n_z, own_d, cols),
             projected_low.reshape(n_dp, rows, cols),
+            raw_low.reshape(n_dp, rows, 128),
             in_full,
+            raw_weight,
             block_part.reshape(n_dp, rows, width),
             upgate_sum.reshape(n_dp, own_d, 2 * units),
             tokens,
@@ -1871,22 +1931,20 @@
             9,
         )
         input_total = input_total.astype(F32)
-        decay_total = decay_rows(decay_total)
+        decay_total = raw_planes.reshape(n_dp, own_d, 2, heads).transpose(1, 2, 0, 3).reshape(own_d, 2 * all_heads)
         upgate_total = upgate_rows(up_total)
-        summed = jnp.sum(lines, axis=0)
         per = 128 // own_d
         place = lax.rem(flat, per) * own_d
         first_total = lax.dynamic_slice_in_dim(summed[0], place, own_d)
         second_total = lax.dynamic_slice_in_dim(summed[1], place, own_d)
         gain_total = summed[2:4].reshape(-1)
-        scale_bias = jnp.sum(lines[:, 4, : 2 * heads].reshape(n_dp, n_z, 2, heads), axis=1)
-        scale_total = scale_bias[:, 0].reshape(-1)
-        bias_total = scale_bias[:, 1].reshape(-1)
-        conv_total = jnp.sum(conv_lines, axis=0)[:taps]
+        scale_total = planes[:, :heads].reshape(-1)
+        bias_total = planes[:, heads : 2 * heads].reshape(-1)
+        conv_total = conv_total[:taps]
     else:
         projected_low, in_grad = lax.optimization_barrier((projected_low, in_grad))
-        back_one = dot(projected_low, in_full, NT, out=BF16)
-        in_sum = owned_parts(in_grad)
+        back_one = (dot(projected_low, in_full, NT) + dot(raw_low, raw_weight, NT)).astype(BF16)
+        in_sum = owned_parts(by_plane(in_grad))
         normed_one_grad = total(back_one, 9)
         result = middle + total(block_part, 7)
         input_part, first_grad = norm_back(inputs, first_root, first_full, normed_one_grad)
@@ -1895,7 +1953,9 @@
         up_total = lax.all_to_all(upgate_sum.reshape(n_dp, own_d, -1), "dp", 0, 0, tiled=True)
         upgate_total = upgate_rows(up_total)
         in_total = lax.all_to_all(in_sum.reshape(n_dp, own_d, -1), "dp", 0, 0, tiled=True)
-        decay_total = decay_rows(in_total[:, :, bounds[-1] :])
+        raw_rows = jnp.zeros((width, 2, all_heads), F32)
+        raw_rows = lax.dynamic_update_slice(raw_rows, raw_grad.reshape(width, 2, heads), (0, 0, here * heads))
+        decay_total = lax.psum_scatter(raw_rows.reshape(width, -1), ("dp", "fsdp"), scatter_dimension=0, tiled=True)
         in_total = in_total.transpose(1, 0, 2).astype(F32)
         input_total = jnp.concatenate(
             [in_total[:, :, a:b].reshape(own_d, -1) for a, b in zip(bounds[:-1], bounds[1:])], axis=1

time: 781 us -> 747 us (0.956)
  Pallas kernels: 579 us -> 559 us
  local copies, waits for them, and re-layouts: 52.4 us -> 36.1 us
    unnamed x74 -> x65, local copies, waits for them, and re-layouts: 21 us -> 8.81 us
    pallas_call x2, Pallas kernels: 182 us -> 172 us  [relay(): pl.pallas_call(kernel, out_shape=out_shape, in_specs=in_specs, out_specs=...]
    pallas_call x1, Pallas kernels: 50.3 us -> 41.2 us  [mixer_backward(): pl.pallas_call(functools.partial(mixer_backward_kernel, heads), grid=(seq...]
    dot_general x6 -> x8, matrix products: 89.1 us -> 94.1 us  [dot(): return lax.dot_general(a, b, dims, preferred_element_type=F32).astype(out)]
  transfers between devices with their start and end apart: 6 -> 6, of which waited for: 2 -> 3; matrix products, arithmetic and copies ran while one was open for 10% -> 13% of each run, Pallas kernels for 41% -> 41%
where the time goes in v5:
time: 747 us; the launch traced here: 742 us
  Pallas kernels  559 us (75%)
  matrix products  94.1 us (13%)
  local copies, waits for them, and re-layouts  36.1 us (5%)
  waiting for transfers between devices  23.8 us (3%)
  between operations  15.6 us (2%)
  other arithmetic  13.1 us (2%)
    pallas_call x2, Pallas kernels, relay(): pl.pallas_call(kernel, out_shape=out_shape, in_specs=in_specs, out_specs=...  172 us
    pallas_call x1, Pallas kernels, conclude(): pl.pallas_call(kernel, out_shape=[f32_rows, f32_rows, jax.ShapeDtypeStruc...  136 us
    pallas_call x1, Pallas kernels, begin(): pl.pallas_call(kernel, out_shape=[jax.ShapeDtypeStruct((8, n_z, own, cols...  121 us
    dot_general x8, matrix products, dot(): return lax.dot_general(a, b, dims, preferred_element_type=F32).astype(out)  94.1 us
    pallas_call x1, Pallas kernels, mixer_forward(): pl.pallas_call(functools.partial(mixer_forward_kernel, heads), grid=(seqs...  52.7 us
    pallas_call x1, Pallas kernels, mixer_backward(): pl.pallas_call(functools.partial(mixer_backward_kernel, heads), grid=(seq...  41.2 us
    pallas_call x1, Pallas kernels, units_forward(): pl.pallas_call(kernel, grid=(blocks,), in_specs=[row(width), whole(weight...  19.6 us
    pallas_call x1, Pallas kernels, units_backward(): pl.pallas_call(kernel, grid=(blocks,), in_specs=[row(width), whole(weight...  16.2 us
  transfers between devices with their start and end apart: 6, of which 3 were waited for; matrix products, arithmetic and copies ran while one was open for 13% of the time, Pallas kernels for 41%

profile of v5, /device:TPU:0, one launch (start us, length us, event | category | flops | bytes accessed | tf_op | source)
XLA Modules:
  0.0 741.6 jit_solution(5127913775385946025)
XLA Ops:
  7.2 1.4 fusion.9
  8.6 0.7 reshape.191
  9.4 0.7 reshape.192
  11.3 2.2 concatenate.24
  13.5 0.7 concatenate.25
  14.2 120.9 %shard_map.237 = (bf16[8,4,64,1536]{3,2,1,0:T(8,128)(2,1)}, bf16[8,64,1408]{2,1,0:T(8,128)(2,1)}, bf16[8,256,2048]{2,1,0:T(8,128)(2,1)}, bf16[8,256,2048]{2,1,0:T(8,128)(2,1)}, bf16[32,32,128]{2,1,0:T(8,128)(2,1)}) custom-call(bf16[64,12288]{1,0:T(8,128)(2,1)} %w_ref.1, bf16[8,64,1408]{2,1,0:T(8,128)(2,1)} %bitcast.82, bf16[256,2048]{1,0:T(8,128)(2,1)} %t_ref.3, ...), custom_call_target="tpu_custom_call" | custom-call | flops 149999992832 | tf_op jit(solution)/shard_map/pallas_call | solution.py:682
  135.1 0.7 all-gather.9.cloned.1.call-update
  135.9 0.7 all-gather.7.cloned.1.call-update
  136.6 0.9 slice.90
  137.6 0.8 slice.91
  138.4 1.6 convert_reduce_fusion
  140.0 1.5 convert_reduce_fusion.1
  141.8 19.8 %fusion.12.proj_ref = f32[2048,1536]{1,0:T(8,128)} fusion(bf16[2048,2048]{1,0:T(8,128)(2,1)} %bitcast.77, bf16[2048,1536]{1,0:T(8,128)(2,1)} %bitcast.104), kind=kOutput, calls=%fused_computation.47 | convolution fusion | flops 12884901888 | bytes 27262976 | tf_op jit(solution)/shard_map/dot_general | solution.py:1664
  162.3 0.8 copy-done.11
  163.1 5.8 fusion.13.raw_ref
  169.1 0.8 reshape.224.gain_ref
  170.4 0.6 dynamic_slice.47
  171.0 52.7 %shard_map.238 = (bf16[2048,512]{1,0:T(8,128)(2,1)S(1)}, f32[8,2,256,256]{3,2,1,0:T(8,128)}, f32[2048,512]{1,0:T(8,128)}, f32[2048,512]{1,0:T(8,128)}, f32[2048,1024]{1,0:T(8,128)}) custom-call(f32[2048,1536]{1,0:T(8,128)} %fusion.12.proj_ref, f32[2048,128]{1,0:T(8,128)S(1)} %fusion.13.raw_ref, f32[4,1024]{1,0:T(4,128)S(1)} %maximum_convert_fusion.1.taps_ref, ...), custom_call_target="tpu_custom_call" | custom-call | flops 54999998464 | tf_op jit(solution)/shard_map/pallas_call | solution.py:170
  223.8 0.6 copy-done
  224.4 1.3 copy-done.4
  225.7 83.3 %shard_map.239 = (f32[256,2048]{1,0:T(8,128)}, bf16[8,256,2048]{2,1,0:T(8,128)(2,1)}) custom-call(bf16[8,256,512]{2,1,0:T(8,128)(2,1)} %bitcast.75, bf16[512,2048]{1,0:T(8,128)(2,1)} %all-gather.5.cloned.1.call-done.first_ref.refs_2_, f32[1,2048]{1,0:T(1,128)} %reshape.224.gain_ref, bf16[256,2048]{1,0:T(8,128)(2,1)} %t_ref.3), custom_call_target="tpu_custom_call" | custom-call | flops 80000000000 | tf_op jit(solution)/shard_map/pallas_call | solution.py:958
  309.1 19.6 %shard_map.240 = (f32[2048,1408]{1,0:T(8,128)}, bf16[2048,704]{1,0:T(8,128)(2,1)S(1)}, bf16[2048,704]{1,0:T(8,128)(2,1)}) custom-call(bf16[2048,2048]{1,0:T(8,128)(2,1)} %bitcast.101, bf16[2048,1408]{1,0:T(8,128)(2,1)} %bitcast.95, f32[8,128]{1,0:T(8,128)S(1)} %broadcast_in_dim.41.s_ref), custom_call_target="tpu_custom_call" | custom-call | flops 20000000000 | tf_op jit(solution)/shard_map/pallas_call | solution.py:1022
  328.7 9.4 %convolution_convert_fusion.3 = bf16[704,2048]{1,0:T(8,128)(2,1)} fusion(bf16[2048,704]{1,0:T(8,128)(2,1)} %get-tuple-element.74, bf16[2048,2048]{1,0:T(8,128)(2,1)S(1)} %bitcast.99), kind=kOutput, calls=%fused_computation.3 | convolution fusion | flops 5907021824 | bytes 14155776 | tf_op jit(solution)/shard_map/dot_general | solution.py:1664
  338.2 3.4 convert_multiply_fusion.refs_1_
  341.6 7.8 %all-gather.7.cloned.1.call-done.w_ref = bf16[704,2048]{1,0:T(8,128)(2,1)} async-done(((bf16[176,2048]{1,0:T(8,128)(2,1)}), bf16[704,2048]{1,0:T(8,128)(2,1)}) %all-gather.7.cloned.1.call-update) | async-done | bytes 2883600 | tf_op jit(solution)/shard_map/all_gather | solution.py:1765
  349.4 1.8 copy-done.2
  351.2 16.2 %shard_map.241 = bf16[2048,1408]{1,0:T(8,128)(2,1)} custom-call(bf16[2048,2048]{1,0:T(8,128)(2,1)} %bitcast.98, bf16[704,2048]{1,0:T(8,128)(2,1)S(1)} %copy-done.2, f32[2048,1408]{1,0:T(8,128)} %get-tuple-element.78.up_ref, f32[8,128]{1,0:T(8,128)S(1)} %broadcast_in_dim.41.s_ref), custom_call_target="tpu_custom_call" | custom-call | flops 12000000000 | tf_op jit(solution)/shard_map/pallas_call | solution.py:1061
  367.4 17.2 %convolution_convert_fusion.2 = bf16[2048,1408]{1,0:T(8,128)(2,1)S(1)} fusion(bf16[2048,2048]{1,0:T(8,128)(2,1)} %bitcast.102, bf16[2048,1408]{1,0:T(8,128)(2,1)} %shard_map.241), kind=kOutput, calls=%fused_computation.2 | convolution fusion | flops 11814043648 | bytes 19922944 | tf_op jit(solution)/shard_map/dot_general | solution.py:1664
  384.7 3.0 copy.75
  387.7 8.8 %convolution_convert_fusion = bf16[2048,2048]{1,0:T(8,128)(2,1)} fusion(bf16[2048,704]{1,0:T(8,128)(2,1)S(1)} %get-tuple-element.82, bf16[704,2048]{1,0:T(8,128)(2,1)S(1)} %copy-done.2), kind=kOutput, calls=%fused_computation | convolution fusion | flops 5909774336 | bytes 14155776 | tf_op jit(solution)/shard_map/dot_general | solution.py:1664
  396.5 10.5 %reduce-scatter.4.cloned.1.call-done = bf16[176,2048]{1,0:T(8,128)(2,1)} async-done(((bf16[704,2048]{1,0:T(8,128)(2,1)}), bf16[176,2048]{1,0:T(8,128)(2,1)}) %reduce-scatter.4.cloned.1.call-update) | async-done | bytes 720912 | tf_op jit(solution)/shard_map/reduce_scatter | solution.py:1847
  407.1 0.7 reshape.226.gain_ref
  408.2 1.3 convert_element_type.87
  409.4 88.8 %shard_map.242 = (f32[256,2048]{1,0:T(8,128)}, bf16[8,256,2048]{2,1,0:T(8,128)(2,1)}, f32[8,256,512]{2,1,0:T(8,128)}, f32[1,2048]{1,0:T(1,128)}) custom-call(bf16[8,256,1408]{2,1,0:T(8,128)(2,1)} %bitcast.108, bf16[2048,1408]{1,0:T(8,128)(2,1)} %bitcast.96, f32[1,2048]{1,0:T(1,128)} %reshape.224.gain_ref, f32[256,2048]{1,0:T(8,128)} %get-tuple-element.84.refs_0_.m_ref, ...), custom_call_target="tpu_custom_call" | custom-call | flops 80000000000 | tf_op jit(solution)/shard_map/pallas_call | solution.py:958
  498.2 9.1 %convolution_convert_fusion.4 = bf16[512,2048]{1,0:T(8,128)(2,1)} fusion(bf16[2048,512]{1,0:T(8,128)(2,1)S(1)} %copy-done.5, bf16[2048,2048]{1,0:T(8,128)(2,1)} %bitcast.103), kind=kOutput, calls=%fused_computation.4 | convolution fusion | flops 4296015872 | bytes 12582912 | tf_op jit(solution)/shard_map/dot_general | solution.py:1664
  507.3 4.0 reduce-scatter.6.cloned.1.call-done
  511.4 41.2 %shard_map.243 = (bf16[2048,1536]{1,0:T(8,128)(2,1)}, bf16[2048,128]{1,0:T(8,128)(2,1)}, f32[4,1024]{1,0:T(4,128)}, f32[1,256]{1,0:T(1,128)}, f32[2,128]{1,0:T(2,128)}) custom-call(f32[2048,1536]{1,0:T(8,128)} %fusion.12.proj_ref, f32[2048,128]{1,0:T(8,128)} %copy-done.6, f32[4,1024]{1,0:T(4,128)} %copy-done, f32[2,128]{1,0:T(2,128)} %copy-done.1, ...), custom_call_target="tpu_custom_call" | custom-call | flops 49999998976 | tf_op jit(solution)/shard_map/pallas_call | solution.py:295
  552.6 0.7 reshape.215
  553.3 4.7 fusion.3
  558.0 0.4 copy.76
  558.4 0.7 reshape.216
  559.5 0.7 concatenate.28.lines_ref
  560.2 19.2 %convolution_convert_fusion.1 = bf16[2048,1536]{1,0:T(8,128)(2,1)} fusion(bf16[2048,2048]{1,0:T(8,128)(2,1)} %bitcast.80, bf16[2048,1536]{1,0:T(8,128)(2,1)} %get-tuple-element.92), kind=kOutput, calls=%fused_computation.1 | convolution fusion | flops 12888047616 | bytes 20971520 | tf_op jit(solution)/shard_map/dot_general | solution.py:1664
  579.4 136.0 %shard_map.244 = (f32[256,2048]{1,0:T(8,128)}, f32[256,2048]{1,0:T(8,128)}, bf16[64,12288]{1,0:T(8,128)(2,1)}, bf16[8,64,1408]{2,1,0:T(8,128)(2,1)}, f32[8,128]{...) custom-call(bf16[8,4,64,1536]{3,2,1,0:T(8,128)(2,1)} %bitcast.107, ...), custom_call_target="tpu_custom_call" | custom-call | flops 120000004096 | tf_op jit(solution)/shard_map/pallas_call | solution.py:1496
  715.5 0.8 fusion.10
  716.3 1.2 slice_bitcast_fusion
  717.5 1.1 fusion.8
  718.6 1.4 fusion.7
  720.0 1.9 convert_element_type.84
  722.0 0.7 copy.78
  722.7 0.6 slice.103
  723.4 0.6 reshape.219
  724.0 0.6 reshape.220
  724.6 1.1 convert_element_type.85
  725.7 0.6 fusion.5
  726.2 0.6 fusion.6
  726.9 0.4 copy.80
  727.3 0.7 reshape.223
  728.2 0.4 copy.79
  728.6 0.7 reshape.222
  729.4 1.8 maximum_convert_fusion
  731.2 0.8 copy-done.8
  732.0 1.3 copy.96
  733.3 1.3 copy.97
  (109 shorter events, 3.5 us)
Async XLA Ops:
  7.2 218.5 %all-gather.5.cloned.1.call-start = ((), (), s32[]{:S(2)}) async-start(), calls=%async_computation.3 | async-start | bytes 2621440 | tf_op jit(solution)/shard_map/all_gather | solution.py:1763
  9.3 1.8 copy-start.23
  9.3 1.8 copy-start.17
  10.1 3.4 copy-start.20
  10.1 3.4 copy-start.21
  135.1 173.9 %all-gather.9.cloned.1.call-start = ((), (), s32[]{:S(2)}) async-start(), calls=%async_computation.8 | async-start | bytes 7208960 | tf_op jit(solution)/shard_map/all_gather | solution.py:1720
  135.8 213.6 %all-gather.7.cloned.1.call-start = ((), (), s32[]{:S(2)}) async-start(), calls=%async_computation.4 | async-start | bytes 3604480 | tf_op jit(solution)/shard_map/all_gather | solution.py:1765
  136.6 270.5 %reduce-scatter.4.cloned.1.call-start = ((), (), s32[]{:S(2)}) async-start(), calls=%async_computation.5 | async-start | bytes 3604480 | tf_op jit(solution)/shard_map/reduce_scatter | solution.py:1847
  162.3 0.8 copy-start.11
  163.1 7.2 copy-start.25
  163.1 7.2 copy-start.26
  163.1 7.9 %copy-start.3 = (f32[256]{0:T(256)S(1)}, f32[256]{0:T(256)}, u32[]{:S(2)}) copy-start(f32[256]{0:T(256)} %param.23) | copy-start | bytes 3076
  168.9 54.8 %copy-start.6 = (f32[2048,128]{1,0:T(8,128)}, f32[2048,128]{1,0:T(8,128)S(1)}, u32[]{:S(2)}) copy-start(f32[2048,128]{1,0:T(8,128)S(1)} %fusion.13.raw_ref) | copy-start | bytes 3145732
  170.4 53.3 %copy-start.1 = (f32[2,128]{1,0:T(2,128)}, f32[2,128]{1,0:T(2,128)S(1)}, u32[]{:S(2)}) copy-start(f32[2,128]{1,0:T(2,128)S(1)} %select_maximum_fusion.decay_ref) | copy-start | bytes 3076
  223.8 0.6 copy-start
  224.4 1.3 copy-start.4
  309.1 19.6 %copy-start.27 = (bf16[8,256,2048]{2,1,0:T(8,128)(2,1)S(1)}, bf16[8,256,2048]{2,1,0:T(8,128)(2,1)}, u32[]{:S(2)}) copy-start(bf16[8,256,2048]{2,1,0:T(8,128)(2,1)} %get-tuple-element.75) | copy-start | bytes 25165828
  338.1 173.2 %reduce-scatter.6.cloned.1.call-start = ((), (), s32[]{:S(2)}) async-start(), calls=%async_computation.6 | async-start | bytes 7208960 | tf_op jit(solution)/shard_map/reduce_scatter | solution.py:1850
  349.4 1.8 copy-start.2
  396.5 10.6 %copy-start.14 = (f32[32,64]{1,0:T(8,128)S(1)}, f32[32,64]{1,0:T(8,128)}, u32[]{:S(2)}) copy-start(f32[32,64]{1,0:T(8,128)} %get-tuple-element.111) | copy-start | bytes 24580
  407.0 1.1 copy-start.10
  407.1 153.2 %reduce-scatter.8.cloned.1.call-start = ((), (), s32[]{:S(2)}) async-start(), calls=%async_computation.7 | async-start | bytes 2621440 | tf_op jit(solution)/shard_map/reduce_scatter | solution.py:1847
  409.4 88.8 %copy-start.5 = (bf16[2048,512]{1,0:T(8,128)(2,1)S(1)}, bf16[2048,512]{1,0:T(8,128)(2,1)}, u32[]{:S(2)}) copy-start(bf16[2048,512]{1,0:T(8,128)(2,1)} %copy-done.4) | copy-start | bytes 6291460
  553.3 5.9 copy-start.15
  553.3 6.1 copy-start.24
  553.3 6.2 copy-start.18
  559.4 20.0 %copy-start.13 = (f32[8,8192]{1,0:T(8,128)}, f32[8,8192]{1,0:T(8,128)S(1)}, u32[]{:S(2)}) copy-start(f32[8,8192]{1,0:T(8,128)S(1)} %dynamic_update_slice.15.conv_ref) | copy-start | bytes 786436
  715.4 4.6 copy-start.9
  715.4 6.5 copy-start.19
  715.4 7.3 copy-start.22
  715.4 7.9 %copy-start.16 = (f32[8,128]{1,0:T(8,128)S(1)}, f32[8,128]{1,0:T(8,128)}, u32[]{:S(2)}) copy-start(f32[8,128]{1,0:T(8,128)} %get-tuple-element.107) | copy-start | bytes 12292
  715.4 9.1 %copy-start.12 = (bf16[128,2048]{1,0:T(8,128)(2,1)S(1)}, bf16[128,2048]{1,0:T(8,128)(2,1)}, u32[]{:S(2)}) copy-start(bf16[128,2048]{1,0:T(8,128)(2,1)} %reduce-scatter.8.cloned.1.call-done) | copy-start | bytes 1572868
  729.4 2.6 copy-start.8
  729.4 3.9 copy-start.7
Sparse Core Ops, SparseCore 0:
  135.2 48.1 all-gather.4
  184.9 105.3 all-gather.8
  291.9 57.4 all-gather.6
  352.1 54.8 reduce-scatter.3
  409.2 102.1 reduce-scatter.5
  514.1 44.3 reduce-scatter.7

commit v6 on v5

--- a/solution.py
+++ b/solution.py
@@ -185,7 +185,7 @@
 
 def mixer_backward_kernel(
     heads, proj_ref, raw_ref, taps_ref, decay_ref, gain_ref, inv_ref, solved_ref, core_ref, pre_ref, grad_ref,
-    low_ref, raw_low_ref, conv_ref, gain_grad_ref, decay_grad_ref,
+    low_ref, conv_ref, gain_grad_ref, decay_grad_ref,
 ):
     length = proj_ref.shape[0]
     count = taps_ref.shape[0]
@@ -281,7 +281,7 @@
     rate_grad = sum_rows(col_ids >= row_ids, cum_grad)
     bias_part = rate_grad * -jnp.exp(decay[0:1]) * sigmoid(shifted)
     raw_grad = jnp.where(lanes < heads, bias_part, beta_grad * beta * (1.0 - beta))
-    raw_low_ref[...] = raw_grad.astype(BF16)
+    low_ref[:, heads * 768 :] = raw_grad.astype(BF16)
     decay_grad_ref[0:1] += jnp.sum(jnp.where(lanes < heads, rate_grad * rate, 0.0), axis=0, keepdims=True)
     decay_grad_ref[1:2] += jnp.sum(jnp.where(lanes < heads, bias_part, 0.0), axis=0, keepdims=True)
 
@@ -297,10 +297,9 @@
         grid=(seqs,),
         in_specs=[row(width), row(128), whole(taps), whole(decay), whole(gain),
                   pl.BlockSpec((None, heads, length, length), lambda s: (s, 0, 0, 0)), row(hv), row(hv), row(taps.shape[1]), row(hv)],
-        out_specs=[row(width), row(128), whole(taps), whole(gain), whole(decay)],
+        out_specs=[row(width + 128), whole(taps), whole(gain), whole(decay)],
         out_shape=[
-            jax.ShapeDtypeStruct((tokens, width), BF16),
-            jax.ShapeDtypeStruct((tokens, 128), BF16),
+            jax.ShapeDtypeStruct((tokens, width + 128), BF16),
             jax.ShapeDtypeStruct(taps.shape, F32),
             jax.ShapeDtypeStruct(gain.shape, F32),
             jax.ShapeDtypeStruct(decay.shape, F32),
@@ -1069,9 +1068,9 @@
     )(cot.reshape(tokens, width), weight, upgate, scales)
 
 
-def conclude(grad, left, raw_left, weight, raw_weight, block, ups, tokens, middle, middle_grad, gain, lines, conv, bounds, cid):
+def conclude(grad, left, weight, raw_weight, block, ups, tokens, middle, middle_grad, gain, lines, conv, bounds, cid):
     n_z = 4
-    _, _, own, cols = grad.shape
+    own, cols = grad.shape[2], grad.shape[3] - 128
     units = ups.shape[2]
     rows, width = tokens.shape
     count = 8 * n_z
@@ -1083,7 +1082,7 @@
     last = n_z - 1
 
     def kernel(
-        g_ref, l_ref, lr_ref, w_ref, wr_ref, b_ref, u_ref, t_ref, m_ref, mg_ref, gain_ref, lines_ref, conv_ref,
+        g_ref, l_ref, w_ref, wr_ref, b_ref, u_ref, t_ref, m_ref, mg_ref, gain_ref, lines_ref, conv_ref,
         result, tg, in_out, u_out, line_sum, line_planes, conv_sum, conv_planes,
         lines_out, conv_out, W, L, own_buf, UD, T, A, B, R, S, A7, B7, R7, X7, line_buf,
         lsem, wsem, osem, mine_sem, us, ur, ds, dr, i_send, i_recv, u_send, u_recv, p_send, p_recv, c_send, c_recv,
@@ -1123,11 +1122,7 @@
         turns = (theirs[0], theirs[2], mine[0], theirs[1], mine[2], theirs[3], mine[1], mine[3])
 
         def load_left(i):
-            q, slot = turns[i], i % 2
-            return (
-                pltpu.make_async_copy(l_ref.at[q], L.at[slot, :, pl.ds(0, cols)], lsem.at[slot]),
-                pltpu.make_async_copy(lr_ref.at[q], L.at[slot, :, pl.ds(cols, 128)], lsem.at[2 + slot]),
-            )
+            return (pltpu.make_async_copy(l_ref.at[turns[i]], L.at[i % 2], lsem.at[i % 2]),)
 
         def start(copies):
             for copy in copies:
@@ -1145,7 +1140,18 @@
         load_grad = pltpu.make_async_copy(mg_ref, tg, wsem.at[2])
 
         def load_own(zz):
-            return pltpu.make_async_copy(g_ref.at[:, zz], own_buf.at[zz], osem.at[zz])
+            return pltpu.make_async_copy(g_ref.at[:, zz, :, pl.ds(0, cols)], own_buf.at[zz], osem.at[zz])
+
+        def give7(k):
+            return remote(b_ref.at[theirs[k]], A7.at[k], sa7.at[k], ra7.at[k], (sib, z))
+
+        def mine7(k):
+            return pltpu.make_async_copy(b_ref.at[mine[k]], X7 if k == 3 else B7.at[k], mine_sem.at[k])
+
+        def start7():
+            for k in (0, 2, 1, 3):
+                give7(k).start()
+                mine7(k).start()
 
         start(load_left(0))
         start(load_weight)
@@ -1173,12 +1179,13 @@
 
             @pl.when(z == 0)
             def _():
-                up(s, o, g_ref.at[q, last - s]).start()
+                up(s, o, g_ref.at[q, last - s, :, pl.ds(0, cols)]).start()
 
             @pl.when(z == last)
             def _():
-                down(s, o, g_ref.at[q, s]).start()
-
+                down(s, o, g_ref.at[q, s, :, pl.ds(0, cols)]).start()
+
+        start7()
         for s in range(last):
             loop(0, 8, functools.partial(start_line, s))
         for zz in range(n_z):
@@ -1323,17 +1330,6 @@
                 ship(0, c, nf).wait_recv()
                 B[1, cut(c)] = (S[cut(c)] + R[0, cut(c)].astype(F32)).astype(BF16)
                 ship(1, c, ng).start()
-
-        def give7(k):
-            return remote(b_ref.at[theirs[k]], A7.at[k], sa7.at[k], ra7.at[k], (sib, z))
-
-        def mine7(k):
-            return pltpu.make_async_copy(b_ref.at[mine[k]], X7 if k == 3 else B7.at[k], mine_sem.at[k])
-
-        def start7():
-            for k in (0, 2, 1, 3):
-                give7(k).start()
-                mine7(k).start()
 
         def send7(k):
             mine7(k).wait()
@@ -1423,23 +1419,23 @@
             keep_up.start()
             loop(1, count, lambda o: conv_packet(o).start())
 
-        def first_work():
+        def first_give():
             wait(load_weight)
             give(0, 0, 0, None)
             give(1, 2, 1, None)
 
         work = (
-            first_work,
+            lambda: (send7(0), send7(2)),
+            first_give,
             lambda: (send_sum(2, 0), give(3, 1, 0, 0)),
-            lambda: (send_sum(4, 2), give(5, 3, 1, 2), start7()),
-            lambda: (keep_sum(6, 1), others()),
+            lambda: (send_sum(4, 2), give(5, 3, 1, 2)),
+            lambda: (second_hop7(), keep_sum(6, 1)),
+            others,
             lambda: (second_hop(), keep_sum(7, 3)),
-            lambda: (send7(0), send7(2)),
-            lambda: finish_rows(),
-            lambda: (send_packets(), loop(1, 8, lambda o: unit_piece(o).start())),
-            lambda: second_hop7(),
+            lambda: (finish7(), loop(1, 8, lambda o: unit_piece(o).start())),
             lambda: None,
-            lambda: finish7(),
+            lambda: (finish_rows(), send_packets()),
+            lambda: None,
             lambda: None,
             lambda: None,
             lambda: None,
@@ -1505,7 +1501,7 @@
             jax.ShapeDtypeStruct((8, conv_cols), F32),
             jax.ShapeDtypeStruct((8, conv_cols), F32),
         ],
-        in_specs=[anywhere] * 7 + [vmem, anywhere, anywhere, vmem, vmem, anywhere],
+        in_specs=[anywhere] * 6 + [vmem, anywhere, anywhere, vmem, vmem, anywhere],
         out_specs=[vmem, vmem, anywhere, anywhere] + [vmem] * 4,
         scratch_shapes=[
             pltpu.VMEM((count, 8, 128), F32),
@@ -1524,7 +1520,7 @@
             blocks(3),
             pltpu.VMEM((rows, width), BF16),
             pltpu.VMEM((8, width), F32),
-            dma((4,)),
+            dma((2,)),
             dma((8,)),
             dma((n_z,)),
             dma((4,)),
@@ -1553,7 +1549,7 @@
         compiler_params=pltpu.CompilerParams(
             collective_id=cid, has_side_effects=True, vmem_limit_bytes=60 << 20
         ),
-    )(grad, left, raw_left, weight, raw_weight, block, ups, tokens, middle, middle_grad, gain, lines, conv)
+    )(grad, left, weight, raw_weight, block, ups, tokens, middle, middle_grad, gain, lines, conv)
 
 
 def gather_small(x, n_dp, n_z, cid):
@@ -1873,7 +1869,7 @@
     output_grad = dot(mixed, middle_all, TN, out=BF16)
     mixed_grad, output_grad, upgate_sum = lax.optimization_barrier((mixed_grad, output_grad, upgate_sum))
     output_total = owned_rows(output_grad)
-    projected_low, raw_low, conv_grad, gain_grad, decay_grad = mixer_backward(
+    projected_low, conv_grad, gain_grad, decay_grad = mixer_backward(
         projected, raw, conv_mine, decay_mine, gain, inverse, solved, core, before_silu, mixed_grad, heads, rows
     )
     projected_low, output_total = lax.optimization_barrier((projected_low, output_total))
@@ -1890,7 +1886,7 @@
         ).astype(F32)
 
     in_grad = dot(normed_all, projected_low, TN, out=BF16)
-    raw_grad = dot(normed_all, raw_low, TN)[:, : 2 * heads]
+    raw_grad = in_grad[:, cols : cols + 2 * heads].astype(F32)
     down_total = down_total.astype(F32)
     output_total = output_total.astype(F32)
     if square:
@@ -1914,9 +1910,8 @@
             conv_lines = lax.dynamic_update_slice(conv_lines, conv_grad[:, a:b], (0, at))
         conv_lines = lax.dynamic_update_slice(conv_lines, raw_grad.reshape(1, -1), (taps, 0))
         result, tokens_grad, input_total, up_total, summed, planes, conv_total, raw_planes = conclude(
-            in_grad.reshape(n_dp, n_z, own_d, cols),
-            projected_low.reshape(n_dp, rows, cols),
-            raw_low.reshape(n_dp, rows, 128),
+            in_grad.reshape(n_dp, n_z, own_d, cols + 128),
+            projected_low.reshape(n_dp, rows, cols + 128),
             in_full,
             raw_weight,
             block_part.reshape(n_dp, rows, width),
@@ -1943,8 +1938,10 @@
         conv_total = conv_total[:taps]
     else:
         projected_low, in_grad = lax.optimization_barrier((projected_low, in_grad))
-        back_one = (dot(projected_low, in_full, NT) + dot(raw_low, raw_weight, NT)).astype(BF16)
-        in_sum = owned_parts(by_plane(in_grad))
+        back_one = (
+            dot(projected_low[:, :cols], in_full, NT) + dot(projected_low[:, cols:], raw_weight, NT)
+        ).astype(BF16)
+        in_sum = owned_parts(by_plane(in_grad[:, :cols]))
         normed_one_grad = total(back_one, 9)
         result = middle + total(block_part, 7)
         input_part, first_grad = norm_back(inputs, first_root, first_full, normed_one_grad)

time: 747 us -> 736 us (0.985)
  Pallas kernels: 559 us -> 545 us
    pallas_call x1, Pallas kernels: 136 us -> 122 us  [conclude(): pl.pallas_call(kernel, out_shape=[f32_rows, f32_rows, jax.ShapeDtypeStruc...]
    dot_general x8 -> x7, matrix products: 94.1 us -> 90.2 us  [dot(): return lax.dot_general(a, b, dims, preferred_element_type=F32).astype(out)]
  transfers between devices with their start and end apart: 6 -> 6, of which waited for: 3 -> 4; matrix products, arithmetic and copies ran while one was open for 13% -> 12% of each run, Pallas kernels for 41% -> 41%
where the time goes in v6:
time: 736 us; the launch traced here: 731 us
  Pallas kernels  545 us (74%)
  matrix products  90.2 us (12%)
  local copies, waits for them, and re-layouts  42 us (6%)
  waiting for transfers between devices  25.1 us (3%)
  between operations  15.6 us (2%)
  other arithmetic  13.2 us (2%)
    pallas_call x2, Pallas kernels, relay(): pl.pallas_call(kernel, out_shape=out_shape, in_specs=in_specs, out_specs=...  172 us
    pallas_call x1, Pallas kernels, conclude(): pl.pallas_call(kernel, out_shape=[f32_rows, f32_rows, jax.ShapeDtypeStruc...  122 us
    pallas_call x1, Pallas kernels, begin(): pl.pallas_call(kernel, out_shape=[jax.ShapeDtypeStruct((8, n_z, own, cols...  121 us
    dot_general x7, matrix products, dot(): return lax.dot_general(a, b, dims, preferred_element_type=F32).astype(out)  90.2 us
    pallas_call x1, Pallas kernels, mixer_forward(): pl.pallas_call(functools.partial(mixer_forward_kernel, heads), grid=(seqs...  52.7 us
    pallas_call x1, Pallas kernels, mixer_backward(): pl.pallas_call(functools.partial(mixer_backward_kernel, heads), grid=(seq...  41.3 us
    pallas_call x1, Pallas kernels, units_forward(): pl.pallas_call(kernel, grid=(blocks,), in_specs=[row(width), whole(weight...  19.6 us
    pallas_call x1, Pallas kernels, units_backward(): pl.pallas_call(kernel, grid=(blocks,), in_specs=[row(width), whole(weight...  16.2 us
  transfers between devices with their start and end apart: 6, of which 4 were waited for; matrix products, arithmetic and copies ran while one was open for 12% of the time, Pallas kernels for 41%

profile of v6, /device:TPU:0, one launch (start us, length us, event | category | flops | bytes accessed | tf_op | source)
XLA Modules:
  0.0 731.4 jit_solution(16902616730329414355)
XLA Ops:
  7.2 1.4 fusion.7
  8.6 0.7 reshape.191
  9.4 0.7 reshape.192
  11.3 2.2 concatenate.24
  13.5 0.7 concatenate.25
  14.2 120.9 %shard_map.237 = (bf16[8,4,64,1536]{3,2,1,0:T(8,128)(2,1)}, bf16[8,64,1408]{2,1,0:T(8,128)(2,1)}, bf16[8,256,2048]{2,1,0:T(8,128)(2,1)}, bf16[8,256,2048]{2,1,0:T(8,128)(2,1)}, bf16[32,32,128]{2,1,0:T(8,128)(2,1)}) custom-call(bf16[64,12288]{1,0:T(8,128)(2,1)} %w_ref.1, bf16[8,64,1408]{2,1,0:T(8,128)(2,1)} %bitcast.76, bf16[256,2048]{1,0:T(8,128)(2,1)} %t_ref.3, ...), custom_call_target="tpu_custom_call" | custom-call | flops 149999992832 | tf_op jit(solution)/shard_map/pallas_call | solution.py:681
  135.1 0.7 all-gather.9.cloned.1.call-update
  135.9 0.7 all-gather.7.cloned.1.call-update
  136.6 0.9 slice.90
  137.6 0.8 slice.91
  138.4 1.6 convert_reduce_fusion
  140.0 1.5 convert_reduce_fusion.1
  141.8 20.1 %fusion.10.proj_ref = f32[2048,1536]{1,0:T(8,128)} fusion(bf16[2048,2048]{1,0:T(8,128)(2,1)} %bitcast.92, bf16[2048,1536]{1,0:T(8,128)(2,1)} %bitcast.102), kind=kOutput, calls=%fused_computation.46 | convolution fusion | flops 12884901888 | bytes 27262976 | tf_op jit(solution)/shard_map/dot_general | solution.py:1660
  162.7 0.8 copy-done.11
  163.5 5.8 fusion.11.raw_ref
  169.5 0.8 reshape.224.gain_ref
  171.4 52.7 %shard_map.238 = (bf16[2048,512]{1,0:T(8,128)(2,1)S(1)}, f32[8,2,256,256]{3,2,1,0:T(8,128)}, f32[2048,512]{1,0:T(8,128)}, f32[2048,512]{1,0:T(8,128)}, f32[2048,1024]{1,0:T(8,128)}) custom-call(f32[2048,1536]{1,0:T(8,128)} %fusion.10.proj_ref, f32[2048,128]{1,0:T(8,128)S(1)} %fusion.11.raw_ref, f32[4,1024]{1,0:T(4,128)S(1)} %maximum_convert_fusion.1.taps_ref, ...), custom_call_target="tpu_custom_call" | custom-call | flops 54999998464 | tf_op jit(solution)/shard_map/pallas_call | solution.py:170
  224.1 0.6 copy-done
  224.7 1.3 copy-done.4
  226.1 83.2 %shard_map.239 = (f32[256,2048]{1,0:T(8,128)}, bf16[8,256,2048]{2,1,0:T(8,128)(2,1)}) custom-call(bf16[8,256,512]{2,1,0:T(8,128)(2,1)} %bitcast.73, bf16[512,2048]{1,0:T(8,128)(2,1)} %all-gather.5.cloned.1.call-done.first_ref.refs_2_, f32[1,2048]{1,0:T(1,128)} %reshape.224.gain_ref, bf16[256,2048]{1,0:T(8,128)(2,1)} %t_ref.3), custom_call_target="tpu_custom_call" | custom-call | flops 80000000000 | tf_op jit(solution)/shard_map/pallas_call | solution.py:957
  309.4 19.6 %shard_map.240 = (f32[2048,1408]{1,0:T(8,128)}, bf16[2048,704]{1,0:T(8,128)(2,1)S(1)}, bf16[2048,704]{1,0:T(8,128)(2,1)}) custom-call(bf16[2048,2048]{1,0:T(8,128)(2,1)} %bitcast.98, bf16[2048,1408]{1,0:T(8,128)(2,1)} %bitcast.89, f32[8,128]{1,0:T(8,128)S(1)} %broadcast_in_dim.41.s_ref), custom_call_target="tpu_custom_call" | custom-call | flops 20000000000 | tf_op jit(solution)/shard_map/pallas_call | solution.py:1021
  329.0 9.4 %convolution_convert_fusion.3 = bf16[704,2048]{1,0:T(8,128)(2,1)} fusion(bf16[2048,704]{1,0:T(8,128)(2,1)} %get-tuple-element.73, bf16[2048,2048]{1,0:T(8,128)(2,1)S(1)} %bitcast.96), kind=kOutput, calls=%fused_computation.3 | convolution fusion | flops 5907021824 | bytes 14155776 | tf_op jit(solution)/shard_map/dot_general | solution.py:1660
  338.4 3.4 convert_multiply_fusion.refs_1_
  341.9 7.6 %all-gather.7.cloned.1.call-done.w_ref = bf16[704,2048]{1,0:T(8,128)(2,1)} async-done(((bf16[176,2048]{1,0:T(8,128)(2,1)}), bf16[704,2048]{1,0:T(8,128)(2,1)}) %all-gather.7.cloned.1.call-update) | async-done | bytes 2883600 | tf_op jit(solution)/shard_map/all_gather | solution.py:1761
  349.5 1.8 copy-done.2
  351.3 16.2 %shard_map.241 = bf16[2048,1408]{1,0:T(8,128)(2,1)} custom-call(bf16[2048,2048]{1,0:T(8,128)(2,1)} %bitcast.95, bf16[704,2048]{1,0:T(8,128)(2,1)S(1)} %copy-done.2, f32[2048,1408]{1,0:T(8,128)} %get-tuple-element.77.up_ref, f32[8,128]{1,0:T(8,128)S(1)} %broadcast_in_dim.41.s_ref), custom_call_target="tpu_custom_call" | custom-call | flops 12000000000 | tf_op jit(solution)/shard_map/pallas_call | solution.py:1060
  367.5 17.2 %convolution_convert_fusion.2 = bf16[2048,1408]{1,0:T(8,128)(2,1)S(1)} fusion(bf16[2048,2048]{1,0:T(8,128)(2,1)} %bitcast.99, bf16[2048,1408]{1,0:T(8,128)(2,1)} %shard_map.241), kind=kOutput, calls=%fused_computation.2 | convolution fusion | flops 11814043648 | bytes 19922944 | tf_op jit(solution)/shard_map/dot_general | solution.py:1660
  384.8 3.0 copy.71
  387.8 8.8 %convolution_convert_fusion = bf16[2048,2048]{1,0:T(8,128)(2,1)} fusion(bf16[2048,704]{1,0:T(8,128)(2,1)S(1)} %get-tuple-element.81, bf16[704,2048]{1,0:T(8,128)(2,1)S(1)} %copy-done.2), kind=kOutput, calls=%fused_computation | convolution fusion | flops 5909774336 | bytes 14155776 | tf_op jit(solution)/shard_map/dot_general | solution.py:1660
  396.6 10.5 %reduce-scatter.4.cloned.1.call-done = bf16[176,2048]{1,0:T(8,128)(2,1)} async-done(((bf16[704,2048]{1,0:T(8,128)(2,1)}), bf16[176,2048]{1,0:T(8,128)(2,1)}) %reduce-scatter.4.cloned.1.call-update) | async-done | bytes 720912 | tf_op jit(solution)/shard_map/reduce_scatter | solution.py:1843
  407.2 0.7 reshape.226.gain_ref
  408.2 1.3 convert_element_type.88
  409.5 88.8 %shard_map.242 = (f32[256,2048]{1,0:T(8,128)}, bf16[8,256,2048]{2,1,0:T(8,128)(2,1)}, f32[8,256,512]{2,1,0:T(8,128)}, f32[1,2048]{1,0:T(1,128)}) custom-call(bf16[8,256,1408]{2,1,0:T(8,128)(2,1)} %bitcast.104, bf16[2048,1408]{1,0:T(8,128)(2,1)} %bitcast.90, f32[1,2048]{1,0:T(1,128)} %reshape.224.gain_ref, f32[256,2048]{1,0:T(8,128)} %get-tuple-element.83.refs_0_.m_ref, ...), custom_call_target="tpu_custom_call" | custom-call | flops 80000000000 | tf_op jit(solution)/shard_map/pallas_call | solution.py:957
  498.3 9.1 %convolution_convert_fusion.4 = bf16[512,2048]{1,0:T(8,128)(2,1)} fusion(bf16[2048,512]{1,0:T(8,128)(2,1)S(1)} %copy-done.5, bf16[2048,2048]{1,0:T(8,128)(2,1)} %bitcast.100), kind=kOutput, calls=%fused_computation.4 | convolution fusion | flops 4296015872 | bytes 12582912 | tf_op jit(solution)/shard_map/dot_general | solution.py:1660
  507.4 4.0 reduce-scatter.6.cloned.1.call-done
  511.5 41.3 %shard_map.243 = (bf16[2048,1664]{1,0:T(8,128)(2,1)}, f32[4,1024]{1,0:T(4,128)}, f32[1,256]{1,0:T(1,128)}, f32[2,128]{1,0:T(2,128)}) custom-call(f32[2048,1536]{1,0:T(8,128)} %fusion.10.proj_ref, f32[2048,128]{1,0:T(8,128)} %copy-done.6, f32[4,1024]{1,0:T(4,128)} %copy-done, f32[2,128]{1,0:T(2,128)} %copy-done.1, f32[1,256]{1,0:T(1,128)} %bitcast.71, ...), custom_call_target="tpu_custom_call" | custom-call | flops 49999998976 | tf_op jit(solution)/shard_map/pallas_call | solution.py:295
  552.7 0.8 reshape.214
  553.5 0.7 slice_bitcast_fusion.1
  554.2 0.7 concatenate.28.lines_ref
  555.0 0.7 slice_dynamic-update-slice_fusion.2
  555.7 0.7 slice_dynamic-update-slice_fusion.1
  556.3 0.7 slice_dynamic-update-slice_fusion
  557.1 1.5 reduce-scatter.8.cloned.1.call-done
  558.6 19.7 %convolution_convert_fusion.1 = bf16[2048,1664]{1,0:T(8,128)(2,1)S(1)} fusion(bf16[2048,2048]{1,0:T(8,128)(2,1)} %bitcast.94, bf16[2048,1664]{1,0:T(8,128)(2,1)} %get-tuple-element.91), kind=kOutput, calls=%fused_computation.1 | convolution fusion | flops 13962051584 | bytes 22020096 | tf_op jit(solution)/shard_map/dot_general | solution.py:1660
  578.3 2.8 copy-done.15
  581.2 0.7 reshape.228
  582.1 0.7 copy-done.13
  582.8 122.2 %shard_map.244 = (f32[256,2048]{1,0:T(8,128)}, f32[256,2048]{1,0:T(8,128)}, bf16[64,12288]{1,0:T(8,128)(2,1)}, bf16[8,64,1408]{2,1,0:T(8,128)(2,1)}, f32[8,128]{...) custom-call(bf16[8,4,64,1664]{3,2,1,0:T(8,128)(2,1)} %bitcast.81, ...), custom_call_target="tpu_custom_call" | custom-call | flops 120000004096 | tf_op jit(solution)/shard_map/pallas_call | solution.py:1492
  705.1 0.8 fusion.8
  705.9 1.2 slice_bitcast_fusion
  707.2 1.1 fusion.6
  708.3 1.4 fusion.5
  709.7 1.9 convert_element_type.85
  711.7 0.7 copy.73
  712.4 0.6 slice.103
  713.1 0.6 reshape.219
  713.7 0.6 reshape.220
  714.3 1.1 convert_element_type.86
  717.0 0.7 reshape.223
  718.3 0.7 reshape.222
  719.1 1.8 maximum_convert_fusion
  720.8 0.8 copy-done.8
  721.6 1.3 copy.91
  723.0 1.3 copy.92
  (106 shorter events, 6.2 us)
Async XLA Ops:
  7.2 218.9 %all-gather.5.cloned.1.call-start = ((), (), s32[]{:S(2)}) async-start(), calls=%async_computation.3 | async-start | bytes 2621440 | tf_op jit(solution)/shard_map/all_gather | solution.py:1759
  9.3 1.8 copy-start.23
  9.3 1.8 copy-start.17
  10.1 3.4 copy-start.20
  10.1 3.4 copy-start.21
  135.1 174.2 %all-gather.9.cloned.1.call-start = ((), (), s32[]{:S(2)}) async-start(), calls=%async_computation.8 | async-start | bytes 7208960 | tf_op jit(solution)/shard_map/all_gather | solution.py:1716
  135.9 213.7 %all-gather.7.cloned.1.call-start = ((), (), s32[]{:S(2)}) async-start(), calls=%async_computation.4 | async-start | bytes 3604480 | tf_op jit(solution)/shard_map/all_gather | solution.py:1761
  136.6 270.5 %reduce-scatter.4.cloned.1.call-start = ((), (), s32[]{:S(2)}) async-start(), calls=%async_computation.5 | async-start | bytes 3604480 | tf_op jit(solution)/shard_map/reduce_scatter | solution.py:1843
  162.6 0.8 copy-start.11
  163.5 7.2 copy-start.24
  163.5 7.2 copy-start.25
  163.5 7.9 %copy-start.3 = (f32[256]{0:T(256)S(1)}, f32[256]{0:T(256)}, u32[]{:S(2)}) copy-start(f32[256]{0:T(256)} %param.23) | copy-start | bytes 3076
  169.3 54.8 %copy-start.6 = (f32[2048,128]{1,0:T(8,128)}, f32[2048,128]{1,0:T(8,128)S(1)}, u32[]{:S(2)}) copy-start(f32[2048,128]{1,0:T(8,128)S(1)} %fusion.11.raw_ref) | copy-start | bytes 3145732
  170.8 53.3 %copy-start.1 = (f32[2,128]{1,0:T(2,128)}, f32[2,128]{1,0:T(2,128)S(1)}, u32[]{:S(2)}) copy-start(f32[2,128]{1,0:T(2,128)S(1)} %select_maximum_fusion.decay_ref) | copy-start | bytes 3076
  224.1 0.6 copy-start
  224.7 1.3 copy-start.4
  309.4 19.6 %copy-start.26 = (bf16[8,256,2048]{2,1,0:T(8,128)(2,1)S(1)}, bf16[8,256,2048]{2,1,0:T(8,128)(2,1)}, u32[]{:S(2)}) copy-start(bf16[8,256,2048]{2,1,0:T(8,128)(2,1)} %get-tuple-element.74) | copy-start | bytes 25165828
  338.4 173.0 %reduce-scatter.6.cloned.1.call-start = ((), (), s32[]{:S(2)}) async-start(), calls=%async_computation.6 | async-start | bytes 7208960 | tf_op jit(solution)/shard_map/reduce_scatter | solution.py:1846
  349.5 1.8 copy-start.2
  396.6 10.6 %copy-start.14 = (f32[32,64]{1,0:T(8,128)S(1)}, f32[32,64]{1,0:T(8,128)}, u32[]{:S(2)}) copy-start(f32[32,64]{1,0:T(8,128)} %get-tuple-element.109) | copy-start | bytes 24580
  407.1 1.1 copy-start.10
  407.2 151.4 %reduce-scatter.8.cloned.1.call-start = ((), (), s32[]{:S(2)}) async-start(), calls=%async_computation.7 | async-start | bytes 2621440 | tf_op jit(solution)/shard_map/reduce_scatter | solution.py:1843
  409.5 88.8 %copy-start.5 = (bf16[2048,512]{1,0:T(8,128)(2,1)S(1)}, bf16[2048,512]{1,0:T(8,128)(2,1)}, u32[]{:S(2)}) copy-start(bf16[2048,512]{1,0:T(8,128)(2,1)} %copy-done.4) | copy-start | bytes 6291460
  511.5 42.8 %copy-start.18 = (f32[1,2048]{1,0:T(1,128)S(1)}, f32[1,2048]{1,0:T(1,128)}, u32[]{:S(2)}) copy-start(f32[1,2048]{1,0:T(1,128)} %get-tuple-element.95) | copy-start | bytes 24580
  578.3 2.8 copy-start.15
  582.1 0.7 copy-start.13
  705.1 4.6 copy-start.9
  705.1 6.5 copy-start.19
  705.1 7.3 %copy-start.22 = (f32[8,256]{1,0:T(8,128)S(1)}, f32[8,256]{1,0:T(8,128)}, u32[]{:S(2)}) copy-start(f32[8,256]{1,0:T(8,128)} %get-tuple-element.104) | copy-start | bytes 24580
  705.1 7.9 %copy-start.16 = (f32[8,128]{1,0:T(8,128)S(1)}, f32[8,128]{1,0:T(8,128)}, u32[]{:S(2)}) copy-start(f32[8,128]{1,0:T(8,128)} %get-tuple-element.105) | copy-start | bytes 12292
  705.1 9.2 %copy-start.12 = (bf16[128,2048]{1,0:T(8,128)(2,1)S(1)}, bf16[128,2048]{1,0:T(8,128)(2,1)}, u32[]{:S(2)}) copy-start(bf16[128,2048]{1,0:T(8,128)(2,1)} %reduce-scatter.8.cloned.1.call-done) | copy-start | bytes 1572868
  719.0 2.6 copy-start.8
  719.0 3.9 copy-start.7
Sparse Core Ops, SparseCore 0:
  135.2 48.1 all-gather.4
  184.9 105.4 all-gather.8
  292.0 57.4 all-gather.6
  352.2 54.8 reduce-scatter.3
  409.3 102.1 reduce-scatter.5
  514.2 44.3 reduce-scatter.7

commit v7 on v6

--- a/solution.py
+++ b/solution.py
@@ -458,10 +458,6 @@
         def partner(o):
             return dev(o // 4, lax.rem(o // 2, 2), lax.rem(core + o, 2))
 
-        def anyone(o):
-            other = lax.rem(flat + o, count)
-            return (other // n_z, lax.rem(other, n_z))
-
         def remote(src, dst, send, recv, device):
             return pltpu.make_async_remote_copy(src, dst, send, recv, device_id=device, device_id_type=MESH)
 
@@ -532,7 +528,12 @@
             return remote(u_ref.at[q], u_out.at[me], g_send.at[o - 1], g_recv.at[o - 1], (q, z))
 
         def tiny(o):
-            return remote(small_ref, small_out.at[flat], small_send.at[o - 1], small_recv.at[o - 1], anyone(o))
+            to = (me, lax.rem(z + o, n_z))
+            return remote(small_ref, small_out.at[flat], small_send.at[o - 1], small_recv.at[o - 1], to)
+
+        def tiny_line(o):
+            at, i = small_out.at[pl.ds(me * n_z, n_z)], n_z - 2 + o
+            return remote(at, at, small_send.at[i], small_recv.at[i], (partner(o), z))
 
         near = (dev(1, 0, core), dev(0, 1, core))
         source, other, across = dev(1 - core, core, core), dev(core, 1 - core, core), dev(1, 1, core)
@@ -602,19 +603,23 @@
         tok_begin, tok_forward, tok_last, tok_finish, tok_close = gather(0, t_ref, toks)
         cot_begin, cot_forward, cot_last, cot_finish, cot_close = gather(1, c_ref, c_out)
 
-        loop(1, count, lambda o: pl.semaphore_signal(bar, inc=1, device_id=anyone(o), device_id_type=MESH))
+        def greet(device):
+            pl.semaphore_signal(bar, inc=1, device_id=device, device_id_type=MESH)
+
+        loop(1, 8, lambda o: greet((partner(o), z)))
+        loop(1, n_z, lambda o: greet((me, lax.rem(z + o, n_z))))
         for src, dst in sections(me):
             pltpu.make_async_copy(src, dst, lsem.at[2]).start()
         keep_u = pltpu.make_async_copy(u_ref.at[me], u_out.at[me], lsem.at[3])
         keep_s = pltpu.make_async_copy(small_ref, small_out.at[flat], lsem.at[4])
         keep_u.start()
         keep_s.start()
-        pl.semaphore_wait(bar, count - 1)
+        pl.semaphore_wait(bar, 7 + n_z - 1)
 
         loop(1, 8, send_piece)
         pltpu.make_async_copy(w_out.at[me, z], w_out.at[me, z], lsem.at[2]).wait()
         pass_on(0, 0)
-        loop(1, count, lambda o: tiny(o).start())
+        loop(1, n_z, lambda o: tiny(o).start())
 
         def first_leg(o):
             landed(o).wait_recv()
@@ -623,14 +628,16 @@
         tok_begin()
         loop(1, 8, first_leg)
         loop(0, 8, lambda o: pass_on(1, o))
+        keep_s.wait()
+        loop(1, n_z, lambda o: tiny(o).wait_recv())
+        loop(1, 8, lambda o: tiny_line(o).start())
         tok_forward()
         cot_begin()
         loop(1, 8, lambda o: unit_piece(o).start())
         loop(0, 4, lambda o: pass_on(2, o))
         tok_last()
         tok_finish()
-        keep_s.wait()
-        loop(1, count, lambda o: tiny(o).wait_recv())
+        loop(1, 8, lambda o: tiny_line(o).wait_recv())
 
         lanes = lax.broadcasted_iota(jnp.int32, (1, 128), 1)
         per = 128 // own
@@ -669,7 +676,8 @@
             loop(0, 8, functools.partial(sent, t))
         loop(1, 8, lambda o: landed(o).wait_send())
         loop(1, 8, lambda o: unit_piece(o).wait())
-        loop(1, count, lambda o: tiny(o).wait_send())
+        loop(1, n_z, lambda o: tiny(o).wait_send())
+        loop(1, 8, lambda o: tiny_line(o).wait_send())
         keep_u.wait()
         tok_close()
         cot_close()
@@ -700,8 +708,8 @@
             dma((legs, 8)),
             dma((legs, 8)),
             dma((legs, 8)),
-            dma((count - 1,)),
-            dma((count - 1,)),
+            dma((n_z + 6,)),
+            dma((n_z + 6,)),
             dma((2, 2, chunks)),
             dma((2, 2, chunks)),
             dma((2, chunks)),
@@ -1867,7 +1875,9 @@
         middle_all = spread(middle_grad.astype(BF16), 8)
         mixed_grad = dot(middle_all, out_full, NT)
     output_grad = dot(mixed, middle_all, TN, out=BF16)
-    mixed_grad, output_grad, upgate_sum = lax.optimization_barrier((mixed_grad, output_grad, upgate_sum))
+    mixed_grad, output_grad, upgate_sum, down_total = lax.optimization_barrier(
+        (mixed_grad, output_grad, upgate_sum, down_total.astype(F32))
+    )
     output_total = owned_rows(output_grad)
     projected_low, conv_grad, gain_grad, decay_grad = mixer_backward(
         projected, raw, conv_mine, decay_mine, gain, inverse, solved, core, before_silu, mixed_grad, heads, rows
@@ -1887,7 +1897,6 @@
 
     in_grad = dot(normed_all, projected_low, TN, out=BF16)
     raw_grad = in_grad[:, cols : cols + 2 * heads].astype(F32)
-    down_total = down_total.astype(F32)
     output_total = output_total.astype(F32)
     if square:
         lines = jnp.concatenate(
@@ -1901,14 +1910,17 @@
             ],
             axis=0,
         )
-        conv_lines = jnp.zeros((8, n_dp * (2 * key + value)), F32)
-        for at, a, b in (
-            (here * key, 0, key),
-            (n_dp * key + here * key, key, 2 * key),
-            (2 * n_dp * key + here * value, 2 * key, 2 * key + value),
-        ):
-            conv_lines = lax.dynamic_update_slice(conv_lines, conv_grad[:, a:b], (0, at))
-        conv_lines = lax.dynamic_update_slice(conv_lines, raw_grad.reshape(1, -1), (taps, 0))
+        mine = jnp.arange(n_dp)[None, :, None] == here
+        conv_lines = jnp.concatenate(
+            [
+                jnp.where(mine, conv_grad[:, None, a:b], 0.0).reshape(taps, -1)
+                for a, b in ((0, key), (key, 2 * key), (2 * key, 2 * key + value))
+            ],
+            axis=1,
+        )
+        conv_lines = jnp.concatenate(
+            [conv_lines, raw_grad.reshape(1, -1), jnp.zeros((7 - taps, conv_lines.shape[1]), F32)], axis=0
+        )
         result, tokens_grad, input_total, up_total, summed, planes, conv_total, raw_planes = conclude(
             in_grad.reshape(n_dp, n_z, own_d, cols + 128),
             projected_low.reshape(n_dp, rows, cols + 128),

time: 736 us -> 731 us (level)
  transfers between devices with their start and end apart: 6 -> 6, of which waited for: 4 -> 4; matrix products, arithmetic and copies ran while one was open for 12% -> 13% of each run, Pallas kernels for 41% -> 41%
where the time goes in v7:
time: 731 us; the launch traced here: 726 us
  Pallas kernels  540 us (74%)
  matrix products  89.9 us (12%)
  local copies, waits for them, and re-layouts  41 us (6%)
  waiting for transfers between devices  25 us (3%)
  between operations  15.6 us (2%)
  other arithmetic  14 us (2%)
    pallas_call x2, Pallas kernels, relay(): pl.pallas_call(kernel, out_shape=out_shape, in_specs=in_specs, out_specs=...  170 us
    pallas_call x1, Pallas kernels, conclude(): pl.pallas_call(kernel, out_shape=[f32_rows, f32_rows, jax.ShapeDtypeStruc...  122 us
    pallas_call x1, Pallas kernels, begin(): pl.pallas_call(kernel, out_shape=[jax.ShapeDtypeStruct((8, n_z, own, cols...  119 us
    dot_general x7, matrix products, dot(): return lax.dot_general(a, b, dims, preferred_element_type=F32).astype(out)  89.9 us
    pallas_call x1, Pallas kernels, mixer_forward(): pl.pallas_call(functools.partial(mixer_forward_kernel, heads), grid=(seqs...  52.7 us
    pallas_call x1, Pallas kernels, mixer_backward(): pl.pallas_call(functools.partial(mixer_backward_kernel, heads), grid=(seq...  41.1 us
    pallas_call x1, Pallas kernels, units_forward(): pl.pallas_call(kernel, grid=(blocks,), in_specs=[row(width), whole(weight...  19.6 us
    pallas_call x1, Pallas kernels, units_backward(): pl.pallas_call(kernel, grid=(blocks,), in_specs=[row(width), whole(weight...  16.2 us
  transfers between devices with their start and end apart: 6, of which 4 were waited for; matrix products, arithmetic and copies ran while one was open for 13% of the time, Pallas kernels for 41%

profile of v7, /device:TPU:0, one launch (start us, length us, event | category | flops | bytes accessed | tf_op | source)
XLA Modules:
  0.0 726.2 jit_solution(6271760659372210009)
XLA Ops:
  7.2 1.4 fusion.7
  8.6 0.7 reshape.208
  9.4 0.7 reshape.209
  11.3 2.2 concatenate.30
  13.5 0.7 concatenate.31
  14.2 118.6 %shard_map.237 = (bf16[8,4,64,1536]{3,2,1,0:T(8,128)(2,1)}, bf16[8,64,1408]{2,1,0:T(8,128)(2,1)}, bf16[8,256,2048]{2,1,0:T(8,128)(2,1)}, bf16[8,256,2048]{2,1,0:T(8,128)(2,1)}, bf16[32,32,128]{2,1,0:T(8,128)(2,1)}) custom-call(bf16[64,12288]{1,0:T(8,128)(2,1)} %w_ref.1, bf16[8,64,1408]{2,1,0:T(8,128)(2,1)} %bitcast.88, bf16[256,2048]{1,0:T(8,128)(2,1)} %t_ref.3, ...), custom_call_target="tpu_custom_call" | custom-call | flops 149999992832 | tf_op jit(solution)/shard_map/pallas_call | solution.py:689
  132.9 0.7 all-gather.9.cloned.1.call-update
  133.6 0.7 all-gather.7.cloned.1.call-update
  134.4 0.9 slice.90
  135.3 0.8 slice.91
  136.1 1.6 convert_reduce_fusion
  137.8 1.5 convert_reduce_fusion.1
  139.5 19.8 %fusion.11.proj_ref = f32[2048,1536]{1,0:T(8,128)} fusion(bf16[2048,2048]{1,0:T(8,128)(2,1)} %bitcast.108, bf16[2048,1536]{1,0:T(8,128)(2,1)} %bitcast.118), kind=kOutput, calls=%fused_computation.53 | convolution fusion | flops 12884901888 | bytes 27262976 | tf_op jit(solution)/shard_map/dot_general | solution.py:1668
  160.0 0.8 copy-done.11
  160.9 5.8 fusion.12.raw_ref
  166.9 0.8 reshape.241.gain_ref
  168.2 0.6 dynamic_slice.47
  168.8 52.7 %shard_map.238 = (bf16[2048,512]{1,0:T(8,128)(2,1)S(1)}, f32[8,2,256,256]{3,2,1,0:T(8,128)}, f32[2048,512]{1,0:T(8,128)}, f32[2048,512]{1,0:T(8,128)}, f32[2048,1024]{1,0:T(8,128)}) custom-call(f32[2048,1536]{1,0:T(8,128)} %fusion.11.proj_ref, f32[2048,128]{1,0:T(8,128)S(1)} %fusion.12.raw_ref, f32[4,1024]{1,0:T(4,128)S(1)} %maximum_convert_fusion.1.taps_ref, ...), custom_call_target="tpu_custom_call" | custom-call | flops 54999998464 | tf_op jit(solution)/shard_map/pallas_call | solution.py:170
  221.5 0.6 copy-done
  222.1 1.3 copy-done.4
  223.4 81.5 %shard_map.239 = (f32[256,2048]{1,0:T(8,128)}, bf16[8,256,2048]{2,1,0:T(8,128)(2,1)}) custom-call(bf16[8,256,512]{2,1,0:T(8,128)(2,1)} %bitcast.85, bf16[512,2048]{1,0:T(8,128)(2,1)} %all-gather.5.cloned.1.call-done.first_ref.refs_2_, f32[1,2048]{1,0:T(1,128)} %reshape.241.gain_ref, bf16[256,2048]{1,0:T(8,128)(2,1)} %t_ref.3), custom_call_target="tpu_custom_call" | custom-call | flops 80000000000 | tf_op jit(solution)/shard_map/pallas_call | solution.py:965
  305.1 19.6 %shard_map.240 = (f32[2048,1408]{1,0:T(8,128)}, bf16[2048,704]{1,0:T(8,128)(2,1)S(1)}, bf16[2048,704]{1,0:T(8,128)(2,1)}) custom-call(bf16[2048,2048]{1,0:T(8,128)(2,1)} %bitcast.114, bf16[2048,1408]{1,0:T(8,128)(2,1)} %bitcast.105, f32[8,128]{1,0:T(8,128)S(1)} %broadcast_in_dim.108.s_ref), custom_call_target="tpu_custom_call" | custom-call | flops 20000000000 | tf_op jit(solution)/shard_map/pallas_call | solution.py:1029
  324.7 9.4 %convolution_convert_fusion.3 = bf16[704,2048]{1,0:T(8,128)(2,1)} fusion(bf16[2048,704]{1,0:T(8,128)(2,1)} %get-tuple-element.74, bf16[2048,2048]{1,0:T(8,128)(2,1)S(1)} %bitcast.112), kind=kOutput, calls=%fused_computation.3 | convolution fusion | flops 5907021824 | bytes 14155776 | tf_op jit(solution)/shard_map/dot_general | solution.py:1668
  334.1 3.4 convert_multiply_fusion.refs_1_
  337.6 7.2 all-gather.7.cloned.1.call-done.w_ref
  344.8 1.8 copy-done.2
  346.6 16.2 %shard_map.241 = bf16[2048,1408]{1,0:T(8,128)(2,1)} custom-call(bf16[2048,2048]{1,0:T(8,128)(2,1)} %bitcast.111, bf16[704,2048]{1,0:T(8,128)(2,1)S(1)} %copy-done.2, f32[2048,1408]{1,0:T(8,128)} %get-tuple-element.78.up_ref, f32[8,128]{1,0:T(8,128)S(1)} %broadcast_in_dim.108.s_ref), custom_call_target="tpu_custom_call" | custom-call | flops 12000000000 | tf_op jit(solution)/shard_map/pallas_call | solution.py:1068
  362.9 17.2 %convolution_convert_fusion.2 = bf16[2048,1408]{1,0:T(8,128)(2,1)S(1)} fusion(bf16[2048,2048]{1,0:T(8,128)(2,1)} %bitcast.115, bf16[2048,1408]{1,0:T(8,128)(2,1)} %shard_map.241), kind=kOutput, calls=%fused_computation.2 | convolution fusion | flops 11814043648 | bytes 19922944 | tf_op jit(solution)/shard_map/dot_general | solution.py:1668
  380.1 3.0 copy.71
  383.1 8.8 %convolution_convert_fusion = bf16[2048,2048]{1,0:T(8,128)(2,1)} fusion(bf16[2048,704]{1,0:T(8,128)(2,1)S(1)} %get-tuple-element.82, bf16[704,2048]{1,0:T(8,128)(2,1)S(1)} %copy-done.2), kind=kOutput, calls=%fused_computation | convolution fusion | flops 5909774336 | bytes 14155776 | tf_op jit(solution)/shard_map/dot_general | solution.py:1668
  392.0 10.5 %reduce-scatter.4.cloned.1.call-done = bf16[176,2048]{1,0:T(8,128)(2,1)} async-done(((bf16[704,2048]{1,0:T(8,128)(2,1)}), bf16[176,2048]{1,0:T(8,128)(2,1)}) %reduce-scatter.4.cloned.1.call-update) | async-done | bytes 720912 | tf_op jit(solution)/shard_map/reduce_scatter | solution.py:1851
  402.5 0.7 reshape.243.gain_ref
  404.0 1.2 convert_element_type.82
  405.3 88.8 %shard_map.242 = (f32[256,2048]{1,0:T(8,128)}, bf16[8,256,2048]{2,1,0:T(8,128)(2,1)}, f32[8,256,512]{2,1,0:T(8,128)}, f32[1,2048]{1,0:T(1,128)}) custom-call(bf16[8,256,1408]{2,1,0:T(8,128)(2,1)} %bitcast.120, bf16[2048,1408]{1,0:T(8,128)(2,1)} %bitcast.106, f32[1,2048]{1,0:T(1,128)} %reshape.241.gain_ref, f32[256,2048]{1,0:T(8,128)} %get-tuple-element.84.refs_0_.m_ref, ...), custom_call_target="tpu_custom_call" | custom-call | flops 80000000000 | tf_op jit(solution)/shard_map/pallas_call | solution.py:965
  494.1 9.1 %convolution_convert_fusion.4 = bf16[512,2048]{1,0:T(8,128)(2,1)} fusion(bf16[2048,512]{1,0:T(8,128)(2,1)S(1)} %copy-done.5, bf16[2048,2048]{1,0:T(8,128)(2,1)} %bitcast.116), kind=kOutput, calls=%fused_computation.4 | convolution fusion | flops 4296015872 | bytes 12582912 | tf_op jit(solution)/shard_map/dot_general | solution.py:1668
  503.2 3.6 reduce-scatter.6.cloned.1.call-done
  506.8 41.1 %shard_map.243 = (bf16[2048,1664]{1,0:T(8,128)(2,1)}, f32[4,1024]{1,0:T(4,128)}, f32[1,256]{1,0:T(1,128)}, f32[2,128]{1,0:T(2,128)}) custom-call(f32[2048,1536]{1,0:T(8,128)} %fusion.11.proj_ref, f32[2048,128]{1,0:T(8,128)} %copy-done.6, f32[4,1024]{1,0:T(4,128)} %copy-done, f32[2,128]{1,0:T(2,128)} %copy-done.1, f32[1,256]{1,0:T(1,128)} %bitcast.83, ...), custom_call_target="tpu_custom_call" | custom-call | flops 49999998976 | tf_op jit(solution)/shard_map/pallas_call | solution.py:295
  547.9 0.8 reshape.231
  548.6 0.7 slice.100
  549.4 0.7 fusion.8
  550.2 0.7 slice_bitcast_fusion.1
  550.9 0.7 concatenate.34.lines_ref
  551.7 2.3 reduce-scatter.8.cloned.1.call-done
  553.9 19.8 %convolution_convert_fusion.1 = bf16[2048,1664]{1,0:T(8,128)(2,1)S(1)} fusion(bf16[2048,2048]{1,0:T(8,128)(2,1)} %bitcast.110, bf16[2048,1664]{1,0:T(8,128)(2,1)} %get-tuple-element.93), kind=kOutput, calls=%fused_computation.1 | convolution fusion | flops 13962051584 | bytes 22020096 | tf_op jit(solution)/shard_map/dot_general | solution.py:1668
  573.7 2.8 copy-done.14
  576.6 0.7 reshape.245
  577.3 0.8 maximum_maximum_fusion.conv_ref
  578.1 121.8 %shard_map.244 = (f32[256,2048]{1,0:T(8,128)}, f32[256,2048]{1,0:T(8,128)}, bf16[64,12288]{1,0:T(8,128)(2,1)}, bf16[8,64,1408]{2,1,0:T(8,128)(2,1)}, f32[8,128]{...) custom-call(bf16[8,4,64,1664]{3,2,1,0:T(8,128)(2,1)} %bitcast.96, ...), custom_call_target="tpu_custom_call" | custom-call | flops 120000004096 | tf_op jit(solution)/shard_map/pallas_call | solution.py:1500
  700.0 0.8 fusion.9
  700.8 1.2 slice_bitcast_fusion
  702.1 1.1 fusion.6
  703.2 1.4 fusion.5
  704.6 1.9 convert_element_type.86
  706.6 0.7 copy.73
  707.3 0.6 slice.103
  708.0 0.6 reshape.236
  708.6 0.6 reshape.237
  709.2 1.1 convert_element_type.87
  711.9 0.7 reshape.240
  713.2 0.7 reshape.239
  714.0 1.8 maximum_convert_fusion
  715.7 0.8 copy-done.8
  716.5 1.3 copy.91
  717.9 1.3 copy.92
  (119 shorter events, 6.0 us)
Async XLA Ops:
  7.2 216.3 %all-gather.5.cloned.1.call-start = ((), (), s32[]{:S(2)}) async-start(), calls=%async_computation.3 | async-start | bytes 2621440 | tf_op jit(solution)/shard_map/all_gather | solution.py:1767
  9.3 1.8 copy-start.22
  9.3 1.8 copy-start.16
  10.1 3.4 copy-start.19
  10.1 3.4 copy-start.20
  132.8 172.2 %all-gather.9.cloned.1.call-start = ((), (), s32[]{:S(2)}) async-start(), calls=%async_computation.8 | async-start | bytes 7208960 | tf_op jit(solution)/shard_map/all_gather | solution.py:1724
  133.6 211.2 %all-gather.7.cloned.1.call-start = ((), (), s32[]{:S(2)}) async-start(), calls=%async_computation.4 | async-start | bytes 3604480 | tf_op jit(solution)/shard_map/all_gather | solution.py:1769
  134.3 268.1 %reduce-scatter.4.cloned.1.call-start = ((), (), s32[]{:S(2)}) async-start(), calls=%async_computation.5 | async-start | bytes 3604480 | tf_op jit(solution)/shard_map/reduce_scatter | solution.py:1851
  160.0 0.8 copy-start.11
  160.9 7.2 copy-start.24
  160.9 7.2 copy-start.25
  160.9 7.9 %copy-start.3 = (f32[256]{0:T(256)S(1)}, f32[256]{0:T(256)}, u32[]{:S(2)}) copy-start(f32[256]{0:T(256)} %param.23) | copy-start | bytes 3076
  166.7 54.8 %copy-start.6 = (f32[2048,128]{1,0:T(8,128)}, f32[2048,128]{1,0:T(8,128)S(1)}, u32[]{:S(2)}) copy-start(f32[2048,128]{1,0:T(8,128)S(1)} %fusion.12.raw_ref) | copy-start | bytes 3145732
  168.2 53.3 %copy-start.1 = (f32[2,128]{1,0:T(2,128)}, f32[2,128]{1,0:T(2,128)S(1)}, u32[]{:S(2)}) copy-start(f32[2,128]{1,0:T(2,128)S(1)} %select_maximum_fusion.decay_ref) | copy-start | bytes 3076
  221.5 0.6 copy-start
  222.1 1.3 copy-start.4
  305.1 19.6 %copy-start.26 = (bf16[8,256,2048]{2,1,0:T(8,128)(2,1)S(1)}, bf16[8,256,2048]{2,1,0:T(8,128)(2,1)}, u32[]{:S(2)}) copy-start(bf16[8,256,2048]{2,1,0:T(8,128)(2,1)} %get-tuple-element.75) | copy-start | bytes 25165828
  334.1 172.7 %reduce-scatter.6.cloned.1.call-start = ((), (), s32[]{:S(2)}) async-start(), calls=%async_computation.6 | async-start | bytes 7208960 | tf_op jit(solution)/shard_map/reduce_scatter | solution.py:1854
  344.8 1.8 copy-start.2
  392.0 10.6 %copy-start.13 = (f32[32,64]{1,0:T(8,128)S(1)}, f32[32,64]{1,0:T(8,128)}, u32[]{:S(2)}) copy-start(f32[32,64]{1,0:T(8,128)} %get-tuple-element.111) | copy-start | bytes 24580
  402.5 1.6 copy-start.10
  402.5 151.4 %reduce-scatter.8.cloned.1.call-start = ((), (), s32[]{:S(2)}) async-start(), calls=%async_computation.7 | async-start | bytes 2621440 | tf_op jit(solution)/shard_map/reduce_scatter | solution.py:1851
  405.3 88.8 %copy-start.5 = (bf16[2048,512]{1,0:T(8,128)(2,1)S(1)}, bf16[2048,512]{1,0:T(8,128)(2,1)}, u32[]{:S(2)}) copy-start(bf16[2048,512]{1,0:T(8,128)(2,1)} %copy-done.4) | copy-start | bytes 6291460
  506.8 44.1 %copy-start.17 = (f32[1,2048]{1,0:T(1,128)S(1)}, f32[1,2048]{1,0:T(1,128)}, u32[]{:S(2)}) copy-start(f32[1,2048]{1,0:T(1,128)} %get-tuple-element.97) | copy-start | bytes 24580
  553.9 23.4 %copy-start.23 = (f32[8]{0:T(128)S(1)}, f32[8]{0:T(128)}, u32[]{:S(2)}) copy-start(f32[8]{0:T(128)} %pad.25.clone) | copy-start | bytes 100
  573.7 2.8 copy-start.14
  700.0 4.6 copy-start.9
  700.0 6.5 copy-start.18
  700.0 7.3 %copy-start.21 = (f32[8,256]{1,0:T(8,128)S(1)}, f32[8,256]{1,0:T(8,128)}, u32[]{:S(2)}) copy-start(f32[8,256]{1,0:T(8,128)} %get-tuple-element.106) | copy-start | bytes 24580
  700.0 7.9 %copy-start.15 = (f32[8,128]{1,0:T(8,128)S(1)}, f32[8,128]{1,0:T(8,128)}, u32[]{:S(2)}) copy-start(f32[8,128]{1,0:T(8,128)} %get-tuple-element.107) | copy-start | bytes 12292
  700.0 9.2 %copy-start.12 = (bf16[128,2048]{1,0:T(8,128)(2,1)S(1)}, bf16[128,2048]{1,0:T(8,128)(2,1)}, u32[]{:S(2)}) copy-start(bf16[128,2048]{1,0:T(8,128)(2,1)} %reduce-scatter.8.cloned.1.call-done) | copy-start | bytes 1572868
  713.9 2.6 copy-start.8
  713.9 3.9 copy-start.7
Sparse Core Ops, SparseCore 0:
  133.0 45.8 all-gather.4
  180.4 105.3 all-gather.8
  287.4 57.3 all-gather.6
  347.6 54.8 reduce-scatter.3
  404.6 102.1 reduce-scatter.5
  509.5 44.4 reduce-scatter.7
